TPU v7x, 512 devices: a whole 4x4x16 slice. The times are simulated.
512 devices in a mesh: expert: 128 (over z, y, core), dp: 4 (over x).
Axes of the slice: x: 4, y: 4, z: 16, core: 2. Of those that a mesh axis runs over, the one named last changes fastest.
Arguments:
- tokens: bfloat16 [65536, 2048], P(('expert', 'dp')), may hold values from -6 to 6
- norm_gain: float32 [2048], replicated, may hold values from 0.25 to 1.75
- routing: int32 [65536, 2], P(('expert', 'dp')), may hold values from 0 to 127, as said below
- gate_scores: float32 [65536, 2], P(('expert', 'dp')), may hold values from 0.05 to 1
- w_gate: bfloat16 [128, 2048, 1024], P('expert', None, 'dp'), may hold values from -0.125 to 0.125
- w_up: bfloat16 [128, 2048, 1024], P('expert', None, 'dp'), may hold values from -0.125 to 0.125
- w_down: bfloat16 [128, 1024, 2048], P('expert', None, 'dp'), may hold values from -0.1875 to 0.1875
Outputs:
- combined: bfloat16 [65536, 2048], P(('expert', 'dp'))
Inputs may be any that keep to these rules, and one draw needn't show every extreme that they name: `routing`: each row names 2 different experts. Two experts, the same on every device, are each named by exactly 4 of the 128 rows of every device; every other expert is named by at most 2 rows of one device, and some reach 2.
All inputs are finite; a program needn't handle non-finite values.
Results may differ from a plain program's by a relative error of at most 0.007.
Values may be sent and summed in bfloat16 or wider, within the bound.
No kernel may reach another device: no remote copies, remote signals or barrier semaphores. Data moves between devices by JAX's collectives and lax.ppermute only.
A program may use at most 128 MiB of HBM per device.

v0:
```python
import jax
import jax.numpy as jnp
from jax import lax
from jax.sharding import PartitionSpec as P


def route_and_compute(pair_rows, flat_ids, onehot, routed, slot_count, gate_w, up_w, down_w):
    experts = onehot.shape[1]
    model_width = pair_rows.shape[1]
    groups = lax.axis_size("dp")
    live_hot = onehot * routed[:, None].astype(jnp.int32)
    slot_rank = jnp.sum((jnp.cumsum(live_hot, axis=0) - live_hot) * live_hot, axis=1)
    target = jnp.where(routed, flat_ids * slot_count + slot_rank, 0)
    slot_range = jnp.arange(experts * slot_count, dtype=jnp.int32)
    dispatch_table = ((slot_range[:, None] == target[None, :]) & routed[None, :]).astype(
        jnp.bfloat16
    )
    outgoing = jnp.dot(dispatch_table, pair_rows, preferred_element_type=jnp.float32).astype(
        jnp.bfloat16
    )
    outgoing = outgoing.reshape(experts, slot_count, model_width)
    incoming = lax.all_to_all(outgoing, "expert", split_axis=0, concat_axis=0, tiled=True)
    shard_rows = lax.all_gather(incoming, "dp", axis=0, tiled=True)
    gate_part = jnp.einsum("nsd,df->nsf", shard_rows, gate_w, preferred_element_type=jnp.float32)
    up_part = jnp.einsum("nsd,df->nsf", shard_rows, up_w, preferred_element_type=jnp.float32)
    hidden = (jax.nn.silu(gate_part) * up_part).astype(jnp.bfloat16)
    flat_hidden = hidden.reshape(-1, hidden.shape[2])
    summed = jnp.dot(
        lax.all_gather(flat_hidden, "dp", axis=1, tiled=True),
        down_w,
        preferred_element_type=jnp.float32,
    )
    results = summed.astype(jnp.bfloat16).reshape(groups, experts, slot_count, down_w.shape[1])
    returned = lax.all_to_all(
        lax.all_to_all(results, "expert", split_axis=1, concat_axis=1, tiled=True),
        "dp",
        split_axis=0,
        concat_axis=3,
        tiled=True,
    )
    returned = returned.reshape(experts * slot_count, model_width)
    return returned[target]


def body(tokens, norm_gain, routing, gate_scores, w_gate, w_up, w_down):
    experts = lax.axis_size("expert")
    tok_count, model_width = tokens.shape
    top_k = routing.shape[1]
    hot_cap = max(1, tok_count // 32)
    spare_cap = (tok_count * top_k - 2 * hot_cap + experts - 3) // (experts - 2)
    as_float = tokens.astype(jnp.float32)
    scale_rms = lax.rsqrt(jnp.mean(as_float * as_float, axis=1, keepdims=True) + 1e-06)
    normed = (as_float * scale_rms * norm_gain).astype(jnp.bfloat16)
    weights = gate_scores / jnp.sum(gate_scores, axis=1, keepdims=True)
    flat_ids = routing.reshape(-1)
    pair_weight = weights.reshape(-1)
    pair_rows = jnp.repeat(normed, top_k, axis=0)
    expert_range = jnp.arange(experts, dtype=jnp.int32)
    onehot = (flat_ids[:, None] == expert_range[None, :]).astype(jnp.int32)
    gate_w = w_gate[0]
    up_w = w_up[0]
    down_w = w_down[0]
    routed = jnp.ones(flat_ids.shape, dtype=bool)
    expert_vals = route_and_compute(
        pair_rows, flat_ids, onehot, routed, max(hot_cap, spare_cap), gate_w, up_w, down_w
    )
    scaled = expert_vals.astype(jnp.float32) * pair_weight[:, None]
    combined = jnp.sum(scaled.reshape(tok_count, top_k, model_width), axis=1)
    return combined.astype(jnp.bfloat16)


def solution(mesh):
    in_specs = (
        P(("expert", "dp"), None),
        P(),
        P(("expert", "dp"), None),
        P(("expert", "dp"), None),
        P("expert", None, "dp"),
        P("expert", None, "dp"),
        P("expert", None, "dp"),
    )
    out_specs = P(("expert", "dp"), None)
    return jax.shard_map(body, mesh=mesh, in_specs=in_specs, out_specs=out_specs, check_vma=False)
```

profile of v0, /device:TPU:33, one launch (start us, length us, event | category | flops | bytes accessed | tf_op | source)
XLA Modules:
  0.0 469.5 jit_solution(12308673314434914330)
XLA Ops:
  6.5 0.9 copy.30
  7.6 0.1 reshape.92
  7.8 0.2 fusion.8
  8.1 0.2 fusion.10
  8.3 1.2 fusion
  9.5 1.2 fusion.2
  10.8 0.6 broadcast_in_dim.5
  11.4 1.2 reshape.94
  12.7 1.9 convolution_convert_fusion.1
  14.6 2.2 reshape.95
  16.8 118.6 %all_to_all.25 = bf16[128,4,2048]{2,1,0:T(4,128)(2,1)S(1)} all-to-all(bf16[128,4,2048]{2,1,0:T(4,128)(2,1)} %reshape.95), channel_id=1, replica_groups=mesh['expert'=128,'dp'=4] {'expert'}, dimensions={0} | all-to-all | bytes 4194304 | tf_op jit(solution)/shard_map/all_to_all | solution.py:22
  135.5 2.5 copy.34
  138.1 0.2 all-gather.5.cloned.1.call-start
  138.3 83.1 %all-gather.3.cloned.1.call-done = bf16[512,4,2048]{2,0,1:T(8,128)(2,1)} async-done(((bf16[128,4,2048]{2,0,1:T(8,128)(2,1)}), bf16[512,4,2048]{2,0,1:T(8,128)(2,1)}) %all-gather.3.cloned.1.call-update) | async-done | bytes 8388624 | tf_op jit(solution)/shard_map/all_gather | solution.py:23
  221.4 5.9 %fusion.4 = f32[512,4,256]{2,0,1:T(8,128)S(1)} fusion(bf16[512,4,2048]{2,0,1:T(8,128)(2,1)} %all-gather.3.cloned.1.call-done, bf16[1,2048,256]{2,1,0:T(8,128)(2,1)S(1)} %copy-done.4), kind=kOutput, calls=%fused_computation.11 | convolution fusion | flops 2147483648 | bytes 11534336 | tf_op jit(solution)/shard_map/nsd,df->nsf/dot_general | solution.py:25
  227.3 2.6 multiply_convert_fusion
  230.0 0.8 copy.35
  230.8 1.1 reshape.96
  231.9 60.0 %all-gather.5.cloned.1.call-done = bf16[2048,1024]{1,0:T(8,128)(2,1)} async-done(((bf16[2048,256]{1,0:T(8,128)(2,1)}), bf16[2048,1024]{1,0:T(8,128)(2,1)}) %all-gather.5.cloned.1.call-update) | async-done | bytes 4194320 | tf_op jit(solution)/shard_map/all_gather | solution.py:29
  291.9 5.9 %convolution_convert_fusion = bf16[2048,512]{1,0:T(8,128)(2,1)} fusion(bf16[2048,1024]{1,0:T(8,128)(2,1)} %all-gather.5.cloned.1.call-done, bf16[1,1024,512]{2,1,0:T(8,128)(2,1)S(1)} %copy-done), kind=kOutput, calls=%fused_computation.1 | convolution fusion | flops 2148532224 | bytes 7340032 | tf_op jit(solution)/shard_map/dot_general | solution.py:28
  297.8 2.5 reshape.97
  300.3 1.2 copy.36
  301.5 116.6 %all_to_all.26 = bf16[4,128,4,512]{3,2,0,1:T(4,128)(2,1)S(1)} all-to-all(bf16[4,128,4,512]{3,2,0,1:T(4,128)(2,1)S(1)} %copy.36), channel_id=1, replica_groups=mesh['expert'=128,'dp'=4] {'expert'}, dimensions={1} | all-to-all | bytes 4194304 | tf_op jit(solution)/shard_map/all_to_all | solution.py:35
  418.1 2.1 copy.37
  420.2 4.0 all-to-all-start.2
  424.3 0.1 mul.74
  424.6 26.1 %all-to-all-done.2 = bf16[4,128,4,512]{3,2,1,0:T(4,128)(2,1)S(1)} async-done(((bf16[4,128,4,512]{3,2,1,0:T(4,128)(2,1)}), bf16[4,128,4,512]{3,2,1,0:T(4,128)(2,1)S(1)}, u32[]{:S(2)}, u32[]{:S(2)}) %all-to-all-start.2) | async-done | bytes 2097184 | tf_op jit(solution)/shard_map/all_to_all | solution.py:34
  450.7 2.7 copy.38
  453.4 0.6 copy.41
  454.0 2.4 gather_fusion
  456.3 2.4 reshape.99
  458.7 3.9 multiply_reduce_fusion
  (32 shorter events, 0.7 us)
Async XLA Ops:
  6.5 285.4 %copy-start = (bf16[1,1024,512]{2,1,0:T(8,128)(2,1)S(1)}, bf16[1,1024,512]{2,1,0:T(8,128)(2,1)}, u32[]{:S(2)}) copy-start(bf16[1,1024,512]{2,1,0:T(8,128)(2,1)} %param.13) | copy-start | bytes 3145732
  6.5 214.9 %all-gather.3.cloned.1.call-start = ((), (), s32[]{:S(2)}) async-start(), calls=%async_computation.3 | async-start | bytes 10485760 | tf_op jit(solution)/shard_map/all_gather | solution.py:23
  138.0 83.4 %copy-start.4 = (bf16[1,2048,256]{2,1,0:T(8,128)(2,1)S(1)}, bf16[1,2048,256]{2,1,0:T(8,128)(2,1)}, u32[]{:S(2)}) copy-start(bf16[1,2048,256]{2,1,0:T(8,128)(2,1)} %param.12) | copy-start | bytes 3145732
  138.0 89.3 %copy-start.5 = (bf16[1,2048,256]{2,1,0:T(8,128)(2,1)S(1)}, bf16[1,2048,256]{2,1,0:T(8,128)(2,1)}, u32[]{:S(2)}) copy-start(bf16[1,2048,256]{2,1,0:T(8,128)(2,1)} %param.11) | copy-start | bytes 3145732
  138.1 153.8 %all-gather.5.cloned.1.call-start = ((), (), s32[]{:S(2)}) async-start(), calls=%async_computation.4 | async-start | bytes 5242880 | tf_op jit(solution)/shard_map/all_gather | solution.py:29
  221.4 5.9 %copy-start.3 = (bf16[512,4,2048]{2,0,1:T(8,128)(2,1)S(1)}, bf16[512,4,2048]{2,0,1:T(8,128)(2,1)}, u32[]{:S(2)}) copy-start(bf16[512,4,2048]{2,0,1:T(8,128)(2,1)} %all-gather.3.cloned.1.call-done) | copy-start | bytes 25165828
  420.2 4.0 copy-start.1
  420.2 4.2 copy-start.2
  420.2 30.5 %all-to-all-start.2 = ((bf16[4,128,4,512]{3,2,1,0:T(4,128)(2,1)}), bf16[4,128,4,512]{3,2,1,0:T(4,128)(2,1)S(1)}, u32[]{:S(2)}, u32[]{:S(2)}) async-start(bf16[4,128,4,512]{3,2,1,0:T(4,128)(2,1)} %copy.37), calls=%async_computation.2 | async-start | bytes 4194304 | tf_op jit(solution)/shard_map/all_to_all | solution.py:34
Sparse Core Ops, SparseCore 0:
  138.2 83.1 all-gather.2
  232.0 59.8 all-gather.4
where the time goes:
time: 470 us; the launch traced here: 469 us
  blocking collectives  235 us (50%)
  waiting for transfers between devices  169 us (36%)
  local copies, waits for them, and re-layouts  24.1 us (5%)
  matrix products  16.3 us (3%)
  between operations  13.6 us (3%)
  other arithmetic  6.89 us (1%)
    all_to_all x1, blocking collectives, route_and_compute(): lax.all_to_all(outgoing, 'expert', split_axis=0, concat_axis=0, tiled=True)  119 us
    all_to_all x1, blocking collectives, route_and_compute(): lax.all_to_all(results, 'expert', split_axis=1, concat_axis=1, tiled=True)  117 us
    all_gather x1, waiting for transfers between devices, route_and_compute(): shard_rows = lax.all_gather(incoming, 'dp', axis=0, tiled=True)  83.1 us
    all_gather x1, waiting for transfers between devices, route_and_compute(): lax.all_gather(flat_hidden, 'dp', axis=1, tiled=True)  60 us
    all_to_all x1, waiting for transfers between devices, route_and_compute(): lax.all_to_all(lax.all_to_all(results, 'expert', split_axis=1, concat_axi...  26.1 us
  transfers between devices with their start and end apart: 3, of which 3 were waited for; matrix products, arithmetic and copies ran while one was open for 0% of the time, Pallas kernels for 0%

commit v1 on v0

v1 whole, which is shorter than its diff:
```python
import jax
import jax.numpy as jnp
from jax import lax
from jax.experimental import pallas as pl
from jax.experimental.pallas import tpu as pltpu
from jax.sharding import Mesh, PartitionSpec as P

E_AXES = ("z", "y", "c")
SLOT = 2
VMEM = pl.BlockSpec(memory_space=pltpu.VMEM)


def first_kernel(tok_ref, gain_ref, rt_ref, main_ref, ext_ref, tgt_ref, hot_ref):
    toks, experts = tok_ref.shape[0], main_ref.shape[0] // SLOT
    x = tok_ref[...].astype(jnp.float32)
    scale = lax.rsqrt(jnp.mean(x * x, axis=1, keepdims=True) + 1e-06)
    normed = (x * scale * gain_ref[...]).astype(jnp.bfloat16)
    lane = lax.broadcasted_iota(jnp.int32, (toks, experts), 1)
    ids = [rt_ref[:, k : k + 1] for k in range(2)]
    hots = [i == lane for i in ids]
    both = (hots[0] | hots[1]).astype(jnp.float32)
    row = lax.broadcasted_iota(jnp.int32, (toks, toks), 0)
    col = lax.broadcasted_iota(jnp.int32, (toks, toks), 1)
    before = (row > col).astype(jnp.bfloat16)
    count = jnp.dot(before, both.astype(jnp.bfloat16), preferred_element_type=jnp.float32)
    busy = jnp.sum(both, axis=0, keepdims=True) > SLOT + 0.5
    eid = lax.broadcasted_iota(jnp.int32, (1, experts), 1)
    low = jnp.min(jnp.where(busy, eid, experts - 1), axis=1, keepdims=True)
    high = jnp.max(jnp.where(busy, eid, 0), axis=1, keepdims=True)
    targets = []
    for k in range(2):
        rank = jnp.sum(jnp.where(hots[k], count, 0.0), axis=1, keepdims=True).astype(jnp.int32)
        over = experts * SLOT + jnp.where(ids[k] == high, 2, 0) + rank - SLOT
        targets.append(jnp.where(rank < SLOT, ids[k] * SLOT + rank, over))
        tgt_ref[:, k : k + 1] = targets[k]
    for ref, base in ((main_ref, 0), (ext_ref, experts * SLOT)):
        slots = max(ref.shape[0], 128)
        slot = lax.broadcasted_iota(jnp.int32, (toks, slots), 1) + base
        pick = ((slot == targets[0]) | (slot == targets[1])).astype(jnp.float32)
        rows = jnp.dot(
            pick.T.astype(jnp.bfloat16), normed, preferred_element_type=jnp.float32
        ).astype(jnp.bfloat16)
        ref[...] = rows[: ref.shape[0]]
    hot_ref[:, 0:1] = low
    hot_ref[:, 1:2] = high


def last_kernel(res_ref, ext_ref, tgt_ref, gs_ref, out_ref):
    toks, slots = out_ref.shape[0], res_ref.shape[0]
    weights = gs_ref[...] / jnp.sum(gs_ref[...], axis=1, keepdims=True)
    total = None
    for ref, base in ((res_ref, 0), (ext_ref, slots)):
        slot = lax.broadcasted_iota(jnp.int32, (toks, ref.shape[0]), 1) + base
        mix = sum(jnp.where(slot == tgt_ref[:, k : k + 1], weights[:, k : k + 1], 0.0) for k in range(2))
        coarse = mix.astype(jnp.bfloat16)
        fine = (mix - coarse.astype(jnp.float32)).astype(jnp.bfloat16)
        for part in (fine, coarse):
            term = jnp.dot(part, ref[...], preferred_element_type=jnp.float32)
            total = term if total is None else total + term
    out_ref[...] = total.astype(jnp.bfloat16)


def flip(n, bit):
    return [(i, i ^ bit) for i in range(n)]


def ring(n, k):
    return [(i, (i + k) % n) for i in range(n)]


def gather_ring(x):
    half = x.shape[0] // 2
    ahead = lax.ppermute(x, "dp", ring(4, -1))
    behind = lax.ppermute(x, "dp", ring(4, 1))
    far_a = lax.ppermute(ahead[:half], "dp", ring(4, -1))
    far_b = lax.ppermute(behind[half:], "dp", ring(4, 1))
    return [x, ahead, jnp.concatenate([far_a, far_b], 0), behind]


def steps_of(mesh):
    steps = []
    for axis in ("z", "y", "c"):
        bit = mesh.shape[axis] // 2
        while bit:
            steps.append((axis, bit))
            bit //= 2
    return steps


def body(mesh, tokens, norm_gain, routing, gate_scores, w_gate, w_up, w_down):
    toks, width = tokens.shape
    experts = 1
    for axis in E_AXES:
        experts *= mesh.shape[axis]
    bf16, f32, i32 = jnp.bfloat16, jnp.float32, jnp.int32
    main, extra, target, hot = pl.pallas_call(
        first_kernel,
        out_shape=[
            jax.ShapeDtypeStruct((experts * SLOT, width), bf16),
            jax.ShapeDtypeStruct((16, width), bf16),
            jax.ShapeDtypeStruct((toks, 2), i32),
            jax.ShapeDtypeStruct((1, 2), i32),
        ],
        in_specs=[VMEM] * 3,
        out_specs=[VMEM] * 4,
        compiler_params=pltpu.CompilerParams(vmem_limit_bytes=40 * 1024 * 1024),
    )(tokens, norm_gain.reshape(1, width), routing)

    gate_all = lax.all_gather(w_gate[0], "dp", axis=0, tiled=False)
    up_all = lax.all_gather(w_up[0], "dp", axis=0, tiled=False)
    down = gather_ring(w_down[0])

    got = lax.all_to_all(main.reshape(experts, SLOT, width), E_AXES, 0, 0, tiled=True)
    steps = steps_of(mesh)
    held = extra[:4].reshape(1, 4 * width)
    for axis, bit in steps:
        held = jnp.concatenate([held, lax.ppermute(held, axis, flip(mesh.shape[axis], bit))], 0)
    place = [lax.axis_index(a) for a in E_AXES]
    me = (place[0] * mesh.shape["y"] + place[1]) * mesh.shape["c"] + place[2]
    low, high = hot[0, 0], hot[0, 1]
    mine = jnp.where(me == low, held[:, : 2 * width], held[:, 2 * width :])
    rows = jnp.concatenate([got.reshape(experts * SLOT, width), mine[:, :width], mine[:, width:]], 0)

    hidden = []
    for q in range(4):
        g = jnp.dot(rows, gate_all[q], preferred_element_type=f32)
        u = jnp.dot(rows, up_all[q], preferred_element_type=f32)
        hidden.append((jax.nn.silu(g) * u).astype(bf16))
    hidden = jnp.concatenate(hidden, 1)
    parts = [jnp.dot(hidden, d, preferred_element_type=f32).astype(bf16) for d in down]
    at = lax.axis_index("dp")
    cols = w_down.shape[2]
    ordered = jnp.zeros((rows.shape[0], width), bf16)
    for k in range(4):
        ordered = lax.dynamic_update_slice(ordered, parts[k], (0, lax.rem(at + k, 4) * cols))
    done = ordered[: experts * SLOT].reshape(experts, SLOT, width)
    back = lax.all_to_all(done, E_AXES, 0, 0, tiled=True).reshape(experts * SLOT, width)

    over = ordered[experts * SLOT :].reshape(2, experts, width)
    over = jnp.concatenate([over[0], over[1]], 1)
    over = jnp.concatenate([over, over], 1)
    away = [me ^ low, me ^ high]
    left = (1 << len(steps)) - 1
    bits = {}
    weight = {"c": 1, "y": mesh.shape["c"], "z": mesh.shape["c"] * mesh.shape["y"]}
    for axis, bit in reversed(steps):
        half = over.shape[0] // 2
        sent = lax.ppermute(over[half:], axis, flip(mesh.shape[axis], bit))
        keep = [(a & left) == 0 for a in away]
        pick = jnp.where(jnp.arange(4 * width)[None, :] < 2 * width, keep[0], keep[1])
        over = jnp.where(pick, over[:half], sent)
        left -= weight[axis] * bit
    over = over.reshape(4, width)

    return pl.pallas_call(
        last_kernel,
        out_shape=jax.ShapeDtypeStruct((toks, width), bf16),
        in_specs=[VMEM] * 4,
        out_specs=VMEM,
        compiler_params=pltpu.CompilerParams(vmem_limit_bytes=40 * 1024 * 1024),
    )(back, jnp.pad(over, ((0, 124), (0, 0))), target, gate_scores)


def solution(mesh):
    fine = Mesh(mesh.devices.reshape(16, 4, 2, 4), ("z", "y", "c", "dp"))
    rows = P((*E_AXES, "dp"), None)
    weights = P(E_AXES, None, "dp")
    return jax.shard_map(
        lambda *args: body(fine, *args),
        mesh=fine,
        in_specs=(rows, P(), rows, rows, weights, weights, weights),
        out_specs=rows,
        check_vma=False,
    )
```

time: 470 us -> 336 us (0.71)
  the two profiles are of different devices: /device:TPU:33 before, /device:TPU:8 now
where the time goes in v1:
time: 336 us; the launch traced here: 334 us
  waiting for transfers between devices  147 us (44%)
  starting transfers between devices  120 us (36%)
  local copies, waits for them, and re-layouts  25.3 us (8%)
  matrix products  17.2 us (5%)
  between operations  15.9 us (5%)
  other arithmetic  5.3 us (2%)
    ppermute x7, waiting for transfers between devices, body(): sent = lax.ppermute(over[half:], axis, flip(mesh.shape[axis], bit))  71.3 us
    ppermute x7, waiting for transfers between devices, body(): lax.ppermute(held, axis, flip(mesh.shape[axis], bit))  63.9 us
    ppermute x7, starting transfers between devices, body(): lax.ppermute(held, axis, flip(mesh.shape[axis], bit))  37.4 us
    ppermute x7, starting transfers between devices, body(): sent = lax.ppermute(over[half:], axis, flip(mesh.shape[axis], bit))  35.8 us
    all_to_all x1, starting transfers between devices, body(): lax.all_to_all(done, E_AXES, 0, 0, tiled=True)  16.9 us
    all_to_all x1, starting transfers between devices, body(): lax.all_to_all(main.reshape(experts, SLOT, width), E_AXES, 0, 0, tiled=True)  16 us
    ppermute x1, waiting for transfers between devices, gather_ring(): behind = lax.ppermute(x, 'dp', ring(4, 1))  11.5 us
    concatenate x4, local copies, waits for them, and re-layouts, body(): jnp.concatenate([held, lax.ppermute(held, axis, flip(mesh.shape[axis], bi...  8.65 us
  transfers between devices with their start and end apart: 22, of which 12 were waited for; matrix products, arithmetic and copies ran while one was open for 10% of the time, Pallas kernels for 0%

profile of v1, /device:TPU:8, one launch (start us, length us, event | category | flops | bytes accessed | tf_op | source)
XLA Modules:
  0.0 334.3 jit_solution(1821286051786043974)
XLA Ops:
  10.9 15.7 %collective-permute-start = (bf16[1,8192]{1,0:T(2,128)(2,1)S(1)}, bf16[1,8192]{1,0:T(2,128)(2,1)S(1)}, u32[]{:S(2)}, u32[]{:S(2)}) collective-permute-start(bf16[1,8192]{1,0:T(2,128)(2,1)S(1)} %bitcast.37), channel_id=1, source_target_pairs={{0,256},{32,288},{64,320},{96,352},{128,384},{160,416},{192,448},{... | collective-permute-start | bytes 49160 | tf_op jit(solution)/shard_map/ppermute | solution.py:117
  28.6 6.1 %collective-permute-start.1 = (bf16[2,8192]{1,0:T(2,128)(2,1)S(1)}, bf16[2,8192]{1,0:T(2,128)(2,1)S(1)}, u32[]{:S(2)}, u32[]{:S(2)}) collective-permute-start(bf16[2,8192]{1,0:T(2,128)(2,1)S(1)} %pad_maximum_fusion.5), channel_id=1, source_target_pairs={{0,128},{32,160},{64,192},{96,224},{128,0},{160,32},{192,64},{224,... | collective-permute-start | bytes 98312 | tf_op jit(solution)/shard_map/ppermute | solution.py:117
  34.7 3.9 %collective-permute-done.1 = bf16[2,8192]{1,0:T(2,128)(2,1)S(1)} collective-permute-done((bf16[2,8192]{1,0:T(2,128)(2,1)S(1)}, bf16[2,8192]{1,0:T(2,128)(2,1)S(1)}, u32[]{:S(2)}, u32[]{:S(2)}) %collective-permute-start.1) | collective-permute-done | bytes 32800 | tf_op jit(solution)/shard_map/ppermute | solution.py:117
  38.8 3.7 %collective-permute-start.2 = (bf16[4,8192]{1,0:T(4,128)(2,1)S(1)}, bf16[4,8192]{1,0:T(4,128)(2,1)S(1)}, u32[]{:S(2)}, u32[]{:S(2)}) collective-permute-start(bf16[4,8192]{1,0:T(4,128)(2,1)S(1)} %pad_maximum_fusion.4), channel_id=1, source_target_pairs={{0,64},{32,96},{64,0},{96,32},{128,192},{160,224},{192,128},{224,1... | collective-permute-start | bytes 196616 | tf_op jit(solution)/shard_map/ppermute | solution.py:117
  44.0 16.0 %all-to-all-start = ((bf16[128,2,2048]{2,1,0:T(2,128)(2,1)}), bf16[128,2,2048]{2,1,0:T(2,128)(2,1)S(1)}, u32[]{:S(2)}, u32[]{:S(2)}) async-start(bf16[128,2,2048]{2,1,0:T(2,128)(2,1)} %reshape.57), calls=%async_computation | async-start | bytes 2097152 | tf_op jit(solution)/shard_map/all_to_all | solution.py:113
  60.3 3.4 %collective-permute-start.3 = (bf16[8,8192]{1,0:T(8,128)(2,1)S(1)}, bf16[8,8192]{1,0:T(8,128)(2,1)S(1)}, u32[]{:S(2)}, u32[]{:S(2)}) collective-permute-start(bf16[8,8192]{1,0:T(8,128)(2,1)S(1)} %pad_maximum_fusion.3), channel_id=1, source_target_pairs={{0,32},{32,0},{64,96},{96,64},{128,160},{160,128},{192,224},{224,1... | collective-permute-start | bytes 393224 | tf_op jit(solution)/shard_map/ppermute | solution.py:117
  63.6 45.9 %collective-permute-done.3 = bf16[8,8192]{1,0:T(8,128)(2,1)S(1)} collective-permute-done((bf16[8,8192]{1,0:T(8,128)(2,1)S(1)}, bf16[8,8192]{1,0:T(8,128)(2,1)S(1)}, u32[]{:S(2)}, u32[]{:S(2)}) %collective-permute-start.3) | collective-permute-done | bytes 131104 | tf_op jit(solution)/shard_map/ppermute | solution.py:117
  109.7 4.0 %collective-permute-start.4 = (bf16[16,8192]{1,0:T(8,128)(2,1)S(1)}, bf16[16,8192]{1,0:T(8,128)(2,1)S(1)}, u32[]{:S(2)}, u32[]{:S(2)}) collective-permute-start(bf16[16,8192]{1,0:T(8,128)(2,1)S(1)} %concatenate.44), channel_id=1, source_target_pairs={{0,16},{8,24},{16,0},{24,8},{1,17},{9,25},{17,1},{25,9},{2,18},{10... | collective-permute-start | bytes 786440 | tf_op jit(solution)/shard_map/ppermute | solution.py:117
  113.7 7.2 %collective-permute-done.4 = bf16[16,8192]{1,0:T(8,128)(2,1)S(1)} collective-permute-done((bf16[16,8192]{1,0:T(8,128)(2,1)S(1)}, bf16[16,8192]{1,0:T(8,128)(2,1)S(1)}, u32[]{:S(2)}, u32[]{:S(2)}) %collective-permute-start.4) | collective-permute-done | bytes 262176 | tf_op jit(solution)/shard_map/ppermute | solution.py:117
  121.3 2.5 collective-permute-start.5
  123.8 3.4 %collective-permute-start.9 = (bf16[1024,512]{1,0:T(8,128)(2,1)}, bf16[1024,512]{1,0:T(8,128)(2,1)}, u32[]{:S(2)}, u32[]{:S(2)}) collective-permute-start(bf16[1024,512]{1,0:T(8,128)(2,1)} %bitcast.45), channel_id=1, source_target_pairs={{0,1},{1,2},{2,3},{3,0},{4,5},{5,6},{6,7},{7,4},{8,9},{9,10},{10,1... | collective-permute-start | bytes 3145736 | tf_op jit(solution)/shard_map/ppermute | solution.py:74
  127.2 3.7 %collective-permute-start.7 = (bf16[1024,512]{1,0:T(8,128)(2,1)}, bf16[1024,512]{1,0:T(8,128)(2,1)}, u32[]{:S(2)}, u32[]{:S(2)}) collective-permute-start(bf16[1024,512]{1,0:T(8,128)(2,1)} %bitcast.46), channel_id=1, source_target_pairs={{0,3},{1,0},{2,1},{3,2},{4,7},{5,4},{6,5},{7,6},{8,11},{9,8},{10,9... | collective-permute-start | bytes 3145736 | tf_op jit(solution)/shard_map/ppermute | solution.py:73
  130.9 5.0 %collective-permute-done.5 = bf16[32,8192]{1,0:T(8,128)(2,1)S(1)} collective-permute-done((bf16[32,8192]{1,0:T(8,128)(2,1)S(1)}, bf16[32,8192]{1,0:T(8,128)(2,1)S(1)}, u32[]{:S(2)}, u32[]{:S(2)}) %collective-permute-start.5) | collective-permute-done | bytes 524320 | tf_op jit(solution)/shard_map/ppermute | solution.py:117
  139.4 11.5 %collective-permute-done.9 = bf16[1024,512]{1,0:T(8,128)(2,1)} collective-permute-done((bf16[1024,512]{1,0:T(8,128)(2,1)}, bf16[1024,512]{1,0:T(8,128)(2,1)}, u32[]{:S(2)}, u32[]{:S(2)}) %collective-permute-start.9) | collective-permute-done | bytes 1048608 | tf_op jit(solution)/shard_map/ppermute | solution.py:74
  152.7 2.2 collective-permute-start.10
  156.8 5.0 %collective-permute-start.8 = (bf16[512,512]{1,0:T(8,128)(2,1)}, bf16[512,512]{1,0:T(8,128)(2,1)}, u32[]{:S(2)}, u32[]{:S(2)}) collective-permute-start(bf16[512,512]{1,0:T(8,128)(2,1)} %slice.153), channel_id=1, source_target_pairs={{0,3},{1,0},{2,1},{3,2},{4,7},{5,4},{6,5},{7,6},{8,11},{9,8},{10,9... | collective-permute-start | bytes 1572872 | tf_op jit(solution)/shard_map/ppermute | solution.py:75
  161.9 7.8 %concatenate.47 = bf16[128,8192]{1,0:T(8,128)(2,1)S(1)} concatenate(bf16[1,8192]{1,0:T(2,128)(2,1)S(1)} %bitcast.44, bf16[1,8192]{1,0:T(2,128)(2,1)S(1)} %collective-permute-done, bf16[2,8192]{1,0:T(2,128)(2,1)} %copy-done.8, bf16[4,8192]{1,0:T(4,128)(2,1)} %copy-done.7, bf16[8,8192]{1,0:T(8,128)(2,1)} %copy-done.5, bf16[16,8192]{1,0:T(8,128)(2,1)S(1)} %collective-permute-done.4, ...), dimensions={0} | concatenate | bytes 4194304 | tf_op jit(solution)/shard_map/concatenate | solution.py:117
  170.3 2.9 fusion.11
  176.4 2.3 fusion.4
  187.4 2.0 fusion
  197.8 3.3 collective-permute-start.12
  201.2 12.8 %collective-permute-done.12 = bf16[32,8192]{1,0:T(8,128)(2,1)} collective-permute-done((bf16[32,8192]{1,0:T(8,128)(2,1)}, bf16[32,8192]{1,0:T(8,128)(2,1)}, u32[]{:S(2)}, u32[]{:S(2)}) %collective-permute-start.12) | collective-permute-done | bytes 524320 | tf_op jit(solution)/shard_map/ppermute | solution.py:148
  215.9 4.2 %collective-permute-start.13 = (bf16[16,8192]{1,0:T(8,128)(2,1)S(1)}, bf16[16,8192]{1,0:T(8,128)(2,1)S(1)}, u32[]{:S(2)}, u32[]{:S(2)}) collective-permute-start(bf16[16,8192]{1,0:T(8,128)(2,1)S(1)} %slice.163), channel_id=1, source_target_pairs={{0,16},{8,24},{16,0},{24,8},{1,17},{9,25},{17,1},{25,9},{2,18},{10... | collective-permute-start | bytes 786440 | tf_op jit(solution)/shard_map/ppermute | solution.py:148
  220.2 6.6 %collective-permute-done.13 = bf16[16,8192]{1,0:T(8,128)(2,1)S(1)} collective-permute-done((bf16[16,8192]{1,0:T(8,128)(2,1)S(1)}, bf16[16,8192]{1,0:T(8,128)(2,1)S(1)}, u32[]{:S(2)}, u32[]{:S(2)}) %collective-permute-start.13) | collective-permute-done | bytes 262176 | tf_op jit(solution)/shard_map/ppermute | solution.py:148
  228.5 3.0 collective-permute-start.14
  233.3 16.9 %all-to-all-start.1 = ((bf16[128,2,2048]{2,1,0:T(2,128)(2,1)}), bf16[128,2,2048]{2,1,0:T(2,128)(2,1)S(1)}, u32[]{:S(2)}, u32[]{:S(2)}) async-start(bf16[128,2,2048]{2,1,0:T(2,128)(2,1)} %reshape.60), calls=%async_computation.1 | async-start | bytes 2097152 | tf_op jit(solution)/shard_map/all_to_all | solution.py:137
  251.1 4.3 %collective-permute-start.15 = (bf16[4,8192]{1,0:T(4,128)(2,1)S(1)}, bf16[4,8192]{1,0:T(4,128)(2,1)S(1)}, u32[]{:S(2)}, u32[]{:S(2)}) collective-permute-start(bf16[4,8192]{1,0:T(4,128)(2,1)S(1)} %slice.167), channel_id=1, source_target_pairs={{0,64},{32,96},{64,0},{96,32},{128,192},{160,224},{192,128},{224,1... | collective-permute-start | bytes 196616 | tf_op jit(solution)/shard_map/ppermute | solution.py:148
  255.4 44.8 %collective-permute-done.15 = bf16[4,8192]{1,0:T(4,128)(2,1)S(1)} collective-permute-done((bf16[4,8192]{1,0:T(4,128)(2,1)S(1)}, bf16[4,8192]{1,0:T(4,128)(2,1)S(1)}, u32[]{:S(2)}, u32[]{:S(2)}) %collective-permute-start.15) | collective-permute-done | bytes 65568 | tf_op jit(solution)/shard_map/ppermute | solution.py:148
  300.3 7.6 %collective-permute-start.16 = (bf16[2,8192]{1,0:T(2,128)(2,1)S(1)}, bf16[2,8192]{1,0:T(2,128)(2,1)S(1)}, u32[]{:S(2)}, u32[]{:S(2)}) collective-permute-start(bf16[2,8192]{1,0:T(2,128)(2,1)S(1)} %slice.169), channel_id=1, source_target_pairs={{0,128},{32,160},{64,192},{96,224},{128,0},{160,32},{192,64},{224,... | collective-permute-start | bytes 98312 | tf_op jit(solution)/shard_map/ppermute | solution.py:148
  308.0 2.4 collective-permute-done.16
  310.5 11.4 %collective-permute-start.17 = (bf16[1,8192]{1,0:T(2,128)(2,1)S(1)}, bf16[1,8192]{1,0:T(2,128)(2,1)S(1)}, u32[]{:S(2)}, u32[]{:S(2)}) collective-permute-start(bf16[1,8192]{1,0:T(2,128)(2,1)S(1)} %slice.171), channel_id=1, source_target_pairs={{0,256},{32,288},{64,320},{96,352},{128,384},{160,416},{192,448},{... | collective-permute-start | bytes 49160 | tf_op jit(solution)/shard_map/ppermute | solution.py:148
  322.1 3.0 collective-permute-done.17
  (102 shorter events, 43.8 us)
Async XLA Ops:
  6.5 163.8 %all-gather.3.cloned.1.call-start = ((), (), s32[]{:S(2)}) async-start(), calls=%async_computation.2 | async-start | bytes 5242880 | tf_op jit(solution)/shard_map/all_gather | solution.py:109
  7.3 169.1 %all-gather.5.cloned.1.call-start = ((), (), s32[]{:S(2)}) async-start(), calls=%async_computation.3 | async-start | bytes 5242880 | tf_op jit(solution)/shard_map/all_gather | solution.py:110
  10.9 17.6 %collective-permute-start = (bf16[1,8192]{1,0:T(2,128)(2,1)S(1)}, bf16[1,8192]{1,0:T(2,128)(2,1)S(1)}, u32[]{:S(2)}, u32[]{:S(2)}) collective-permute-start(bf16[1,8192]{1,0:T(2,128)(2,1)S(1)} %bitcast.37), channel_id=1, source_target_pairs={{0,256},{32,288},{64,320},{96,352},{128,384},{160,416},{192,448},{... | collective-permute-start | bytes 49160 | tf_op jit(solution)/shard_map/ppermute | solution.py:117
  28.6 10.1 %collective-permute-start.1 = (bf16[2,8192]{1,0:T(2,128)(2,1)S(1)}, bf16[2,8192]{1,0:T(2,128)(2,1)S(1)}, u32[]{:S(2)}, u32[]{:S(2)}) collective-permute-start(bf16[2,8192]{1,0:T(2,128)(2,1)S(1)} %pad_maximum_fusion.5), channel_id=1, source_target_pairs={{0,128},{32,160},{64,192},{96,224},{128,0},{160,32},{192,64},{224,... | collective-permute-start | bytes 98312 | tf_op jit(solution)/shard_map/ppermute | solution.py:117
  38.7 97.2 %copy-start.8 = (bf16[2,8192]{1,0:T(2,128)(2,1)}, bf16[2,8192]{1,0:T(2,128)(2,1)S(1)}, u32[]{:S(2)}) copy-start(bf16[2,8192]{1,0:T(2,128)(2,1)S(1)} %collective-permute-done.1) | copy-start | bytes 98308
  38.8 21.3 %collective-permute-start.2 = (bf16[4,8192]{1,0:T(4,128)(2,1)S(1)}, bf16[4,8192]{1,0:T(4,128)(2,1)S(1)}, u32[]{:S(2)}, u32[]{:S(2)}) collective-permute-start(bf16[4,8192]{1,0:T(4,128)(2,1)S(1)} %pad_maximum_fusion.4), channel_id=1, source_target_pairs={{0,64},{32,96},{64,0},{96,32},{128,192},{160,224},{192,128},{224,1... | collective-permute-start | bytes 196616 | tf_op jit(solution)/shard_map/ppermute | solution.py:117
  44.0 125.8 %all-to-all-start = ((bf16[128,2,2048]{2,1,0:T(2,128)(2,1)}), bf16[128,2,2048]{2,1,0:T(2,128)(2,1)S(1)}, u32[]{:S(2)}, u32[]{:S(2)}) async-start(bf16[128,2,2048]{2,1,0:T(2,128)(2,1)} %reshape.57), calls=%async_computation | async-start | bytes 2097152 | tf_op jit(solution)/shard_map/all_to_all | solution.py:113
  60.1 92.6 %copy-start.7 = (bf16[4,8192]{1,0:T(4,128)(2,1)}, bf16[4,8192]{1,0:T(4,128)(2,1)S(1)}, u32[]{:S(2)}) copy-start(bf16[4,8192]{1,0:T(4,128)(2,1)S(1)} %collective-permute-done.2) | copy-start | bytes 196612
  60.3 49.3 %collective-permute-start.3 = (bf16[8,8192]{1,0:T(8,128)(2,1)S(1)}, bf16[8,8192]{1,0:T(8,128)(2,1)S(1)}, u32[]{:S(2)}, u32[]{:S(2)}) collective-permute-start(bf16[8,8192]{1,0:T(8,128)(2,1)S(1)} %pad_maximum_fusion.3), channel_id=1, source_target_pairs={{0,32},{32,0},{64,96},{96,64},{128,160},{160,128},{192,224},{224,1... | collective-permute-start | bytes 393224 | tf_op jit(solution)/shard_map/ppermute | solution.py:117
  109.5 43.2 %copy-start.5 = (bf16[8,8192]{1,0:T(8,128)(2,1)}, bf16[8,8192]{1,0:T(8,128)(2,1)S(1)}, u32[]{:S(2)}) copy-start(bf16[8,8192]{1,0:T(8,128)(2,1)S(1)} %collective-permute-done.3) | copy-start | bytes 393220
  109.7 11.3 %collective-permute-start.4 = (bf16[16,8192]{1,0:T(8,128)(2,1)S(1)}, bf16[16,8192]{1,0:T(8,128)(2,1)S(1)}, u32[]{:S(2)}, u32[]{:S(2)}) collective-permute-start(bf16[16,8192]{1,0:T(8,128)(2,1)S(1)} %concatenate.44), channel_id=1, source_target_pairs={{0,16},{8,24},{16,0},{24,8},{1,17},{9,25},{17,1},{25,9},{2,18},{10... | collective-permute-start | bytes 786440 | tf_op jit(solution)/shard_map/ppermute | solution.py:117
  121.3 14.6 %collective-permute-start.5 = (bf16[32,8192]{1,0:T(8,128)(2,1)S(1)}, bf16[32,8192]{1,0:T(8,128)(2,1)S(1)}, u32[]{:S(2)}, u32[]{:S(2)}) collective-permute-start(bf16[32,8192]{1,0:T(8,128)(2,1)S(1)} %concatenate.45), channel_id=1, source_target_pairs={{0,8},{8,0},{16,24},{24,16},{1,9},{9,1},{17,25},{25,17},{2,10},{10... | collective-permute-start | bytes 1572872 | tf_op jit(solution)/shard_map/ppermute | solution.py:117
  123.8 27.1 %collective-permute-start.9 = (bf16[1024,512]{1,0:T(8,128)(2,1)}, bf16[1024,512]{1,0:T(8,128)(2,1)}, u32[]{:S(2)}, u32[]{:S(2)}) collective-permute-start(bf16[1024,512]{1,0:T(8,128)(2,1)} %bitcast.45), channel_id=1, source_target_pairs={{0,1},{1,2},{2,3},{3,0},{4,5},{5,6},{6,7},{7,4},{8,9},{9,10},{10,1... | collective-permute-start | bytes 3145736 | tf_op jit(solution)/shard_map/ppermute | solution.py:74
  127.2 27.7 %collective-permute-start.7 = (bf16[1024,512]{1,0:T(8,128)(2,1)}, bf16[1024,512]{1,0:T(8,128)(2,1)}, u32[]{:S(2)}, u32[]{:S(2)}) collective-permute-start(bf16[1024,512]{1,0:T(8,128)(2,1)} %bitcast.46), channel_id=1, source_target_pairs={{0,3},{1,0},{2,1},{3,2},{4,7},{5,4},{6,5},{7,6},{8,11},{9,8},{10,9... | collective-permute-start | bytes 3145736 | tf_op jit(solution)/shard_map/ppermute | solution.py:73
  135.8 21.0 %copy-start.6 = (bf16[32,8192]{1,0:T(8,128)(2,1)}, bf16[32,8192]{1,0:T(8,128)(2,1)S(1)}, u32[]{:S(2)}) copy-start(bf16[32,8192]{1,0:T(8,128)(2,1)S(1)} %collective-permute-done.5) | copy-start | bytes 1572868
  136.3 25.6 %collective-permute-start.6 = (bf16[64,8192]{1,0:T(8,128)(2,1)S(1)}, bf16[64,8192]{1,0:T(8,128)(2,1)}, u32[]{:S(2)}, u32[]{:S(2)}) collective-permute-start(bf16[64,8192]{1,0:T(8,128)(2,1)S(1)} %concatenate.46), channel_id=1, source_target_pairs={{0,4},{4,0},{1,5},{5,1},{2,6},{6,2},{3,7},{7,3},{8,12},{12,8},{9,1... | collective-permute-start | bytes 3145736 | tf_op jit(solution)/shard_map/ppermute | solution.py:117
  152.7 32.7 %collective-permute-start.10 = (bf16[512,512]{1,0:T(8,128)(2,1)}, bf16[512,512]{1,0:T(8,128)(2,1)}, u32[]{:S(2)}, u32[]{:S(2)}) collective-permute-start(bf16[512,512]{1,0:T(8,128)(2,1)} %slice.154), channel_id=1, source_target_pairs={{0,1},{1,2},{2,3},{3,0},{4,5},{5,6},{6,7},{7,4},{8,9},{9,10},{10,1... | collective-permute-start | bytes 1572872 | tf_op jit(solution)/shard_map/ppermute | solution.py:76
  156.8 28.6 %collective-permute-start.8 = (bf16[512,512]{1,0:T(8,128)(2,1)}, bf16[512,512]{1,0:T(8,128)(2,1)}, u32[]{:S(2)}, u32[]{:S(2)}) collective-permute-start(bf16[512,512]{1,0:T(8,128)(2,1)} %slice.153), channel_id=1, source_target_pairs={{0,3},{1,0},{2,1},{3,2},{4,7},{5,4},{6,5},{7,6},{8,11},{9,8},{10,9... | collective-permute-start | bytes 1572872 | tf_op jit(solution)/shard_map/ppermute | solution.py:75
  170.3 2.9 copy-start.10
  176.4 2.7 copy-start.11
  176.4 2.8 copy-start.13
  189.4 1.4 copy-start.2
  191.0 4.7 %collective-permute-start.11 = (bf16[64,8192]{1,0:T(8,128)(2,1)S(1)}, bf16[64,8192]{1,0:T(8,128)(2,1)}, u32[]{:S(2)}, u32[]{:S(2)}) collective-permute-start(bf16[64,8192]{1,0:T(8,128)(2,1)S(1)} %slice.159), channel_id=1, source_target_pairs={{0,4},{4,0},{1,5},{5,1},{2,6},{6,2},{3,7},{7,3},{8,12},{12,8},{9,1... | collective-permute-start | bytes 3145736 | tf_op jit(solution)/shard_map/ppermute | solution.py:148
  197.0 34.6 %copy-start.3 = (bf16[512,2048]{1,0:T(8,128)(2,1)S(1)}, bf16[512,2048]{1,0:T(8,128)(2,1)}, u32[]{:S(2)}) copy-start(bf16[512,2048]{1,0:T(8,128)(2,1)} %copy-done.2) | copy-start | bytes 6291460
  197.8 16.2 %collective-permute-start.12 = (bf16[32,8192]{1,0:T(8,128)(2,1)}, bf16[32,8192]{1,0:T(8,128)(2,1)}, u32[]{:S(2)}, u32[]{:S(2)}) collective-permute-start(bf16[32,8192]{1,0:T(8,128)(2,1)} %slice.161), channel_id=1, source_target_pairs={{0,8},{8,0},{16,24},{24,16},{1,9},{9,1},{17,25},{25,17},{2,10},{10... | collective-permute-start | bytes 1572872 | tf_op jit(solution)/shard_map/ppermute | solution.py:148
  215.9 10.9 %collective-permute-start.13 = (bf16[16,8192]{1,0:T(8,128)(2,1)S(1)}, bf16[16,8192]{1,0:T(8,128)(2,1)S(1)}, u32[]{:S(2)}, u32[]{:S(2)}) collective-permute-start(bf16[16,8192]{1,0:T(8,128)(2,1)S(1)} %slice.163), channel_id=1, source_target_pairs={{0,16},{8,24},{16,0},{24,8},{1,17},{9,25},{17,1},{25,9},{2,18},{10... | collective-permute-start | bytes 786440 | tf_op jit(solution)/shard_map/ppermute | solution.py:148
  228.5 21.6 %collective-permute-start.14 = (bf16[8,8192]{1,0:T(8,128)(2,1)}, bf16[8,8192]{1,0:T(8,128)(2,1)}, u32[]{:S(2)}, u32[]{:S(2)}) collective-permute-start(bf16[8,8192]{1,0:T(8,128)(2,1)} %slice.165), channel_id=1, source_target_pairs={{0,32},{32,0},{64,96},{96,64},{128,160},{160,128},{192,224},{224,1... | collective-permute-start | bytes 393224 | tf_op jit(solution)/shard_map/ppermute | solution.py:148
  231.7 90.2 %copy-start.9 = (f32[128,2]{0,1:T(2,128)S(1)}, f32[128,2]{0,1:T(2,128)}, u32[]{:S(2)}) copy-start(f32[128,2]{0,1:T(2,128)} %param.10) | copy-start | bytes 3076
  233.3 92.0 %all-to-all-start.1 = ((bf16[128,2,2048]{2,1,0:T(2,128)(2,1)}), bf16[128,2,2048]{2,1,0:T(2,128)(2,1)S(1)}, u32[]{:S(2)}, u32[]{:S(2)}) async-start(bf16[128,2,2048]{2,1,0:T(2,128)(2,1)} %reshape.60), calls=%async_computation.1 | async-start | bytes 2097152 | tf_op jit(solution)/shard_map/all_to_all | solution.py:137
  251.1 49.1 %collective-permute-start.15 = (bf16[4,8192]{1,0:T(4,128)(2,1)S(1)}, bf16[4,8192]{1,0:T(4,128)(2,1)S(1)}, u32[]{:S(2)}, u32[]{:S(2)}) collective-permute-start(bf16[4,8192]{1,0:T(4,128)(2,1)S(1)} %slice.167), channel_id=1, source_target_pairs={{0,64},{32,96},{64,0},{96,32},{128,192},{160,224},{192,128},{224,1... | collective-permute-start | bytes 196616 | tf_op jit(solution)/shard_map/ppermute | solution.py:148
  300.3 10.1 %collective-permute-start.16 = (bf16[2,8192]{1,0:T(2,128)(2,1)S(1)}, bf16[2,8192]{1,0:T(2,128)(2,1)S(1)}, u32[]{:S(2)}, u32[]{:S(2)}) collective-permute-start(bf16[2,8192]{1,0:T(2,128)(2,1)S(1)} %slice.169), channel_id=1, source_target_pairs={{0,128},{32,160},{64,192},{96,224},{128,0},{160,32},{192,64},{224,... | collective-permute-start | bytes 98312 | tf_op jit(solution)/shard_map/ppermute | solution.py:148
  310.5 14.6 %collective-permute-start.17 = (bf16[1,8192]{1,0:T(2,128)(2,1)S(1)}, bf16[1,8192]{1,0:T(2,128)(2,1)S(1)}, u32[]{:S(2)}, u32[]{:S(2)}) collective-permute-start(bf16[1,8192]{1,0:T(2,128)(2,1)S(1)} %slice.171), channel_id=1, source_target_pairs={{0,256},{32,288},{64,320},{96,352},{128,384},{160,416},{192,448},{... | collective-permute-start | bytes 49160 | tf_op jit(solution)/shard_map/ppermute | solution.py:148
  (4 other events, 3.8 us)
Sparse Core Ops, SparseCore 0:
  9.5 60.2 all-gather.2
  71.9 56.3 all-gather.4

commit v2 on v1

v2 whole, which is shorter than its diff:
```python
import jax
import jax.numpy as jnp
from jax import lax
from jax.experimental import pallas as pl
from jax.experimental.pallas import tpu as pltpu
from jax.sharding import Mesh, PartitionSpec as P

E_AXES = ("z", "y", "c")
PLANE = ("y", "c")
SLOT = 2
VMEM = pl.BlockSpec(memory_space=pltpu.VMEM)
SMEM = pl.BlockSpec(memory_space=pltpu.SMEM)


def matmul(a, b):
    return jnp.dot(a, b, preferred_element_type=jnp.float32)


def iota(shape, dim):
    return lax.broadcasted_iota(jnp.int32, shape, dim)


def first_kernel(plane, tok_ref, gain_ref, rt_ref, out_ref, tgt_ref, hot_ref):
    toks, width = tok_ref.shape
    slots = out_ref.shape[0]
    experts, piece = slots // SLOT, width // plane
    x = tok_ref[...].astype(jnp.float32)
    scale = lax.rsqrt(jnp.mean(x * x, axis=1, keepdims=True) + 1e-06)
    normed = (x * scale * gain_ref[...]).astype(jnp.bfloat16)
    lane = iota((toks, experts), 1)
    ids = [rt_ref[:, k : k + 1] for k in range(2)]
    hots = [i == lane for i in ids]
    both = (hots[0] | hots[1]).astype(jnp.float32)
    before = (iota((toks, toks), 0) > iota((toks, toks), 1)).astype(jnp.bfloat16)
    count = matmul(before, both.astype(jnp.bfloat16))
    busy = jnp.sum(both, axis=0, keepdims=True) > SLOT + 0.5
    eid = iota((1, experts), 1)
    low = jnp.min(jnp.where(busy, eid, experts - 1), axis=1, keepdims=True)
    high = jnp.max(jnp.where(busy, eid, 0), axis=1, keepdims=True)
    targets = []
    for k in range(2):
        rank = jnp.sum(jnp.where(hots[k], count, 0.0), axis=1, keepdims=True).astype(jnp.int32)
        over = slots + jnp.where(ids[k] == high, SLOT, 0) + rank - SLOT
        targets.append(jnp.where(rank < SLOT, ids[k] * SLOT + rank, over))
        tgt_ref[:, k : k + 1] = targets[k]
    slot = iota((toks, slots), 1)

    def pick(wanted):
        chosen = ((wanted == targets[0]) | (wanted == targets[1])).astype(jnp.float32)
        return chosen.T.astype(jnp.bfloat16)

    out_ref[:, :width] = matmul(pick(slot), normed).astype(jnp.bfloat16)
    owner = (iota((slots, toks), 0) // SLOT) % plane
    for h in range(2):
        chosen = pick(slots + h * SLOT + slot % SLOT)
        total = jnp.zeros((slots, piece), jnp.float32)
        for j in range(plane):
            part = matmul(chosen, normed[:, j * piece : (j + 1) * piece])
            total = jnp.where(owner[:, :1] == j, part, total)
        out_ref[:, width + h * piece : width + (h + 1) * piece] = total.astype(jnp.bfloat16)
    hot_ref[:, 0:1] = low
    hot_ref[:, 1:2] = high


def last_kernel(plane, hot_ref, res_ref, tgt_ref, gs_ref, out_ref):
    toks, width = out_ref.shape
    slots, piece = res_ref.shape[0], width // plane
    weights = gs_ref[...] / jnp.sum(gs_ref[...], axis=1, keepdims=True)

    def mix(wanted, alive=True):
        hits = [(wanted == tgt_ref[:, k : k + 1]) & alive for k in range(2)]
        exact = sum(jnp.where(hits[k], weights[:, k : k + 1], 0.0) for k in range(2))
        coarse = exact.astype(jnp.bfloat16)
        return (exact - coarse.astype(jnp.float32)).astype(jnp.bfloat16), coarse

    usual = mix(iota((toks, slots), 1))
    spot = iota((toks, plane * SLOT), 1)
    over = []
    for h in range(2):
        start = pl.multiple_of(hot_ref[h] // plane * (plane * SLOT), plane * SLOT)
        over.append(res_ref[pl.ds(start, plane * SLOT), width + h * piece : width + (h + 1) * piece])
    for j in range(plane):
        cols = slice(j * piece, (j + 1) * piece)
        total = sum(matmul(p, res_ref[:, cols]) for p in usual)
        for h in range(2):
            parts = mix(slots + h * SLOT + spot % SLOT, spot // SLOT == j)
            total += sum(matmul(p, over[h]) for p in parts)
        out_ref[:, cols] = total.astype(jnp.bfloat16)


def hidden_of(rows, both_ref, hid_ref):
    for q in range(both_ref.shape[0]):
        cols = both_ref.shape[2] // 2
        g, u = matmul(rows, both_ref[q, :, :cols]), matmul(rows, both_ref[q, :, cols:])
        hid_ref[:, q * cols : (q + 1) * cols] = (jax.nn.silu(g) * u).astype(jnp.bfloat16)


def results(hidden, down, at):
    own, ahead, far_a, far_b, behind = down
    half = far_a.shape[0]
    yield at, matmul(hidden, own[...])
    yield lax.rem(at + 1, 4), matmul(hidden, ahead[...])
    yield lax.rem(at + 2, 4), matmul(hidden[:, :half], far_a[...]) + matmul(hidden[:, half:], far_b[...])
    yield lax.rem(at + 3, 4), matmul(hidden, behind[...])


def main_kernel(at_ref, rows_ref, both_ref, *refs):
    down, out_ref, hid_ref = refs[:5], *refs[5:]
    hidden_of(rows_ref[:, : both_ref.shape[1]], both_ref, hid_ref)
    for index, value in results(hid_ref[...], down, at_ref[0]):
        cols = value.shape[1]
        out_ref[:, pl.ds(pl.multiple_of(index * cols, cols), cols)] = value.astype(jnp.bfloat16)


def extra_kernel(at_ref, rows_ref, both_ref, *refs):
    down, out_ref, row_ref, hid_ref = refs[:5], *refs[5:]
    pieces, _, piece = rows_ref.shape
    for j in range(pieces):
        row_ref[:, j * piece : (j + 1) * piece] = rows_ref[j]
    hidden_of(row_ref[...], both_ref, hid_ref)
    for index, value in results(hid_ref[...], down, at_ref[0]):
        parts = value.shape[1] // piece
        for i in range(parts):
            out_ref[index * parts + i] = value[:, i * piece : (i + 1) * piece].astype(jnp.bfloat16)


def ring(n, k):
    return [(i, (i + k) % n) for i in range(n)]


def gather_ring(x):
    half = x.shape[0] // 2
    ahead, behind = lax.ppermute(x, "dp", ring(4, -1)), lax.ppermute(x, "dp", ring(4, 1))
    far_a = lax.ppermute(ahead[:half], "dp", ring(4, -1))
    far_b = lax.ppermute(behind[half:], "dp", ring(4, 1))
    return x, ahead, far_a, far_b, behind


def call(kernel, out, *args, scalars=0, scratch=()):
    return pl.pallas_call(
        kernel,
        out_shape=out,
        in_specs=[SMEM] * scalars + [VMEM] * (len(args) - scalars),
        out_specs=jax.tree.map(lambda _: VMEM, out),
        scratch_shapes=list(scratch),
        compiler_params=pltpu.CompilerParams(vmem_limit_bytes=44 * 1024 * 1024),
    )(*args)


def body(mesh, tokens, norm_gain, routing, gate_scores, w_gate, w_up, w_down):
    toks, width = tokens.shape
    plane = mesh.shape["y"] * mesh.shape["c"]
    experts = mesh.shape["z"] * plane
    slots, piece = experts * SLOT, width // plane
    bf16, i32, shape = jnp.bfloat16, jnp.int32, jax.ShapeDtypeStruct
    units = w_gate.shape[2] * 4

    both = lax.all_gather(jnp.concatenate([w_gate[0], w_up[0]], 1), "dp", axis=0, tiled=False)
    down = gather_ring(w_down[0])
    sent, target, hot = call(
        lambda *refs: first_kernel(plane, *refs),
        [shape((slots, width + 2 * piece), bf16), shape((toks, 2), i32), shape((1, 2), i32)],
        tokens,
        norm_gain.reshape(1, width),
        routing,
    )
    trade = lambda x: lax.all_to_all(
        x.reshape(experts, SLOT, x.shape[1]), E_AXES, 0, 0, tiled=True
    ).reshape(x.shape)
    at = lax.axis_index("dp").reshape(1)
    z = lax.axis_index("z")
    hot = hot.reshape(2)
    low, high = hot[0], hot[1]

    got = trade(sent)
    to_low = (jnp.arange(plane) == low % plane) & (z == low // plane)
    packed = jnp.where(
        to_low[:, None, None], got[None, :, width : width + piece], got[None, :, width + piece :]
    )
    pieces = lax.all_to_all(packed, PLANE, 0, 0, tiled=True)
    hid = pltpu.VMEM((slots, units), bf16)
    over = call(
        extra_kernel,
        shape((plane, slots, piece), bf16),
        at, pieces, both, *down,
        scalars=1,
        scratch=[pltpu.VMEM((slots, width), bf16), hid],
    )
    over = lax.all_to_all(over, PLANE, 0, 0, tiled=True)
    done = call(main_kernel, shape((slots, width), bf16), at, got, both, *down, scalars=1, scratch=[hid])
    take = lambda h: lax.dynamic_index_in_dim(over, h % plane, 0, keepdims=False)
    back = trade(jnp.concatenate([done, take(low), take(high)], 1))
    return call(
        lambda *refs: last_kernel(plane, *refs),
        shape((toks, width), bf16),
        hot, back, target, gate_scores,
        scalars=1,
    )


def solution(mesh):
    fine = Mesh(mesh.devices.reshape(16, 4, 2, 4), ("z", "y", "c", "dp"))
    rows = P((*E_AXES, "dp"), None)
    weights = P(E_AXES, None, "dp")
    return jax.shard_map(
        lambda *args: body(fine, *args),
        mesh=fine,
        in_specs=(rows, P(), rows, rows, weights, weights, weights),
        out_specs=rows,
        check_vma=False,
    )
```

time: 336 us -> 263 us (0.78)
  the two profiles are of different devices: /device:TPU:8 before, /device:TPU:33 now
where the time goes in v2:
time: 263 us; the launch traced here: 262 us
  waiting for transfers between devices  148 us (56%)
  starting transfers between devices  56.9 us (22%)
  Pallas kernels  19 us (7%)
  between operations  18.3 us (7%)
  local copies, waits for them, and re-layouts  13.5 us (5%)
  other arithmetic  6.64 us (3%)
    all_to_all x2, waiting for transfers between devices, body(): lax.all_to_all(x.reshape(experts, SLOT, x.shape[1]), E_AXES, 0, 0, tiled=...  123 us
    all_to_all x2, starting transfers between devices, body(): lax.all_to_all(x.reshape(experts, SLOT, x.shape[1]), E_AXES, 0, 0, tiled=...  35.2 us
    ppermute x1, waiting for transfers between devices, gather_ring(): far_a = lax.ppermute(ahead[:half], 'dp', ring(4, -1))  20.1 us
    pallas_call x4, Pallas kernels, call(): pl.pallas_call(kernel, out_shape=out, in_specs=[SMEM] * scalars + [VMEM]...  19 us
  transfers between devices with their start and end apart: 9, of which 6 were waited for; matrix products, arithmetic and copies ran while one was open for 4% of the time, Pallas kernels for 3%

profile of v2, /device:TPU:33, one launch (start us, length us, event | category | flops | bytes accessed | tf_op | source)
XLA Modules:
  0.0 262.3 jit_solution(5363710217845037799)
XLA Ops:
  6.5 3.1 %pad_maximum_fusion = bf16[2048,512]{1,0:T(8,128)(2,1)} fusion(bf16[2048,256]{1,0:T(8,128)(2,1)} %bitcast.13, bf16[2048,256]{1,0:T(8,128)(2,1)} %bitcast.14), kind=kLoop, calls=%fused_computation | loop fusion | flops 4194304 | bytes 4194304 | tf_op jit(solution)/shard_map/concatenate | solution.py:158
  9.7 0.6 copy-done.4
  10.7 1.5 shard_map.73
  12.2 1.4 reshape.38
  13.6 19.9 %all-to-all-start = ((bf16[128,2,2560]{2,1,0:T(2,128)(2,1)}), bf16[128,2,2560]{2,1,0:T(2,128)(2,1)}, u32[]{:S(2)}, u32[]{:S(2)}) async-start(bf16[128,2,2560]{2,1,0:T(2,128)(2,1)} %reshape.38), calls=%async_computation | async-start | bytes 2621440 | tf_op jit(solution)/shard_map/all_to_all | solution.py:167
  33.5 4.4 %collective-permute-start = (bf16[1024,512]{1,0:T(8,128)(2,1)}, bf16[1024,512]{1,0:T(8,128)(2,1)S(1)}, u32[]{:S(2)}, u32[]{:S(2)}) collective-permute-start(bf16[1024,512]{1,0:T(8,128)(2,1)} %bitcast.6.refs_0_), channel_id=1, source_target_pairs={{0,3},{1,0},{2,1},{3,2},{4,7},{5,4},{6,5},{7,6},{8,11},{9,8},{10,9... | collective-permute-start | bytes 3145736 | tf_op jit(solution)/shard_map/ppermute | solution.py:133
  37.9 1.9 collective-permute-start.2
  39.8 0.7 fusion.1
  43.1 56.5 %all-to-all-done = bf16[128,2,2560]{2,1,0:T(2,128)(2,1)} async-done(((bf16[128,2,2560]{2,1,0:T(2,128)(2,1)}), bf16[128,2,2560]{2,1,0:T(2,128)(2,1)}, u32[]{:S(2)}, u32[]{:S(2)}) %all-to-all-start) | async-done | bytes 1310752 | tf_op jit(solution)/shard_map/all_to_all | solution.py:167
  99.5 3.2 %reshape.39.rows_ref = bf16[256,2560]{1,0:T(8,128)(2,1)S(1)} reshape(bf16[128,2,2560]{2,1,0:T(2,128)(2,1)} %all-to-all-done) | data formatting | bytes 2621440 | tf_op jit(solution)/shard_map/reshape | solution.py:169
  102.8 1.2 broadcast_select_fusion
  103.9 4.2 %all-to-all-start.1 = ((bf16[8,256,256]{2,1,0:T(8,128)(2,1)}), bf16[8,256,256]{2,1,0:T(8,128)(2,1)}, u32[]{:S(2)}, u32[]{:S(2)}) async-start(bf16[8,256,256]{2,1,0:T(8,128)(2,1)} %broadcast_select_fusion), calls=%async_computation.1 | async-start | bytes 2097152 | tf_op jit(solution)/shard_map/all_to_all | solution.py:180
  108.1 0.8 slice.26
  109.0 4.4 %collective-permute-start.1 = (bf16[512,512]{1,0:T(8,128)(2,1)}, bf16[512,512]{1,0:T(8,128)(2,1)}, u32[]{:S(2)}, u32[]{:S(2)}) collective-permute-start(bf16[512,512]{1,0:T(8,128)(2,1)} %slice.26), channel_id=1, source_target_pairs={{0,3},{1,0},{2,1},{3,2},{4,7},{5,4},{6,5},{7,6},{8,11},{9,8},{10,9... | collective-permute-start | bytes 1572872 | tf_op jit(solution)/shard_map/ppermute | solution.py:134
  113.4 0.8 slice.27
  114.2 1.9 collective-permute-start.3
  116.1 20.1 %collective-permute-done.1.refs_2_ = bf16[512,512]{1,0:T(8,128)(2,1)} collective-permute-done((bf16[512,512]{1,0:T(8,128)(2,1)}, bf16[512,512]{1,0:T(8,128)(2,1)}, u32[]{:S(2)}, u32[]{:S(2)}) %collective-permute-start.1) | collective-permute-done | bytes 524320 | tf_op jit(solution)/shard_map/ppermute | solution.py:134
  136.2 1.9 collective-permute-done.3.refs_3_
  138.1 0.3 all-gather.3.cloned.1.call-done
  138.4 7.6 %shard_map.75 = bf16[8,256,256]{2,1,0:T(8,128)(2,1)S(1)} custom-call(s32[1]{0:T(128)} %bitcast.2.at_ref, bf16[8,256,256]{2,1,0:T(8,128)(2,1)} %all-to-all-done.1.rows_ref, bf16[4,2048,512]{2,1,0:T(8,128)(2,1)} %bitcast.11, bf16[1024,512]{1,0:T(8,128)(2,1)} %bitcast.6.refs_0_, bf16[1024,512]{1,0:T(8,128)(2,1)S(1)} %collective-permute-done.refs_1_, ...), custom_call_target="tpu_custom_call" | custom-call | tf_op jit(solution)/shard_map/pallas_call | solution.py:140
  146.0 1.0 copy-done
  147.0 5.0 %all-to-all-start.2 = ((bf16[8,256,256]{2,1,0:T(8,128)(2,1)}), bf16[8,256,256]{2,1,0:T(8,128)(2,1)}, u32[]{:S(2)}, u32[]{:S(2)}) async-start(bf16[8,256,256]{2,1,0:T(8,128)(2,1)} %copy-done), calls=%async_computation.2 | async-start | bytes 2097152 | tf_op jit(solution)/shard_map/all_to_all | solution.py:189
  154.0 7.3 %shard_map.74 = bf16[256,2048]{1,0:T(8,128)(2,1)S(1)} custom-call(s32[1]{0:T(128)} %bitcast.2.at_ref, bf16[256,2560]{1,0:T(8,128)(2,1)S(1)} %reshape.39.rows_ref, bf16[4,2048,512]{2,1,0:T(8,128)(2,1)} %bitcast.12, bf16[1024,512]{1,0:T(8,128)(2,1)} %bitcast.6.refs_0_, bf16[1024,512]{1,0:T(8,128)(2,1)S(1)} %collective-permute-done.refs_1_, ...), custom_call_target="tpu_custom_call" | custom-call | tf_op jit(solution)/shard_map/pallas_call | solution.py:140
  161.4 1.0 copy-done.1
  162.4 1.7 concatenate.14
  164.1 3.0 %all-to-all-done.2 = bf16[8,256,256]{2,1,0:T(8,128)(2,1)} async-done(((bf16[8,256,256]{2,1,0:T(8,128)(2,1)}), bf16[8,256,256]{2,1,0:T(8,128)(2,1)}, u32[]{:S(2)}, u32[]{:S(2)}) %all-to-all-start.2) | async-done | bytes 1048608 | tf_op jit(solution)/shard_map/all_to_all | solution.py:189
  167.2 1.0 constant_dynamic-slice_fusion.1
  168.3 2.4 pad_maximum_fusion.1
  170.7 15.3 %all-to-all-start.3 = ((bf16[128,2,2560]{2,1,0:T(2,128)(2,1)}), bf16[128,2,2560]{2,1,0:T(2,128)(2,1)S(1)}, u32[]{:S(2)}, u32[]{:S(2)}) async-start(bf16[128,2,2560]{2,1,0:T(2,128)(2,1)} %pad_maximum_fusion.1), calls=%async_computation.3 | async-start | bytes 2621440 | tf_op jit(solution)/shard_map/all_to_all | solution.py:167
  186.1 66.2 %all-to-all-done.3 = bf16[128,2,2560]{2,1,0:T(2,128)(2,1)S(1)} async-done(((bf16[128,2,2560]{2,1,0:T(2,128)(2,1)}), bf16[128,2,2560]{2,1,0:T(2,128)(2,1)S(1)}, u32[]{:S(2)}, u32[]{:S(2)}) %all-to-all-start.3) | async-done | bytes 1310752 | tf_op jit(solution)/shard_map/all_to_all | solution.py:167
  252.4 0.5 reshape.40.refs_1_
  252.9 2.6 shard_map.76
  (20 shorter events, 0.7 us)
Async XLA Ops:
  6.5 131.9 %all-gather.3.cloned.1.call-start = ((), (), s32[]{:S(2)}) async-start(), calls=%async_computation.4 | async-start | bytes 10485760 | tf_op jit(solution)/shard_map/all_gather | solution.py:158
  9.6 0.7 copy-start.4
  9.6 1.1 copy-start.2
  9.6 1.1 copy-start.3
  13.6 86.0 %all-to-all-start = ((bf16[128,2,2560]{2,1,0:T(2,128)(2,1)}), bf16[128,2,2560]{2,1,0:T(2,128)(2,1)}, u32[]{:S(2)}, u32[]{:S(2)}) async-start(bf16[128,2,2560]{2,1,0:T(2,128)(2,1)} %reshape.38), calls=%async_computation | async-start | bytes 2621440 | tf_op jit(solution)/shard_map/all_to_all | solution.py:167
  33.5 74.7 %collective-permute-start = (bf16[1024,512]{1,0:T(8,128)(2,1)}, bf16[1024,512]{1,0:T(8,128)(2,1)S(1)}, u32[]{:S(2)}, u32[]{:S(2)}) collective-permute-start(bf16[1024,512]{1,0:T(8,128)(2,1)} %bitcast.6.refs_0_), channel_id=1, source_target_pairs={{0,3},{1,0},{2,1},{3,2},{4,7},{5,4},{6,5},{7,6},{8,11},{9,8},{10,9... | collective-permute-start | bytes 3145736 | tf_op jit(solution)/shard_map/ppermute | solution.py:133
  37.9 75.5 %collective-permute-start.2 = (bf16[1024,512]{1,0:T(8,128)(2,1)}, bf16[1024,512]{1,0:T(8,128)(2,1)S(1)}, u32[]{:S(2)}, u32[]{:S(2)}) collective-permute-start(bf16[1024,512]{1,0:T(8,128)(2,1)} %bitcast.6.refs_0_), channel_id=1, source_target_pairs={{0,1},{1,2},{2,3},{3,0},{4,5},{5,6},{6,7},{7,4},{8,9},{9,10},{10,1... | collective-permute-start | bytes 3145736 | tf_op jit(solution)/shard_map/ppermute | solution.py:133
  103.9 34.2 %all-to-all-start.1 = ((bf16[8,256,256]{2,1,0:T(8,128)(2,1)}), bf16[8,256,256]{2,1,0:T(8,128)(2,1)}, u32[]{:S(2)}, u32[]{:S(2)}) async-start(bf16[8,256,256]{2,1,0:T(8,128)(2,1)} %broadcast_select_fusion), calls=%async_computation.1 | async-start | bytes 2097152 | tf_op jit(solution)/shard_map/all_to_all | solution.py:180
  109.0 27.3 %collective-permute-start.1 = (bf16[512,512]{1,0:T(8,128)(2,1)}, bf16[512,512]{1,0:T(8,128)(2,1)}, u32[]{:S(2)}, u32[]{:S(2)}) collective-permute-start(bf16[512,512]{1,0:T(8,128)(2,1)} %slice.26), channel_id=1, source_target_pairs={{0,3},{1,0},{2,1},{3,2},{4,7},{5,4},{6,5},{7,6},{8,11},{9,8},{10,9... | collective-permute-start | bytes 1572872 | tf_op jit(solution)/shard_map/ppermute | solution.py:134
  114.2 23.9 %collective-permute-start.3 = (bf16[512,512]{1,0:T(8,128)(2,1)}, bf16[512,512]{1,0:T(8,128)(2,1)}, u32[]{:S(2)}, u32[]{:S(2)}) collective-permute-start(bf16[512,512]{1,0:T(8,128)(2,1)} %slice.27), channel_id=1, source_target_pairs={{0,1},{1,2},{2,3},{3,0},{4,5},{5,6},{6,7},{7,4},{8,9},{9,10},{10,1... | collective-permute-start | bytes 1572872 | tf_op jit(solution)/shard_map/ppermute | solution.py:135
  146.0 1.0 copy-start
  147.0 20.2 %all-to-all-start.2 = ((bf16[8,256,256]{2,1,0:T(8,128)(2,1)}), bf16[8,256,256]{2,1,0:T(8,128)(2,1)}, u32[]{:S(2)}, u32[]{:S(2)}) async-start(bf16[8,256,256]{2,1,0:T(8,128)(2,1)} %copy-done), calls=%async_computation.2 | async-start | bytes 2097152 | tf_op jit(solution)/shard_map/all_to_all | solution.py:189
  161.4 1.0 copy-start.1
  168.3 17.7 %copy-start.5 = (f32[128,2]{0,1:T(2,128)S(1)}, f32[128,2]{0,1:T(2,128)}, u32[]{:S(2)}) copy-start(f32[128,2]{0,1:T(2,128)} %param.10) | copy-start | bytes 3076
  170.7 81.7 %all-to-all-start.3 = ((bf16[128,2,2560]{2,1,0:T(2,128)(2,1)}), bf16[128,2,2560]{2,1,0:T(2,128)(2,1)S(1)}, u32[]{:S(2)}, u32[]{:S(2)}) async-start(bf16[128,2,2560]{2,1,0:T(2,128)(2,1)} %pad_maximum_fusion.1), calls=%async_computation.3 | async-start | bytes 2621440 | tf_op jit(solution)/shard_map/all_to_all | solution.py:167
Sparse Core Ops, SparseCore 0:
  9.8 128.5 all-gather.2

commit v3 on v2

--- a/solution.py
+++ b/solution.py
@@ -62,9 +62,9 @@
     hot_ref[:, 1:2] = high
 
 
-def last_kernel(plane, hot_ref, res_ref, tgt_ref, gs_ref, out_ref):
+def last_kernel(plane, hot_ref, res_ref, more_ref, tgt_ref, gs_ref, out_ref):
     toks, width = out_ref.shape
-    slots, piece = res_ref.shape[0], width // plane
+    slots, piece, near = res_ref.shape[0], width // plane, res_ref.shape[1]
     weights = gs_ref[...] / jnp.sum(gs_ref[...], axis=1, keepdims=True)
 
     def mix(wanted, alive=True):
@@ -75,68 +75,101 @@
 
     usual = mix(iota((toks, slots), 1))
     spot = iota((toks, plane * SLOT), 1)
+    base = width - near
     over = []
     for h in range(2):
         start = pl.multiple_of(hot_ref[h] // plane * (plane * SLOT), plane * SLOT)
-        over.append(res_ref[pl.ds(start, plane * SLOT), width + h * piece : width + (h + 1) * piece])
+        over.append(more_ref[pl.ds(start, plane * SLOT), base + h * piece : base + (h + 1) * piece])
     for j in range(plane):
-        cols = slice(j * piece, (j + 1) * piece)
-        total = sum(matmul(p, res_ref[:, cols]) for p in usual)
+        start = j * piece
+        rows = res_ref[:, start : start + piece] if start < near else (
+            more_ref[:, start - near : start - near + piece]
+        )
+        total = sum(matmul(p, rows) for p in usual)
         for h in range(2):
             parts = mix(slots + h * SLOT + spot % SLOT, spot // SLOT == j)
             total += sum(matmul(p, over[h]) for p in parts)
-        out_ref[:, cols] = total.astype(jnp.bfloat16)
-
-
-def hidden_of(rows, both_ref, hid_ref):
-    for q in range(both_ref.shape[0]):
-        cols = both_ref.shape[2] // 2
-        g, u = matmul(rows, both_ref[q, :, :cols]), matmul(rows, both_ref[q, :, cols:])
-        hid_ref[:, q * cols : (q + 1) * cols] = (jax.nn.silu(g) * u).astype(jnp.bfloat16)
-
-
-def results(hidden, down, at):
-    own, ahead, far_a, far_b, behind = down
+        out_ref[:, start : start + piece] = total.astype(jnp.bfloat16)
+
+
+def blocks_of(at, all_ref, own, ahead, far_a, far_b, behind):
+    deep = all_ref.shape[1] * 2 // 3
     half = far_a.shape[0]
-    yield at, matmul(hidden, own[...])
-    yield lax.rem(at + 1, 4), matmul(hidden, ahead[...])
-    yield lax.rem(at + 2, 4), matmul(hidden[:, :half], far_a[...]) + matmul(hidden[:, half:], far_b[...])
-    yield lax.rem(at + 3, 4), matmul(hidden, behind[...])
-
-
-def main_kernel(at_ref, rows_ref, both_ref, *refs):
-    down, out_ref, hid_ref = refs[:5], *refs[5:]
-    hidden_of(rows_ref[:, : both_ref.shape[1]], both_ref, hid_ref)
-    for index, value in results(hid_ref[...], down, at_ref[0]):
+    for k, ref in enumerate((own, ahead, None, behind)):
+        index = lax.rem(at + k, 4)
+        if ref is None:
+            up, right = [far_a, far_b.at[: deep - half]], [far_b.at[deep - half :]]
+        else:
+            up, right = [ref.at[:deep]], [ref.at[deep:]]
+        yield index, [all_ref.at[index, :deep]], up, ([all_ref.at[index, deep:]], right)
+
+
+def product(rows, parts):
+    start, total = 0, None
+    for ref in parts:
+        term = matmul(rows[:, start : start + ref.shape[0]], ref[...])
+        total = term if total is None else total + term
+        start += ref.shape[0]
+    return total
+
+
+def expert(at, rows, weights, hid_ref, put):
+    for index, gate, up, _ in blocks_of(at, *weights):
+        g, u = product(rows, gate), product(rows, up)
+        cols = g.shape[1]
+        hid_ref[:, pl.ds(pl.multiple_of(index * cols, cols), cols)] = (jax.nn.silu(g) * u).astype(
+            jnp.bfloat16
+        )
+    for index, _, _, down in blocks_of(at, *weights):
+        for i, d in enumerate(down):
+            put(index * 2 + i, product(hid_ref[...], d).astype(jnp.bfloat16))
+
+
+def main_kernel(at_ref, rows_ref, *refs):
+    weights, out_ref, hid_ref = refs[:6], *refs[6:]
+
+    def put(index, value):
         cols = value.shape[1]
-        out_ref[:, pl.ds(pl.multiple_of(index * cols, cols), cols)] = value.astype(jnp.bfloat16)
-
-
-def extra_kernel(at_ref, rows_ref, both_ref, *refs):
-    down, out_ref, row_ref, hid_ref = refs[:5], *refs[5:]
+        out_ref[:, pl.ds(pl.multiple_of(index * cols, cols), cols)] = value
+
+    expert(at_ref[0], rows_ref[:, : out_ref.shape[1]], weights, hid_ref, put)
+
+
+def extra_kernel(at_ref, rows_ref, *refs):
+    weights, out_ref, row_ref, hid_ref = refs[:6], *refs[6:]
     pieces, _, piece = rows_ref.shape
     for j in range(pieces):
         row_ref[:, j * piece : (j + 1) * piece] = rows_ref[j]
-    hidden_of(row_ref[...], both_ref, hid_ref)
-    for index, value in results(hid_ref[...], down, at_ref[0]):
-        parts = value.shape[1] // piece
-        for i in range(parts):
-            out_ref[index * parts + i] = value[:, i * piece : (i + 1) * piece].astype(jnp.bfloat16)
+
+    def put(index, value):
+        out_ref[index ^ at_ref[1]] = value
+
+    expert(at_ref[0], row_ref[...], weights, hid_ref, put)
 
 
 def ring(n, k):
     return [(i, (i + k) % n) for i in range(n)]
+
+
+def pass_kernel(ahead_ref, behind_ref, a_ref, b_ref):
+    half = a_ref.shape[0]
+    a_ref[...] = ahead_ref[:half]
+    b_ref[...] = behind_ref[half:]
 
 
 def gather_ring(x):
     half = x.shape[0] // 2
     ahead, behind = lax.ppermute(x, "dp", ring(4, -1)), lax.ppermute(x, "dp", ring(4, 1))
-    far_a = lax.ppermute(ahead[:half], "dp", ring(4, -1))
-    far_b = lax.ppermute(behind[half:], "dp", ring(4, 1))
-    return x, ahead, far_a, far_b, behind
-
-
-def call(kernel, out, *args, scalars=0, scratch=()):
+    part = jax.ShapeDtypeStruct((half, x.shape[1]), x.dtype)
+    a, b = call(pass_kernel, [part, part], ahead, behind, flops=40000000000)
+    return x, ahead, a, b, behind
+
+
+def pass_on(x, ahead, a, b, behind):
+    return x, ahead, lax.ppermute(a, "dp", ring(4, -1)), lax.ppermute(b, "dp", ring(4, 1)), behind
+
+
+def call(kernel, out, *args, scalars=0, scratch=(), flops=None):
     return pl.pallas_call(
         kernel,
         out_shape=out,
@@ -144,6 +177,9 @@
         out_specs=jax.tree.map(lambda _: VMEM, out),
         scratch_shapes=list(scratch),
         compiler_params=pltpu.CompilerParams(vmem_limit_bytes=44 * 1024 * 1024),
+        cost_estimate=None
+        if flops is None
+        else pl.CostEstimate(flops=flops, bytes_accessed=0, transcendentals=0),
     )(*args)
 
 
@@ -155,8 +191,9 @@
     bf16, i32, shape = jnp.bfloat16, jnp.int32, jax.ShapeDtypeStruct
     units = w_gate.shape[2] * 4
 
-    both = lax.all_gather(jnp.concatenate([w_gate[0], w_up[0]], 1), "dp", axis=0, tiled=False)
-    down = gather_ring(w_down[0])
+    cols = w_down.shape[2] // 2
+    gate = lax.all_gather(jnp.concatenate([w_gate[0], w_down[0, :, :cols]], 0), "dp", axis=0, tiled=False)
+    packed = gather_ring(jnp.concatenate([w_up[0], w_down[0, :, cols:]], 0))
     sent, target, hot = call(
         lambda *refs: first_kernel(plane, *refs),
         [shape((slots, width + 2 * piece), bf16), shape((toks, 2), i32), shape((1, 2), i32)],
@@ -172,28 +209,46 @@
     hot = hot.reshape(2)
     low, high = hot[0], hot[1]
 
-    got = trade(sent)
+    packed = pass_on(*packed)
+    got, packed = lax.optimization_barrier((trade(sent), packed))
     to_low = (jnp.arange(plane) == low % plane) & (z == low // plane)
-    packed = jnp.where(
+    parcel = jnp.where(
         to_low[:, None, None], got[None, :, width : width + piece], got[None, :, width + piece :]
     )
-    pieces = lax.all_to_all(packed, PLANE, 0, 0, tiled=True)
+    pieces = lax.all_to_all(parcel, PLANE, 0, 0, tiled=True)
     hid = pltpu.VMEM((slots, units), bf16)
+    done = call(main_kernel, shape((slots, width), bf16), at, got, gate, *packed, scalars=1, scratch=[hid])
+    near = width - 2 * piece
+    tie = lax.optimization_barrier((done, pieces))
+    done, pieces = tie
+    res = trade(done[:, :near])
+    spot = lax.axis_index("y") * mesh.shape["c"] + lax.axis_index("c")
     over = call(
         extra_kernel,
         shape((plane, slots, piece), bf16),
-        at, pieces, both, *down,
+        jnp.stack([at[0], spot]), pieces, gate, *packed,
         scalars=1,
         scratch=[pltpu.VMEM((slots, width), bf16), hid],
     )
-    over = lax.all_to_all(over, PLANE, 0, 0, tiled=True)
-    done = call(main_kernel, shape((slots, width), bf16), at, got, both, *down, scalars=1, scratch=[hid])
-    take = lambda h: lax.dynamic_index_in_dim(over, h % plane, 0, keepdims=False)
-    back = trade(jnp.concatenate([done, take(low), take(high)], 1))
+    over = [over[0]] + [
+        lax.ppermute(over[b], PLANE, [(j, j ^ b) for j in range(plane)]) for b in range(1, plane)
+    ]
+
+    def take(h):
+        gap = spot ^ (h % plane)
+        value = over[0]
+        for b in range(1, plane):
+            value = jnp.where(gap == b, over[b], value)
+        return value
+
+    more, res = lax.optimization_barrier(
+        (jnp.concatenate([done[:, near:], take(low), take(high)], 1), res)
+    )
+    more = trade(more)
     return call(
         lambda *refs: last_kernel(plane, *refs),
         shape((toks, width), bf16),
-        hot, back, target, gate_scores,
+        hot, res, more, target, gate_scores,
         scalars=1,
     )
 

time: 263 us -> 267 us (1.015)
  waiting for transfers between devices: 148 us -> 104 us
  starting transfers between devices: 56.9 us -> 92.9 us
  local copies, waits for them, and re-layouts: 13.5 us -> 24.9 us
    all_to_all x2 -> x3, waiting for transfers between devices: 123 us -> 69.6 us  [body(): lax.all_to_all(x.reshape(experts, SLOT, x.shape[1]), E_AXES, 0, 0, tiled=...]
    ppermute x2 -> x9, starting transfers between devices: 6.29 us -> 27.4 us  [the longest x7 22.2 us: body(): lax.ppermute(over[b], PLANE, [(j, j ^ b) for j in range(plane)])]
    ppermute x2 -> x9, waiting for transfers between devices: 22 us -> 3.49 us  [the longest x7 3.49 us: body(): lax.ppermute(over[b], PLANE, [(j, j ^ b) for j in range(plane)])]
    ppermute x1, waiting for transfers between devices: 0.01 us -> 17.1 us  [gather_ring(): lax.ppermute(x, 'dp', ring(4, -1))]
    all_to_all x2 -> x3, starting transfers between devices: 35.2 us -> 50.6 us  [body(): lax.all_to_all(x.reshape(experts, SLOT, x.shape[1]), E_AXES, 0, 0, tiled=...]
    ppermute x1, waiting for transfers between devices: 0.01 us -> 7.91 us  [gather_ring(): lax.ppermute(x, 'dp', ring(4, 1))]
    reshape x1 -> x3, local copies, waits for them, and re-layouts: 1.42 us -> 7.94 us  [body(): x.reshape(experts, SLOT, x.shape[1])]
    concatenate x2 -> x3, other arithmetic: 5.49 us -> 1.4 us  [the longest x1 1.24 us: body(): jnp.concatenate([w_gate[0], w_down[0, :, :cols]], 0)]
  transfers between devices with their start and end apart: 9 -> 16, of which waited for: 6 -> 8; matrix products, arithmetic and copies ran while one was open for 4% -> 4% of each run, Pallas kernels for 3% -> 7%
where the time goes in v3:
time: 267 us; the launch traced here: 265 us
  waiting for transfers between devices  104 us (39%)
  starting transfers between devices  92.9 us (35%)
  local copies, waits for them, and re-layouts  24.9 us (9%)
  Pallas kernels  21.3 us (8%)
  between operations  18.1 us (7%)
  other arithmetic  4.57 us (2%)
    all_to_all x3, waiting for transfers between devices, body(): lax.all_to_all(x.reshape(experts, SLOT, x.shape[1]), E_AXES, 0, 0, tiled=...  69.6 us
    all_to_all x3, starting transfers between devices, body(): lax.all_to_all(x.reshape(experts, SLOT, x.shape[1]), E_AXES, 0, 0, tiled=...  50.6 us
    ppermute x7, starting transfers between devices, body(): lax.ppermute(over[b], PLANE, [(j, j ^ b) for j in range(plane)])  22.2 us
    pallas_call x5, Pallas kernels, call(): pl.pallas_call(kernel, out_shape=out, in_specs=[SMEM] * scalars + [VMEM]...  21.3 us
    ppermute x1, waiting for transfers between devices, gather_ring(): lax.ppermute(x, 'dp', ring(4, -1))  17.1 us
    all_to_all x1, starting transfers between devices, body(): pieces = lax.all_to_all(parcel, PLANE, 0, 0, tiled=True)  8.57 us
    reshape x3, local copies, waits for them, and re-layouts, body(): x.reshape(experts, SLOT, x.shape[1])  7.94 us
    ppermute x1, waiting for transfers between devices, gather_ring(): lax.ppermute(x, 'dp', ring(4, 1))  7.91 us
  transfers between devices with their start and end apart: 16, of which 8 were waited for; matrix products, arithmetic and copies ran while one was open for 4% of the time, Pallas kernels for 7%

profile of v3, /device:TPU:33, one launch (start us, length us, event | category | flops | bytes accessed | tf_op | source)
XLA Modules:
  0.0 265.5 jit_solution(3208692203716663740)
XLA Ops:
  10.6 4.4 %collective-permute-start = (bf16[3072,256]{1,0:T(8,128)(2,1)S(1)}, bf16[3072,256]{1,0:T(8,128)(2,1)S(1)}, u32[]{:S(2)}, u32[]{:S(2)}) collective-permute-start(bf16[3072,256]{1,0:T(8,128)(2,1)S(1)} %pad_maximum_fusion.refs_1_), channel_id=1, source_target_pairs={{0,3},{1,0},{2,1},{3,2},{4,7},{5,4},{6,5},{7,6},{8,11},{9,8},{10,9... | collective-permute-start | bytes 4718600 | tf_op jit(solution)/shard_map/ppermute | solution.py:162
  15.0 1.9 collective-permute-start.1
  18.1 1.5 shard_map.73
  20.8 4.0 %reshape.41 = bf16[128,2,2560]{2,1,0:T(2,128)(2,1)} reshape(bf16[256,2560]{1,0:T(8,128)(2,1)} %copy-done.5) | data formatting | bytes 2621440 | tf_op jit(solution)/shard_map/reshape | solution.py:205
  24.7 20.2 %all-to-all-start = ((bf16[128,2,2560]{2,1,0:T(2,128)(2,1)}), bf16[128,2,2560]{2,1,0:T(2,128)(2,1)}, u32[]{:S(2)}, u32[]{:S(2)}) async-start(bf16[128,2,2560]{2,1,0:T(2,128)(2,1)} %reshape.41), calls=%async_computation | async-start | bytes 2621440 | tf_op jit(solution)/shard_map/all_to_all | solution.py:204
  44.9 17.1 %collective-permute-done.ahead_ref.refs_2_ = bf16[3072,256]{1,0:T(8,128)(2,1)S(1)} collective-permute-done((bf16[3072,256]{1,0:T(8,128)(2,1)S(1)}, bf16[3072,256]{1,0:T(8,128)(2,1)S(1)}, u32[]{:S(2)}, u32[]{:S(2)}) %collective-permute-start) | collective-permute-done | bytes 1572896 | tf_op jit(solution)/shard_map/ppermute | solution.py:162
  62.0 7.9 %collective-permute-done.1.behind_ref.refs_5_ = bf16[3072,256]{1,0:T(8,128)(2,1)} collective-permute-done((bf16[3072,256]{1,0:T(8,128)(2,1)S(1)}, bf16[3072,256]{1,0:T(8,128)(2,1)}, u32[]{:S(2)}, u32[]{:S(2)}) %collective-permute-start.1) | collective-permute-done | bytes 1572896 | tf_op jit(solution)/shard_map/ppermute | solution.py:162
  69.9 2.6 shard_map.74
  72.5 1.9 collective-permute-start.2
  74.4 3.4 %collective-permute-start.3 = (bf16[1536,256]{1,0:T(8,128)(2,1)}, bf16[1536,256]{1,0:T(8,128)(2,1)}, u32[]{:S(2)}, u32[]{:S(2)}) collective-permute-start(bf16[1536,256]{1,0:T(8,128)(2,1)} %get-tuple-element.23), channel_id=1, source_target_pairs={{0,1},{1,2},{2,3},{3,0},{4,5},{5,6},{6,7},{7,4},{8,9},{9,10},{10,1... | collective-permute-start | bytes 2359304 | tf_op jit(solution)/shard_map/ppermute | solution.py:169
  81.0 30.0 %all-to-all-done = bf16[128,2,2560]{2,1,0:T(2,128)(2,1)} async-done(((bf16[128,2,2560]{2,1,0:T(2,128)(2,1)}), bf16[128,2,2560]{2,1,0:T(2,128)(2,1)}, u32[]{:S(2)}, u32[]{:S(2)}) %all-to-all-start) | async-done | bytes 1310752 | tf_op jit(solution)/shard_map/all_to_all | solution.py:204
  111.0 3.2 %reshape.42.rows_ref = bf16[256,2560]{1,0:T(8,128)(2,1)S(1)} reshape(bf16[128,2,2560]{2,1,0:T(2,128)(2,1)} %all-to-all-done) | data formatting | bytes 2621440 | tf_op jit(solution)/shard_map/reshape | solution.py:206
  115.4 8.6 %all-to-all-start.1 = ((bf16[8,256,256]{2,1,0:T(8,128)(2,1)}), bf16[8,256,256]{2,1,0:T(8,128)(2,1)}, u32[]{:S(2)}, u32[]{:S(2)}) async-start(bf16[8,256,256]{2,1,0:T(8,128)(2,1)} %broadcast_select_fusion), calls=%async_computation.1 | async-start | bytes 2097152 | tf_op jit(solution)/shard_map/all_to_all | solution.py:218
  125.4 7.2 %shard_map.75 = bf16[256,2048]{1,0:T(8,128)(2,1)S(1)} custom-call(s32[1]{0:T(128)} %bitcast.2.at_ref, bf16[256,2560]{1,0:T(8,128)(2,1)S(1)} %reshape.42.rows_ref, bf16[4,3072,256]{2,1,0:T(8,128)(2,1)} %bitcast.35, bf16[3072,256]{1,0:T(8,128)(2,1)S(1)} %pad_maximum_fusion.refs_1_, bf16[3072,256]{1,0:T(8,128)(2,1)S(1)} %copy-done.1, ...), custom_call_target="tpu_custom_call" | custom-call | tf_op jit(solution)/shard_map/pallas_call | solution.py:173
  133.6 5.6 %all-to-all-done.1.rows_ref = bf16[8,256,256]{2,1,0:T(8,128)(2,1)} async-done(((bf16[8,256,256]{2,1,0:T(8,128)(2,1)}), bf16[8,256,256]{2,1,0:T(8,128)(2,1)}, u32[]{:S(2)}, u32[]{:S(2)}) %all-to-all-start.1) | async-done | bytes 1048608 | tf_op jit(solution)/shard_map/all_to_all | solution.py:218
  139.2 2.1 slice.65
  141.2 3.0 %reshape.43 = bf16[128,2,1536]{2,1,0:T(2,128)(2,1)} reshape(bf16[256,1536]{1,0:T(8,128)(2,1)} %slice.65) | data formatting | bytes 1572864 | tf_op jit(solution)/shard_map/reshape | solution.py:205
  144.2 20.8 %all-to-all-start.2 = ((bf16[128,2,1536]{2,1,0:T(2,128)(2,1)}), bf16[128,2,1536]{2,1,0:T(2,128)(2,1)}, u32[]{:S(2)}, u32[]{:S(2)}) async-start(bf16[128,2,1536]{2,1,0:T(2,128)(2,1)} %reshape.43), calls=%async_computation.2 | async-start | bytes 1572864 | tf_op jit(solution)/shard_map/all_to_all | solution.py:204
  165.1 7.5 %shard_map.76 = bf16[8,256,256]{2,1,0:T(8,128)(2,1)S(1)} custom-call(s32[2]{0:T(128)S(1)} %pad_add_fusion.at_ref, bf16[8,256,256]{2,1,0:T(8,128)(2,1)} %all-to-all-done.1.rows_ref, bf16[4,3072,256]{2,1,0:T(8,128)(2,1)} %bitcast.36, bf16[3072,256]{1,0:T(8,128)(2,1)S(1)} %pad_maximum_fusion.refs_1_, bf16[3072,256]{1,0:T(8,128)(2,1)S(1)} %copy-done.2, ...), custom_call_target="tpu_custom_call" | custom-call | tf_op jit(solution)/shard_map/pallas_call | solution.py:173
  173.7 4.7 %collective-permute-start.4 = (bf16[256,256]{1,0:T(8,128)(2,1)S(1)}, bf16[256,256]{1,0:T(8,128)(2,1)S(1)}, u32[]{:S(2)}, u32[]{:S(2)}) collective-permute-start(bf16[256,256]{1,0:T(8,128)(2,1)S(1)} %get-tuple-element.43), channel_id=1, source_target_pairs={{0,28},{4,24},{8,20},{12,16},{16,12},{20,8},{24,4},{28,0},{1,29},{... | collective-permute-start | bytes 393224 | tf_op jit(solution)/shard_map/ppermute | solution.py:234
  178.4 2.2 collective-permute-start.5
  180.6 3.7 %collective-permute-start.6 = (bf16[256,256]{1,0:T(8,128)(2,1)S(1)}, bf16[256,256]{1,0:T(8,128)(2,1)S(1)}, u32[]{:S(2)}, u32[]{:S(2)}) collective-permute-start(bf16[256,256]{1,0:T(8,128)(2,1)S(1)} %get-tuple-element.41), channel_id=1, source_target_pairs={{0,20},{4,16},{8,28},{12,24},{16,4},{20,0},{24,12},{28,8},{1,21},{... | collective-permute-start | bytes 393224 | tf_op jit(solution)/shard_map/ppermute | solution.py:234
  184.3 3.4 %collective-permute-start.7 = (bf16[256,256]{1,0:T(8,128)(2,1)S(1)}, bf16[256,256]{1,0:T(8,128)(2,1)S(1)}, u32[]{:S(2)}, u32[]{:S(2)}) collective-permute-start(bf16[256,256]{1,0:T(8,128)(2,1)S(1)} %get-tuple-element.40), channel_id=1, source_target_pairs={{0,16},{4,20},{8,24},{12,28},{16,0},{20,4},{24,8},{28,12},{1,17},{... | collective-permute-start | bytes 393224 | tf_op jit(solution)/shard_map/ppermute | solution.py:234
  187.7 2.2 collective-permute-start.8
  189.9 3.3 %collective-permute-start.9 = (bf16[256,256]{1,0:T(8,128)(2,1)S(1)}, bf16[256,256]{1,0:T(8,128)(2,1)S(1)}, u32[]{:S(2)}, u32[]{:S(2)}) collective-permute-start(bf16[256,256]{1,0:T(8,128)(2,1)S(1)} %get-tuple-element.38), channel_id=1, source_target_pairs={{0,8},{4,12},{8,0},{12,4},{16,24},{20,28},{24,16},{28,20},{1,9},{5... | collective-permute-start | bytes 393224 | tf_op jit(solution)/shard_map/ppermute | solution.py:234
  193.3 2.2 collective-permute-done.5
  195.4 2.7 %collective-permute-start.10 = (bf16[256,256]{1,0:T(8,128)(2,1)S(1)}, bf16[256,256]{1,0:T(8,128)(2,1)S(1)}, u32[]{:S(2)}, u32[]{:S(2)}) collective-permute-start(bf16[256,256]{1,0:T(8,128)(2,1)S(1)} %get-tuple-element.37), channel_id=1, source_target_pairs={{0,4},{4,0},{8,12},{12,8},{16,20},{20,16},{24,28},{28,24},{1,5},{5... | collective-permute-start | bytes 393224 | tf_op jit(solution)/shard_map/ppermute | solution.py:234
  203.2 6.1 %all-to-all-done.2 = bf16[128,2,1536]{2,1,0:T(2,128)(2,1)} async-done(((bf16[128,2,1536]{2,1,0:T(2,128)(2,1)}), bf16[128,2,1536]{2,1,0:T(2,128)(2,1)}, u32[]{:S(2)}, u32[]{:S(2)}) %all-to-all-start.2) | async-done | bytes 786464 | tf_op jit(solution)/shard_map/all_to_all | solution.py:204
  209.3 2.3 reshape.44.refs_1_
  212.6 9.7 %all-to-all-start.3 = ((bf16[128,2,1024]{2,1,0:T(2,128)(2,1)}), bf16[128,2,1024]{2,1,0:T(2,128)(2,1)S(1)}, u32[]{:S(2)}, u32[]{:S(2)}) async-start(bf16[128,2,1024]{2,1,0:T(2,128)(2,1)} %reshape.45), calls=%async_computation.3 | async-start | bytes 1048576 | tf_op jit(solution)/shard_map/all_to_all | solution.py:204
  222.4 33.5 %all-to-all-done.3 = bf16[128,2,1024]{2,1,0:T(2,128)(2,1)S(1)} async-done(((bf16[128,2,1024]{2,1,0:T(2,128)(2,1)}), bf16[128,2,1024]{2,1,0:T(2,128)(2,1)S(1)}, u32[]{:S(2)}, u32[]{:S(2)}) %all-to-all-start.3) | async-done | bytes 524320 | tf_op jit(solution)/shard_map/all_to_all | solution.py:204
  256.1 2.6 shard_map.77
  (53 shorter events, 16.3 us)
Async XLA Ops:
  6.5 1.5 copy-start.8
  6.5 117.4 %all-gather.3.cloned.1.call-start = ((), (), s32[]{:S(2)}) async-start(), calls=%async_computation.4 | async-start | bytes 7864320 | tf_op jit(solution)/shard_map/all_gather | solution.py:195
  9.3 1.2 copy-start.9
  10.5 6.4 %copy-start.10 = (s32[128,2]{0,1:T(2,128)S(1)}, s32[128,2]{0,1:T(2,128)}, u32[]{:S(2)}) copy-start(s32[128,2]{0,1:T(2,128)} %param.9) | copy-start | bytes 3076
  10.5 6.6 %copy-start.7 = (f32[2048]{0:T(1024)S(1)}, f32[2048]{0:T(1024)}, u32[]{:S(2)}) copy-start(f32[2048]{0:T(1024)} %param.8) | copy-start | bytes 24580
  10.6 51.3 %collective-permute-start = (bf16[3072,256]{1,0:T(8,128)(2,1)S(1)}, bf16[3072,256]{1,0:T(8,128)(2,1)S(1)}, u32[]{:S(2)}, u32[]{:S(2)}) collective-permute-start(bf16[3072,256]{1,0:T(8,128)(2,1)S(1)} %pad_maximum_fusion.refs_1_), channel_id=1, source_target_pairs={{0,3},{1,0},{2,1},{3,2},{4,7},{5,4},{6,5},{7,6},{8,11},{9,8},{10,9... | collective-permute-start | bytes 4718600 | tf_op jit(solution)/shard_map/ppermute | solution.py:162
  15.0 54.8 %collective-permute-start.1 = (bf16[3072,256]{1,0:T(8,128)(2,1)S(1)}, bf16[3072,256]{1,0:T(8,128)(2,1)}, u32[]{:S(2)}, u32[]{:S(2)}) collective-permute-start(bf16[3072,256]{1,0:T(8,128)(2,1)S(1)} %pad_maximum_fusion.refs_1_), channel_id=1, source_target_pairs={{0,1},{1,2},{2,3},{3,0},{4,5},{5,6},{6,7},{7,4},{8,9},{9,10},{10,1... | collective-permute-start | bytes 4718600 | tf_op jit(solution)/shard_map/ppermute | solution.py:162
  17.1 1.0 copy-start.6
  19.6 1.2 copy-start.5
  24.7 86.2 %all-to-all-start = ((bf16[128,2,2560]{2,1,0:T(2,128)(2,1)}), bf16[128,2,2560]{2,1,0:T(2,128)(2,1)}, u32[]{:S(2)}, u32[]{:S(2)}) async-start(bf16[128,2,2560]{2,1,0:T(2,128)(2,1)} %reshape.41), calls=%async_computation | async-start | bytes 2621440 | tf_op jit(solution)/shard_map/all_to_all | solution.py:204
  62.0 10.5 %copy-start = (bf16[3072,256]{1,0:T(8,128)(2,1)}, bf16[3072,256]{1,0:T(8,128)(2,1)S(1)}, u32[]{:S(2)}) copy-start(bf16[3072,256]{1,0:T(8,128)(2,1)S(1)} %collective-permute-done.ahead_ref.refs_2_) | copy-start | bytes 4718596
  72.5 41.7 %collective-permute-start.2 = (bf16[1536,256]{1,0:T(8,128)(2,1)}, bf16[1536,256]{1,0:T(8,128)(2,1)}, u32[]{:S(2)}, u32[]{:S(2)}) collective-permute-start(bf16[1536,256]{1,0:T(8,128)(2,1)} %get-tuple-element.22), channel_id=1, source_target_pairs={{0,3},{1,0},{2,1},{3,2},{4,7},{5,4},{6,5},{7,6},{8,11},{9,8},{10,9... | collective-permute-start | bytes 2359304 | tf_op jit(solution)/shard_map/ppermute | solution.py:169
  74.4 39.8 %collective-permute-start.3 = (bf16[1536,256]{1,0:T(8,128)(2,1)}, bf16[1536,256]{1,0:T(8,128)(2,1)}, u32[]{:S(2)}, u32[]{:S(2)}) collective-permute-start(bf16[1536,256]{1,0:T(8,128)(2,1)} %get-tuple-element.23), channel_id=1, source_target_pairs={{0,1},{1,2},{2,3},{3,0},{4,5},{5,6},{6,7},{7,4},{8,9},{9,10},{10,1... | collective-permute-start | bytes 2359304 | tf_op jit(solution)/shard_map/ppermute | solution.py:169
  115.4 23.8 %all-to-all-start.1 = ((bf16[8,256,256]{2,1,0:T(8,128)(2,1)}), bf16[8,256,256]{2,1,0:T(8,128)(2,1)}, u32[]{:S(2)}, u32[]{:S(2)}) async-start(bf16[8,256,256]{2,1,0:T(8,128)(2,1)} %broadcast_select_fusion), calls=%async_computation.1 | async-start | bytes 2097152 | tf_op jit(solution)/shard_map/all_to_all | solution.py:218
  124.0 1.4 copy-start.1
  132.6 1.0 copy-start.4
  141.2 23.9 %copy-start.2 = (bf16[3072,256]{1,0:T(8,128)(2,1)S(1)}, bf16[3072,256]{1,0:T(8,128)(2,1)}, u32[]{:S(2)}) copy-start(bf16[3072,256]{1,0:T(8,128)(2,1)} %copy-done) | copy-start | bytes 4718596
  144.2 65.1 %all-to-all-start.2 = ((bf16[128,2,1536]{2,1,0:T(2,128)(2,1)}), bf16[128,2,1536]{2,1,0:T(2,128)(2,1)}, u32[]{:S(2)}, u32[]{:S(2)}) async-start(bf16[128,2,1536]{2,1,0:T(2,128)(2,1)} %reshape.43), calls=%async_computation.2 | async-start | bytes 1572864 | tf_op jit(solution)/shard_map/all_to_all | solution.py:204
  172.6 1.0 copy-start.3
  173.7 29.4 %slice-start = ((bf16[256,2048]{1,0:T(8,128)(2,1)}), bf16[256,512]{1,0:T(8,128)(2,1)S(1)}, s32[]{:S(2)}) async-start(bf16[256,2048]{1,0:T(8,128)(2,1)} %copy-done.4), calls=%async_computation.5 | async-start | bytes 524288 | tf_op jit(solution)/shard_map/slice | solution.py:245
  173.7 16.2 %collective-permute-start.4 = (bf16[256,256]{1,0:T(8,128)(2,1)S(1)}, bf16[256,256]{1,0:T(8,128)(2,1)S(1)}, u32[]{:S(2)}, u32[]{:S(2)}) collective-permute-start(bf16[256,256]{1,0:T(8,128)(2,1)S(1)} %get-tuple-element.43), channel_id=1, source_target_pairs={{0,28},{4,24},{8,20},{12,16},{16,12},{20,8},{24,4},{28,0},{1,29},{... | collective-permute-start | bytes 393224 | tf_op jit(solution)/shard_map/ppermute | solution.py:234
  178.4 17.1 %collective-permute-start.5 = (bf16[256,256]{1,0:T(8,128)(2,1)S(1)}, bf16[256,256]{1,0:T(8,128)(2,1)S(1)}, u32[]{:S(2)}, u32[]{:S(2)}) collective-permute-start(bf16[256,256]{1,0:T(8,128)(2,1)S(1)} %get-tuple-element.42), channel_id=1, source_target_pairs={{0,24},{4,28},{8,16},{12,20},{16,8},{20,12},{24,0},{28,4},{1,25},{... | collective-permute-start | bytes 393224 | tf_op jit(solution)/shard_map/ppermute | solution.py:234
  180.6 19.3 %collective-permute-start.6 = (bf16[256,256]{1,0:T(8,128)(2,1)S(1)}, bf16[256,256]{1,0:T(8,128)(2,1)S(1)}, u32[]{:S(2)}, u32[]{:S(2)}) collective-permute-start(bf16[256,256]{1,0:T(8,128)(2,1)S(1)} %get-tuple-element.41), channel_id=1, source_target_pairs={{0,20},{4,16},{8,28},{12,24},{16,4},{20,0},{24,12},{28,8},{1,21},{... | collective-permute-start | bytes 393224 | tf_op jit(solution)/shard_map/ppermute | solution.py:234
  184.3 15.6 %collective-permute-start.7 = (bf16[256,256]{1,0:T(8,128)(2,1)S(1)}, bf16[256,256]{1,0:T(8,128)(2,1)S(1)}, u32[]{:S(2)}, u32[]{:S(2)}) collective-permute-start(bf16[256,256]{1,0:T(8,128)(2,1)S(1)} %get-tuple-element.40), channel_id=1, source_target_pairs={{0,16},{4,20},{8,24},{12,28},{16,0},{20,4},{24,8},{28,12},{1,17},{... | collective-permute-start | bytes 393224 | tf_op jit(solution)/shard_map/ppermute | solution.py:234
  187.7 12.2 %collective-permute-start.8 = (bf16[256,256]{1,0:T(8,128)(2,1)S(1)}, bf16[256,256]{1,0:T(8,128)(2,1)S(1)}, u32[]{:S(2)}, u32[]{:S(2)}) collective-permute-start(bf16[256,256]{1,0:T(8,128)(2,1)S(1)} %get-tuple-element.39), channel_id=1, source_target_pairs={{0,12},{4,8},{8,4},{12,0},{16,28},{20,24},{24,20},{28,16},{1,13},{... | collective-permute-start | bytes 393224 | tf_op jit(solution)/shard_map/ppermute | solution.py:234
  189.9 11.2 %collective-permute-start.9 = (bf16[256,256]{1,0:T(8,128)(2,1)S(1)}, bf16[256,256]{1,0:T(8,128)(2,1)S(1)}, u32[]{:S(2)}, u32[]{:S(2)}) collective-permute-start(bf16[256,256]{1,0:T(8,128)(2,1)S(1)} %get-tuple-element.38), channel_id=1, source_target_pairs={{0,8},{4,12},{8,0},{12,4},{16,24},{20,28},{24,16},{28,20},{1,9},{5... | collective-permute-start | bytes 393224 | tf_op jit(solution)/shard_map/ppermute | solution.py:234
  195.4 5.7 %collective-permute-start.10 = (bf16[256,256]{1,0:T(8,128)(2,1)S(1)}, bf16[256,256]{1,0:T(8,128)(2,1)S(1)}, u32[]{:S(2)}, u32[]{:S(2)}) collective-permute-start(bf16[256,256]{1,0:T(8,128)(2,1)S(1)} %get-tuple-element.37), channel_id=1, source_target_pairs={{0,4},{4,0},{8,12},{12,8},{16,20},{20,16},{24,28},{28,24},{1,5},{5... | collective-permute-start | bytes 393224 | tf_op jit(solution)/shard_map/ppermute | solution.py:234
  203.2 19.1 %copy-start.11 = (f32[128,2]{0,1:T(2,128)S(1)}, f32[128,2]{0,1:T(2,128)}, u32[]{:S(2)}) copy-start(f32[128,2]{0,1:T(2,128)} %param.10) | copy-start | bytes 3076
  212.6 43.3 %all-to-all-start.3 = ((bf16[128,2,1024]{2,1,0:T(2,128)(2,1)}), bf16[128,2,1024]{2,1,0:T(2,128)(2,1)S(1)}, u32[]{:S(2)}, u32[]{:S(2)}) async-start(bf16[128,2,1024]{2,1,0:T(2,128)(2,1)} %reshape.45), calls=%async_computation.3 | async-start | bytes 1048576 | tf_op jit(solution)/shard_map/all_to_all | solution.py:204
Sparse Core Ops, SparseCore 0:
  9.5 112.7 all-gather.2

commit v4 on v3

--- a/solution.py
+++ b/solution.py
@@ -64,7 +64,7 @@
 
 def last_kernel(plane, hot_ref, res_ref, more_ref, tgt_ref, gs_ref, out_ref):
     toks, width = out_ref.shape
-    slots, piece, near = res_ref.shape[0], width // plane, res_ref.shape[1]
+    slots, piece = res_ref.shape[0], width // plane
     weights = gs_ref[...] / jnp.sum(gs_ref[...], axis=1, keepdims=True)
 
     def mix(wanted, alive=True):
@@ -75,17 +75,13 @@
 
     usual = mix(iota((toks, slots), 1))
     spot = iota((toks, plane * SLOT), 1)
-    base = width - near
     over = []
     for h in range(2):
         start = pl.multiple_of(hot_ref[h] // plane * (plane * SLOT), plane * SLOT)
-        over.append(more_ref[pl.ds(start, plane * SLOT), base + h * piece : base + (h + 1) * piece])
+        over.append(more_ref[pl.ds(start, plane * SLOT), h * piece : (h + 1) * piece])
     for j in range(plane):
         start = j * piece
-        rows = res_ref[:, start : start + piece] if start < near else (
-            more_ref[:, start - near : start - near + piece]
-        )
-        total = sum(matmul(p, rows) for p in usual)
+        total = sum(matmul(p, res_ref[:, start : start + piece]) for p in usual)
         for h in range(2):
             parts = mix(slots + h * SLOT + spot % SLOT, spot // SLOT == j)
             total += sum(matmul(p, over[h]) for p in parts)
@@ -218,10 +214,8 @@
     pieces = lax.all_to_all(parcel, PLANE, 0, 0, tiled=True)
     hid = pltpu.VMEM((slots, units), bf16)
     done = call(main_kernel, shape((slots, width), bf16), at, got, gate, *packed, scalars=1, scratch=[hid])
-    near = width - 2 * piece
-    tie = lax.optimization_barrier((done, pieces))
-    done, pieces = tie
-    res = trade(done[:, :near])
+    done, pieces = lax.optimization_barrier((done, pieces))
+    res = trade(done)
     spot = lax.axis_index("y") * mesh.shape["c"] + lax.axis_index("c")
     over = call(
         extra_kernel,
@@ -241,9 +235,7 @@
             value = jnp.where(gap == b, over[b], value)
         return value
 
-    more, res = lax.optimization_barrier(
-        (jnp.concatenate([done[:, near:], take(low), take(high)], 1), res)
-    )
+    more, res = lax.optimization_barrier((jnp.concatenate([take(low), take(high)], 1), res))
     more = trade(more)
     return call(
         lambda *refs: last_kernel(plane, *refs),

time: 267 us -> 260 us (0.974)
  local copies, waits for them, and re-layouts: 24.9 us -> 21.2 us
  starting transfers between devices: 92.9 us -> 89.7 us
    all_to_all x3, starting transfers between devices: 50.6 us -> 47.4 us  [body(): lax.all_to_all(x.reshape(experts, SLOT, x.shape[1]), E_AXES, 0, 0, tiled=...]
where the time goes in v4:
time: 260 us; the launch traced here: 259 us
  waiting for transfers between devices  103 us (40%)
  starting transfers between devices  89.7 us (34%)
  Pallas kernels  21.4 us (8%)
  local copies, waits for them, and re-layouts  21.2 us (8%)
  between operations  18.4 us (7%)
  other arithmetic  4.58 us (2%)
    all_to_all x3, waiting for transfers between devices, body(): lax.all_to_all(x.reshape(experts, SLOT, x.shape[1]), E_AXES, 0, 0, tiled=...  69.2 us
    all_to_all x3, starting transfers between devices, body(): lax.all_to_all(x.reshape(experts, SLOT, x.shape[1]), E_AXES, 0, 0, tiled=...  47.4 us
    ppermute x7, starting transfers between devices, body(): lax.ppermute(over[b], PLANE, [(j, j ^ b) for j in range(plane)])  22.1 us
    pallas_call x5, Pallas kernels, call(): pl.pallas_call(kernel, out_shape=out, in_specs=[SMEM] * scalars + [VMEM]...  21.4 us
    ppermute x1, waiting for transfers between devices, gather_ring(): lax.ppermute(x, 'dp', ring(4, -1))  17.2 us
    all_to_all x1, starting transfers between devices, body(): pieces = lax.all_to_all(parcel, PLANE, 0, 0, tiled=True)  8.68 us
    ppermute x1, waiting for transfers between devices, gather_ring(): lax.ppermute(x, 'dp', ring(4, 1))  7.91 us
    reshape x3, local copies, waits for them, and re-layouts, body(): x.reshape(experts, SLOT, x.shape[1])  7.34 us
  transfers between devices with their start and end apart: 16, of which 8 were waited for; matrix products, arithmetic and copies ran while one was open for 4% of the time, Pallas kernels for 7%

profile of v4, /device:TPU:33, one launch (start us, length us, event | category | flops | bytes accessed | tf_op | source)
XLA Modules:
  0.0 258.7 jit_solution(1286523480082532826)
XLA Ops:
  10.7 4.4 %collective-permute-start = (bf16[3072,256]{1,0:T(8,128)(2,1)S(1)}, bf16[3072,256]{1,0:T(8,128)(2,1)S(1)}, u32[]{:S(2)}, u32[]{:S(2)}) collective-permute-start(bf16[3072,256]{1,0:T(8,128)(2,1)S(1)} %pad_maximum_fusion.refs_1_), channel_id=1, source_target_pairs={{0,3},{1,0},{2,1},{3,2},{4,7},{5,4},{6,5},{7,6},{8,11},{9,8},{10,9... | collective-permute-start | bytes 4718600 | tf_op jit(solution)/shard_map/ppermute | solution.py:158
  15.1 1.9 collective-permute-start.1
  18.2 1.5 shard_map.73
  20.7 4.0 %reshape.38 = bf16[128,2,2560]{2,1,0:T(2,128)(2,1)} reshape(bf16[256,2560]{1,0:T(8,128)(2,1)} %copy-done.5) | data formatting | bytes 2621440 | tf_op jit(solution)/shard_map/reshape | solution.py:201
  24.7 20.2 %all-to-all-start = ((bf16[128,2,2560]{2,1,0:T(2,128)(2,1)}), bf16[128,2,2560]{2,1,0:T(2,128)(2,1)}, u32[]{:S(2)}, u32[]{:S(2)}) async-start(bf16[128,2,2560]{2,1,0:T(2,128)(2,1)} %reshape.38), calls=%async_computation | async-start | bytes 2621440 | tf_op jit(solution)/shard_map/all_to_all | solution.py:200
  44.9 17.2 %collective-permute-done.ahead_ref.refs_2_ = bf16[3072,256]{1,0:T(8,128)(2,1)S(1)} collective-permute-done((bf16[3072,256]{1,0:T(8,128)(2,1)S(1)}, bf16[3072,256]{1,0:T(8,128)(2,1)S(1)}, u32[]{:S(2)}, u32[]{:S(2)}) %collective-permute-start) | collective-permute-done | bytes 1572896 | tf_op jit(solution)/shard_map/ppermute | solution.py:158
  62.0 7.9 %collective-permute-done.1.behind_ref.refs_5_ = bf16[3072,256]{1,0:T(8,128)(2,1)} collective-permute-done((bf16[3072,256]{1,0:T(8,128)(2,1)S(1)}, bf16[3072,256]{1,0:T(8,128)(2,1)}, u32[]{:S(2)}, u32[]{:S(2)}) %collective-permute-start.1) | collective-permute-done | bytes 1572896 | tf_op jit(solution)/shard_map/ppermute | solution.py:158
  69.9 2.6 %shard_map.74 = (bf16[1536,256]{1,0:T(8,128)(2,1)}, bf16[1536,256]{1,0:T(8,128)(2,1)}) custom-call(bf16[3072,256]{1,0:T(8,128)(2,1)S(1)} %collective-permute-done.ahead_ref.refs_2_, bf16[3072,256]{1,0:T(8,128)(2,1)} %collective-permute-done.1.behind_ref.refs_5_), custom_call_target="tpu_custom_call" | custom-call | flops 40000000000 | tf_op jit(solution)/shard_map/pallas_call | solution.py:169
  72.6 1.9 collective-permute-start.2
  74.5 3.4 %collective-permute-start.3 = (bf16[1536,256]{1,0:T(8,128)(2,1)}, bf16[1536,256]{1,0:T(8,128)(2,1)}, u32[]{:S(2)}, u32[]{:S(2)}) collective-permute-start(bf16[1536,256]{1,0:T(8,128)(2,1)} %get-tuple-element.23), channel_id=1, source_target_pairs={{0,1},{1,2},{2,3},{3,0},{4,5},{5,6},{6,7},{7,4},{8,9},{9,10},{10,1... | collective-permute-start | bytes 2359304 | tf_op jit(solution)/shard_map/ppermute | solution.py:165
  81.1 29.8 %all-to-all-done = bf16[128,2,2560]{2,1,0:T(2,128)(2,1)} async-done(((bf16[128,2,2560]{2,1,0:T(2,128)(2,1)}), bf16[128,2,2560]{2,1,0:T(2,128)(2,1)}, u32[]{:S(2)}, u32[]{:S(2)}) %all-to-all-start) | async-done | bytes 1310752 | tf_op jit(solution)/shard_map/all_to_all | solution.py:200
  110.9 3.2 %reshape.39.rows_ref = bf16[256,2560]{1,0:T(8,128)(2,1)S(1)} reshape(bf16[128,2,2560]{2,1,0:T(2,128)(2,1)} %all-to-all-done) | data formatting | bytes 2621440 | tf_op jit(solution)/shard_map/reshape | solution.py:202
  115.3 8.7 %all-to-all-start.1 = ((bf16[8,256,256]{2,1,0:T(8,128)(2,1)}), bf16[8,256,256]{2,1,0:T(8,128)(2,1)}, u32[]{:S(2)}, u32[]{:S(2)}) async-start(bf16[8,256,256]{2,1,0:T(8,128)(2,1)} %broadcast_select_fusion), calls=%async_computation.1 | async-start | bytes 2097152 | tf_op jit(solution)/shard_map/all_to_all | solution.py:214
  125.4 7.2 %shard_map.75 = bf16[256,2048]{1,0:T(8,128)(2,1)S(1)} custom-call(s32[1]{0:T(128)} %bitcast.3.at_ref, bf16[256,2560]{1,0:T(8,128)(2,1)S(1)} %reshape.39.rows_ref, bf16[4,3072,256]{2,1,0:T(8,128)(2,1)} %bitcast.35, bf16[3072,256]{1,0:T(8,128)(2,1)S(1)} %pad_maximum_fusion.refs_1_, bf16[3072,256]{1,0:T(8,128)(2,1)S(1)} %copy-done.1, ...), custom_call_target="tpu_custom_call" | custom-call | tf_op jit(solution)/shard_map/pallas_call | solution.py:169
  133.6 5.6 %all-to-all-done.1.rows_ref = bf16[8,256,256]{2,1,0:T(8,128)(2,1)} async-done(((bf16[8,256,256]{2,1,0:T(8,128)(2,1)}), bf16[8,256,256]{2,1,0:T(8,128)(2,1)}, u32[]{:S(2)}, u32[]{:S(2)}) %all-to-all-start.1) | async-done | bytes 1048608 | tf_op jit(solution)/shard_map/all_to_all | solution.py:214
  139.2 2.6 reshape.40
  141.8 20.8 %all-to-all-start.2 = ((bf16[128,2,2048]{2,1,0:T(2,128)(2,1)}), bf16[128,2,2048]{2,1,0:T(2,128)(2,1)}, u32[]{:S(2)}, u32[]{:S(2)}) async-start(bf16[128,2,2048]{2,1,0:T(2,128)(2,1)} %reshape.40), calls=%async_computation.2 | async-start | bytes 2097152 | tf_op jit(solution)/shard_map/all_to_all | solution.py:200
  162.7 7.5 %shard_map.76 = bf16[8,256,256]{2,1,0:T(8,128)(2,1)S(1)} custom-call(s32[2]{0:T(128)S(1)} %pad_add_fusion.at_ref, bf16[8,256,256]{2,1,0:T(8,128)(2,1)} %all-to-all-done.1.rows_ref, bf16[4,3072,256]{2,1,0:T(8,128)(2,1)} %bitcast.36, bf16[3072,256]{1,0:T(8,128)(2,1)S(1)} %pad_maximum_fusion.refs_1_, bf16[3072,256]{1,0:T(8,128)(2,1)S(1)} %copy-done.2, ...), custom_call_target="tpu_custom_call" | custom-call | tf_op jit(solution)/shard_map/pallas_call | solution.py:169
  171.2 4.6 %collective-permute-start.4 = (bf16[256,256]{1,0:T(8,128)(2,1)S(1)}, bf16[256,256]{1,0:T(8,128)(2,1)S(1)}, u32[]{:S(2)}, u32[]{:S(2)}) collective-permute-start(bf16[256,256]{1,0:T(8,128)(2,1)S(1)} %get-tuple-element.43), channel_id=1, source_target_pairs={{0,28},{4,24},{8,20},{12,16},{16,12},{20,8},{24,4},{28,0},{1,29},{... | collective-permute-start | bytes 393224 | tf_op jit(solution)/shard_map/ppermute | solution.py:228
  175.8 2.2 collective-permute-start.5
  178.0 3.7 %collective-permute-start.6 = (bf16[256,256]{1,0:T(8,128)(2,1)S(1)}, bf16[256,256]{1,0:T(8,128)(2,1)S(1)}, u32[]{:S(2)}, u32[]{:S(2)}) collective-permute-start(bf16[256,256]{1,0:T(8,128)(2,1)S(1)} %get-tuple-element.41), channel_id=1, source_target_pairs={{0,20},{4,16},{8,28},{12,24},{16,4},{20,0},{24,12},{28,8},{1,21},{... | collective-permute-start | bytes 393224 | tf_op jit(solution)/shard_map/ppermute | solution.py:228
  181.7 3.4 %collective-permute-start.7 = (bf16[256,256]{1,0:T(8,128)(2,1)S(1)}, bf16[256,256]{1,0:T(8,128)(2,1)S(1)}, u32[]{:S(2)}, u32[]{:S(2)}) collective-permute-start(bf16[256,256]{1,0:T(8,128)(2,1)S(1)} %get-tuple-element.40), channel_id=1, source_target_pairs={{0,16},{4,20},{8,24},{12,28},{16,0},{20,4},{24,8},{28,12},{1,17},{... | collective-permute-start | bytes 393224 | tf_op jit(solution)/shard_map/ppermute | solution.py:228
  185.1 2.2 collective-permute-start.8
  187.4 3.3 %collective-permute-start.9 = (bf16[256,256]{1,0:T(8,128)(2,1)S(1)}, bf16[256,256]{1,0:T(8,128)(2,1)S(1)}, u32[]{:S(2)}, u32[]{:S(2)}) collective-permute-start(bf16[256,256]{1,0:T(8,128)(2,1)S(1)} %get-tuple-element.38), channel_id=1, source_target_pairs={{0,8},{4,12},{8,0},{12,4},{16,24},{20,28},{24,16},{28,20},{1,9},{5... | collective-permute-start | bytes 393224 | tf_op jit(solution)/shard_map/ppermute | solution.py:228
  190.7 1.8 collective-permute-done.5
  192.5 2.7 %collective-permute-start.10 = (bf16[256,256]{1,0:T(8,128)(2,1)S(1)}, bf16[256,256]{1,0:T(8,128)(2,1)S(1)}, u32[]{:S(2)}, u32[]{:S(2)}) collective-permute-start(bf16[256,256]{1,0:T(8,128)(2,1)S(1)} %get-tuple-element.37), channel_id=1, source_target_pairs={{0,4},{4,0},{8,12},{12,8},{16,20},{20,16},{24,28},{28,24},{1,5},{5... | collective-permute-start | bytes 393224 | tf_op jit(solution)/shard_map/ppermute | solution.py:228
  197.3 1.7 collective-permute-done.9
  200.9 16.9 %all-to-all-done.2 = bf16[128,2,2048]{2,1,0:T(2,128)(2,1)} async-done(((bf16[128,2,2048]{2,1,0:T(2,128)(2,1)}), bf16[128,2,2048]{2,1,0:T(2,128)(2,1)}, u32[]{:S(2)}, u32[]{:S(2)}) %all-to-all-start.2) | async-done | bytes 1048608 | tf_op jit(solution)/shard_map/all_to_all | solution.py:200
  217.9 1.5 reshape.41.refs_1_
  220.1 6.4 %all-to-all-start.3 = ((bf16[128,2,512]{2,1,0:T(2,128)(2,1)}), bf16[128,2,512]{2,1,0:T(2,128)(2,1)S(1)}, u32[]{:S(2)}, u32[]{:S(2)}) async-start(bf16[128,2,512]{2,1,0:T(2,128)(2,1)} %reshape.42), calls=%async_computation.3 | async-start | bytes 524288 | tf_op jit(solution)/shard_map/all_to_all | solution.py:200
  226.7 22.4 %all-to-all-done.3 = bf16[128,2,512]{2,1,0:T(2,128)(2,1)S(1)} async-done(((bf16[128,2,512]{2,1,0:T(2,128)(2,1)}), bf16[128,2,512]{2,1,0:T(2,128)(2,1)S(1)}, u32[]{:S(2)}, u32[]{:S(2)}) %all-to-all-start.3) | async-done | bytes 262176 | tf_op jit(solution)/shard_map/all_to_all | solution.py:200
  249.3 2.6 shard_map.77
  (50 shorter events, 14.7 us)
Async XLA Ops:
  6.5 1.5 copy-start.8
  6.5 117.5 %all-gather.3.cloned.1.call-start = ((), (), s32[]{:S(2)}) async-start(), calls=%async_computation.4 | async-start | bytes 7864320 | tf_op jit(solution)/shard_map/all_gather | solution.py:191
  9.4 1.2 copy-start.9
  10.6 6.4 %copy-start.10 = (s32[128,2]{0,1:T(2,128)S(1)}, s32[128,2]{0,1:T(2,128)}, u32[]{:S(2)}) copy-start(s32[128,2]{0,1:T(2,128)} %param.9) | copy-start | bytes 3076
  10.6 6.6 %copy-start.7 = (f32[2048]{0:T(1024)S(1)}, f32[2048]{0:T(1024)}, u32[]{:S(2)}) copy-start(f32[2048]{0:T(1024)} %param.8) | copy-start | bytes 24580
  10.7 51.3 %collective-permute-start = (bf16[3072,256]{1,0:T(8,128)(2,1)S(1)}, bf16[3072,256]{1,0:T(8,128)(2,1)S(1)}, u32[]{:S(2)}, u32[]{:S(2)}) collective-permute-start(bf16[3072,256]{1,0:T(8,128)(2,1)S(1)} %pad_maximum_fusion.refs_1_), channel_id=1, source_target_pairs={{0,3},{1,0},{2,1},{3,2},{4,7},{5,4},{6,5},{7,6},{8,11},{9,8},{10,9... | collective-permute-start | bytes 4718600 | tf_op jit(solution)/shard_map/ppermute | solution.py:158
  15.1 54.8 %collective-permute-start.1 = (bf16[3072,256]{1,0:T(8,128)(2,1)S(1)}, bf16[3072,256]{1,0:T(8,128)(2,1)}, u32[]{:S(2)}, u32[]{:S(2)}) collective-permute-start(bf16[3072,256]{1,0:T(8,128)(2,1)S(1)} %pad_maximum_fusion.refs_1_), channel_id=1, source_target_pairs={{0,1},{1,2},{2,3},{3,0},{4,5},{5,6},{6,7},{7,4},{8,9},{9,10},{10,1... | collective-permute-start | bytes 4718600 | tf_op jit(solution)/shard_map/ppermute | solution.py:158
  17.2 1.0 copy-start.6
  19.7 1.1 copy-start.5
  24.7 86.2 %all-to-all-start = ((bf16[128,2,2560]{2,1,0:T(2,128)(2,1)}), bf16[128,2,2560]{2,1,0:T(2,128)(2,1)}, u32[]{:S(2)}, u32[]{:S(2)}) async-start(bf16[128,2,2560]{2,1,0:T(2,128)(2,1)} %reshape.38), calls=%async_computation | async-start | bytes 2621440 | tf_op jit(solution)/shard_map/all_to_all | solution.py:200
  62.0 10.5 %copy-start = (bf16[3072,256]{1,0:T(8,128)(2,1)}, bf16[3072,256]{1,0:T(8,128)(2,1)S(1)}, u32[]{:S(2)}) copy-start(bf16[3072,256]{1,0:T(8,128)(2,1)S(1)} %collective-permute-done.ahead_ref.refs_2_) | copy-start | bytes 4718596
  72.6 41.6 %collective-permute-start.2 = (bf16[1536,256]{1,0:T(8,128)(2,1)}, bf16[1536,256]{1,0:T(8,128)(2,1)}, u32[]{:S(2)}, u32[]{:S(2)}) collective-permute-start(bf16[1536,256]{1,0:T(8,128)(2,1)} %get-tuple-element.22), channel_id=1, source_target_pairs={{0,3},{1,0},{2,1},{3,2},{4,7},{5,4},{6,5},{7,6},{8,11},{9,8},{10,9... | collective-permute-start | bytes 2359304 | tf_op jit(solution)/shard_map/ppermute | solution.py:165
  74.5 39.7 %collective-permute-start.3 = (bf16[1536,256]{1,0:T(8,128)(2,1)}, bf16[1536,256]{1,0:T(8,128)(2,1)}, u32[]{:S(2)}, u32[]{:S(2)}) collective-permute-start(bf16[1536,256]{1,0:T(8,128)(2,1)} %get-tuple-element.23), channel_id=1, source_target_pairs={{0,1},{1,2},{2,3},{3,0},{4,5},{5,6},{6,7},{7,4},{8,9},{9,10},{10,1... | collective-permute-start | bytes 2359304 | tf_op jit(solution)/shard_map/ppermute | solution.py:165
  115.3 23.9 %all-to-all-start.1 = ((bf16[8,256,256]{2,1,0:T(8,128)(2,1)}), bf16[8,256,256]{2,1,0:T(8,128)(2,1)}, u32[]{:S(2)}, u32[]{:S(2)}) async-start(bf16[8,256,256]{2,1,0:T(8,128)(2,1)} %broadcast_select_fusion), calls=%async_computation.1 | async-start | bytes 2097152 | tf_op jit(solution)/shard_map/all_to_all | solution.py:214
  124.0 1.4 copy-start.1
  132.6 1.0 copy-start.4
  141.8 20.9 %copy-start.2 = (bf16[3072,256]{1,0:T(8,128)(2,1)S(1)}, bf16[3072,256]{1,0:T(8,128)(2,1)}, u32[]{:S(2)}) copy-start(bf16[3072,256]{1,0:T(8,128)(2,1)} %copy-done) | copy-start | bytes 4718596
  141.8 76.1 %all-to-all-start.2 = ((bf16[128,2,2048]{2,1,0:T(2,128)(2,1)}), bf16[128,2,2048]{2,1,0:T(2,128)(2,1)}, u32[]{:S(2)}, u32[]{:S(2)}) async-start(bf16[128,2,2048]{2,1,0:T(2,128)(2,1)} %reshape.40), calls=%async_computation.2 | async-start | bytes 2097152 | tf_op jit(solution)/shard_map/all_to_all | solution.py:200
  170.2 1.0 copy-start.3
  171.2 16.1 %collective-permute-start.4 = (bf16[256,256]{1,0:T(8,128)(2,1)S(1)}, bf16[256,256]{1,0:T(8,128)(2,1)S(1)}, u32[]{:S(2)}, u32[]{:S(2)}) collective-permute-start(bf16[256,256]{1,0:T(8,128)(2,1)S(1)} %get-tuple-element.43), channel_id=1, source_target_pairs={{0,28},{4,24},{8,20},{12,16},{16,12},{20,8},{24,4},{28,0},{1,29},{... | collective-permute-start | bytes 393224 | tf_op jit(solution)/shard_map/ppermute | solution.py:228
  175.8 16.7 %collective-permute-start.5 = (bf16[256,256]{1,0:T(8,128)(2,1)S(1)}, bf16[256,256]{1,0:T(8,128)(2,1)S(1)}, u32[]{:S(2)}, u32[]{:S(2)}) collective-permute-start(bf16[256,256]{1,0:T(8,128)(2,1)S(1)} %get-tuple-element.42), channel_id=1, source_target_pairs={{0,24},{4,28},{8,16},{12,20},{16,8},{20,12},{24,0},{28,4},{1,25},{... | collective-permute-start | bytes 393224 | tf_op jit(solution)/shard_map/ppermute | solution.py:228
  178.0 19.3 %collective-permute-start.6 = (bf16[256,256]{1,0:T(8,128)(2,1)S(1)}, bf16[256,256]{1,0:T(8,128)(2,1)S(1)}, u32[]{:S(2)}, u32[]{:S(2)}) collective-permute-start(bf16[256,256]{1,0:T(8,128)(2,1)S(1)} %get-tuple-element.41), channel_id=1, source_target_pairs={{0,20},{4,16},{8,28},{12,24},{16,4},{20,0},{24,12},{28,8},{1,21},{... | collective-permute-start | bytes 393224 | tf_op jit(solution)/shard_map/ppermute | solution.py:228
  181.7 15.5 %collective-permute-start.7 = (bf16[256,256]{1,0:T(8,128)(2,1)S(1)}, bf16[256,256]{1,0:T(8,128)(2,1)S(1)}, u32[]{:S(2)}, u32[]{:S(2)}) collective-permute-start(bf16[256,256]{1,0:T(8,128)(2,1)S(1)} %get-tuple-element.40), channel_id=1, source_target_pairs={{0,16},{4,20},{8,24},{12,28},{16,0},{20,4},{24,8},{28,12},{1,17},{... | collective-permute-start | bytes 393224 | tf_op jit(solution)/shard_map/ppermute | solution.py:228
  185.1 12.1 %collective-permute-start.8 = (bf16[256,256]{1,0:T(8,128)(2,1)S(1)}, bf16[256,256]{1,0:T(8,128)(2,1)S(1)}, u32[]{:S(2)}, u32[]{:S(2)}) collective-permute-start(bf16[256,256]{1,0:T(8,128)(2,1)S(1)} %get-tuple-element.39), channel_id=1, source_target_pairs={{0,12},{4,8},{8,4},{12,0},{16,28},{20,24},{24,20},{28,16},{1,13},{... | collective-permute-start | bytes 393224 | tf_op jit(solution)/shard_map/ppermute | solution.py:228
  187.4 11.6 %collective-permute-start.9 = (bf16[256,256]{1,0:T(8,128)(2,1)S(1)}, bf16[256,256]{1,0:T(8,128)(2,1)S(1)}, u32[]{:S(2)}, u32[]{:S(2)}) collective-permute-start(bf16[256,256]{1,0:T(8,128)(2,1)S(1)} %get-tuple-element.38), channel_id=1, source_target_pairs={{0,8},{4,12},{8,0},{12,4},{16,24},{20,28},{24,16},{28,20},{1,9},{5... | collective-permute-start | bytes 393224 | tf_op jit(solution)/shard_map/ppermute | solution.py:228
  192.5 6.5 %collective-permute-start.10 = (bf16[256,256]{1,0:T(8,128)(2,1)S(1)}, bf16[256,256]{1,0:T(8,128)(2,1)S(1)}, u32[]{:S(2)}, u32[]{:S(2)}) collective-permute-start(bf16[256,256]{1,0:T(8,128)(2,1)S(1)} %get-tuple-element.37), channel_id=1, source_target_pairs={{0,4},{4,0},{8,12},{12,8},{16,20},{20,16},{24,28},{28,24},{1,5},{5... | collective-permute-start | bytes 393224 | tf_op jit(solution)/shard_map/ppermute | solution.py:228
  200.9 25.6 %copy-start.11 = (f32[128,2]{0,1:T(2,128)S(1)}, f32[128,2]{0,1:T(2,128)}, u32[]{:S(2)}) copy-start(f32[128,2]{0,1:T(2,128)} %param.10) | copy-start | bytes 3076
  220.1 29.0 %all-to-all-start.3 = ((bf16[128,2,512]{2,1,0:T(2,128)(2,1)}), bf16[128,2,512]{2,1,0:T(2,128)(2,1)S(1)}, u32[]{:S(2)}, u32[]{:S(2)}) async-start(bf16[128,2,512]{2,1,0:T(2,128)(2,1)} %reshape.42), calls=%async_computation.3 | async-start | bytes 524288 | tf_op jit(solution)/shard_map/all_to_all | solution.py:200
Sparse Core Ops, SparseCore 0:
  9.5 112.7 all-gather.2

commit v5 on v4

--- a/solution.py
+++ b/solution.py
@@ -22,8 +22,9 @@
 
 def first_kernel(plane, tok_ref, gain_ref, rt_ref, out_ref, tgt_ref, hot_ref):
     toks, width = tok_ref.shape
-    slots = out_ref.shape[0]
-    experts, piece = slots // SLOT, width // plane
+    experts, piece = out_ref.shape[0], width // plane
+    slots = experts * SLOT
+    shaped = lambda v: v.astype(jnp.bfloat16).reshape(experts, SLOT, v.shape[1])
     x = tok_ref[...].astype(jnp.float32)
     scale = lax.rsqrt(jnp.mean(x * x, axis=1, keepdims=True) + 1e-06)
     normed = (x * scale * gain_ref[...]).astype(jnp.bfloat16)
@@ -49,7 +50,7 @@
         chosen = ((wanted == targets[0]) | (wanted == targets[1])).astype(jnp.float32)
         return chosen.T.astype(jnp.bfloat16)
 
-    out_ref[:, :width] = matmul(pick(slot), normed).astype(jnp.bfloat16)
+    out_ref[:, :, :width] = shaped(matmul(pick(slot), normed))
     owner = (iota((slots, toks), 0) // SLOT) % plane
     for h in range(2):
         chosen = pick(slots + h * SLOT + slot % SLOT)
@@ -57,14 +58,14 @@
         for j in range(plane):
             part = matmul(chosen, normed[:, j * piece : (j + 1) * piece])
             total = jnp.where(owner[:, :1] == j, part, total)
-        out_ref[:, width + h * piece : width + (h + 1) * piece] = total.astype(jnp.bfloat16)
+        out_ref[:, :, width + h * piece : width + (h + 1) * piece] = shaped(total)
     hot_ref[:, 0:1] = low
     hot_ref[:, 1:2] = high
 
 
 def last_kernel(plane, hot_ref, res_ref, more_ref, tgt_ref, gs_ref, out_ref):
     toks, width = out_ref.shape
-    slots, piece = res_ref.shape[0], width // plane
+    slots, piece = res_ref.shape[0] * SLOT, width // plane
     weights = gs_ref[...] / jnp.sum(gs_ref[...], axis=1, keepdims=True)
 
     def mix(wanted, alive=True):
@@ -77,11 +78,13 @@
     spot = iota((toks, plane * SLOT), 1)
     over = []
     for h in range(2):
-        start = pl.multiple_of(hot_ref[h] // plane * (plane * SLOT), plane * SLOT)
-        over.append(more_ref[pl.ds(start, plane * SLOT), h * piece : (h + 1) * piece])
+        start = hot_ref[h] // plane * plane
+        rows = more_ref[pl.ds(start, plane), :, h * piece : (h + 1) * piece]
+        over.append(rows.reshape(plane * SLOT, piece))
     for j in range(plane):
         start = j * piece
-        total = sum(matmul(p, res_ref[:, start : start + piece]) for p in usual)
+        rows = res_ref[:, :, start : start + piece].reshape(slots, piece)
+        total = sum(matmul(p, rows) for p in usual)
         for h in range(2):
             parts = mix(slots + h * SLOT + spot % SLOT, spot // SLOT == j)
             total += sum(matmul(p, over[h]) for p in parts)
@@ -122,13 +125,16 @@
 
 
 def main_kernel(at_ref, rows_ref, *refs):
-    weights, out_ref, hid_ref = refs[:6], *refs[6:]
+    weights, out_ref, hid_ref, row_ref = refs[:6], *refs[6:]
 
     def put(index, value):
         cols = value.shape[1]
-        out_ref[:, pl.ds(pl.multiple_of(index * cols, cols), cols)] = value
-
-    expert(at_ref[0], rows_ref[:, : out_ref.shape[1]], weights, hid_ref, put)
+        out_ref[:, :, pl.ds(pl.multiple_of(index * cols, cols), cols)] = value.reshape(
+            out_ref.shape[0], out_ref.shape[1], cols
+        )
+
+    row_ref[...] = rows_ref[:, :, : out_ref.shape[2]].reshape(row_ref.shape)
+    expert(at_ref[0], row_ref[...], weights, hid_ref, put)
 
 
 def extra_kernel(at_ref, rows_ref, *refs):
@@ -192,14 +198,15 @@
     packed = gather_ring(jnp.concatenate([w_up[0], w_down[0, :, cols:]], 0))
     sent, target, hot = call(
         lambda *refs: first_kernel(plane, *refs),
-        [shape((slots, width + 2 * piece), bf16), shape((toks, 2), i32), shape((1, 2), i32)],
+        [shape((experts, SLOT, width + 2 * piece), bf16), shape((toks, 2), i32), shape((1, 2), i32)],
         tokens,
         norm_gain.reshape(1, width),
         routing,
     )
     trade = lambda x: lax.all_to_all(
-        x.reshape(experts, SLOT, x.shape[1]), E_AXES, 0, 0, tiled=True
-    ).reshape(x.shape)
+        x if x.ndim == 3 else x.reshape(experts, SLOT, x.shape[1]), E_AXES, 0, 0, tiled=True
+    )
+    flat = lambda x: x.reshape(slots, x.shape[2])
     at = lax.axis_index("dp").reshape(1)
     z = lax.axis_index("z")
     hot = hot.reshape(2)
@@ -207,13 +214,14 @@
 
     packed = pass_on(*packed)
     got, packed = lax.optimization_barrier((trade(sent), packed))
+    extra = flat(got[:, :, width:])
     to_low = (jnp.arange(plane) == low % plane) & (z == low // plane)
     parcel = jnp.where(
-        to_low[:, None, None], got[None, :, width : width + piece], got[None, :, width + piece :]
+        to_low[:, None, None], extra[None, :, :piece], extra[None, :, piece:]
     )
     pieces = lax.all_to_all(parcel, PLANE, 0, 0, tiled=True)
     hid = pltpu.VMEM((slots, units), bf16)
-    done = call(main_kernel, shape((slots, width), bf16), at, got, gate, *packed, scalars=1, scratch=[hid])
+    done = call(main_kernel, shape((experts, SLOT, width), bf16), at, got, gate, *packed, scalars=1, scratch=[hid, pltpu.VMEM((slots, width), bf16)])
     done, pieces = lax.optimization_barrier((done, pieces))
     res = trade(done)
     spot = lax.axis_index("y") * mesh.shape["c"] + lax.axis_index("c")

time: 260 us -> 257 us (0.988)
  local copies, waits for them, and re-layouts: 21.2 us -> 5.68 us
  waiting for transfers between devices: 103 us -> 113 us
  Pallas kernels: 21.4 us -> 24 us
    ppermute x1, waiting for transfers between devices: 0.01 us -> 28.3 us  [pass_on(): lax.ppermute(a, 'dp', ring(4, -1))]
    all_to_all x3, waiting for transfers between devices: 69.2 us -> 41.7 us  [body(): lax.all_to_all(x if x.ndim == 3 else x.reshape(experts, SLOT, x.shape[1])...]
    reshape x3 -> x1, local copies, waits for them, and re-layouts: 7.34 us -> 0.8 us  [body(): x.reshape(experts, SLOT, x.shape[1])]
    ppermute x1, waiting for transfers between devices: 17.2 us -> 22.6 us  [gather_ring(): lax.ppermute(x, 'dp', ring(4, -1))]
    reshape x3 -> x1, local copies, waits for them, and re-layouts: 4.75 us -> 0.1 us  [body(): flat = lambda x: x.reshape(slots, x.shape[2])]
    unnamed x26 -> x16, local copies, waits for them, and re-layouts: 7.05 us -> 2.5 us
    ppermute x1, waiting for transfers between devices: 0.01 us -> 3.14 us  [pass_on(): lax.ppermute(b, 'dp', ring(4, 1))]
  transfers between devices with their start and end apart: 16 -> 16, of which waited for: 8 -> 9; matrix products, arithmetic and copies ran while one was open for 4% -> 2% of each run, Pallas kernels for 7% -> 8%
where the time goes in v5:
time: 257 us; the launch traced here: 256 us
  waiting for transfers between devices  113 us (44%)
  starting transfers between devices  90.8 us (35%)
  Pallas kernels  24 us (9%)
  between operations  18.4 us (7%)
  local copies, waits for them, and re-layouts  5.68 us (2%)
  other arithmetic  4.03 us (2%)
    all_to_all x3, starting transfers between devices, body(): lax.all_to_all(x if x.ndim == 3 else x.reshape(experts, SLOT, x.shape[1])...  46.8 us
    all_to_all x3, waiting for transfers between devices, body(): lax.all_to_all(x if x.ndim == 3 else x.reshape(experts, SLOT, x.shape[1])...  41.7 us
    ppermute x1, waiting for transfers between devices, pass_on(): lax.ppermute(a, 'dp', ring(4, -1))  28.3 us
    pallas_call x5, Pallas kernels, call(): pl.pallas_call(kernel, out_shape=out, in_specs=[SMEM] * scalars + [VMEM]...  24 us
    ppermute x1, waiting for transfers between devices, gather_ring(): lax.ppermute(x, 'dp', ring(4, -1))  22.6 us
    ppermute x7, starting transfers between devices, body(): lax.ppermute(over[b], PLANE, [(j, j ^ b) for j in range(plane)])  22 us
    all_to_all x1, starting transfers between devices, body(): pieces = lax.all_to_all(parcel, PLANE, 0, 0, tiled=True)  10.3 us
    ppermute x1, waiting for transfers between devices, gather_ring(): lax.ppermute(x, 'dp', ring(4, 1))  7.91 us
  transfers between devices with their start and end apart: 16, of which 9 were waited for; matrix products, arithmetic and copies ran while one was open for 2% of the time, Pallas kernels for 8%

profile of v5, /device:TPU:33, one launch (start us, length us, event | category | flops | bytes accessed | tf_op | source)
XLA Modules:
  0.0 256.2 jit_solution(14336012577980453148)
XLA Ops:
  6.5 1.4 slice_bitcast_fusion
  8.1 1.3 pad_maximum_fusion.1
  9.4 1.4 pad_maximum_fusion.refs_1_
  10.8 4.4 %collective-permute-start = (bf16[3072,256]{1,0:T(8,128)(2,1)S(1)}, bf16[3072,256]{1,0:T(8,128)(2,1)}, u32[]{:S(2)}, u32[]{:S(2)}) collective-permute-start(bf16[3072,256]{1,0:T(8,128)(2,1)S(1)} %pad_maximum_fusion.refs_1_), channel_id=1, source_target_pairs={{0,3},{1,0},{2,1},{3,2},{4,7},{5,4},{6,5},{7,6},{8,11},{9,8},{10,9... | collective-permute-start | bytes 4718600 | tf_op jit(solution)/shard_map/ppermute | solution.py:164
  15.2 1.9 collective-permute-start.1
  17.2 1.5 shard_map.73
  19.8 19.8 %all-to-all-start = ((bf16[128,2,2560]{2,1,0:T(2,128)(2,1)}), bf16[128,2,2560]{2,1,0:T(2,128)(2,1)S(1)}, u32[]{:S(2)}, u32[]{:S(2)}) async-start(bf16[128,2,2560]{2,1,0:T(2,128)(2,1)} %copy-done.1), calls=%async_computation | async-start | bytes 2621440 | tf_op jit(solution)/shard_map/all_to_all | solution.py:206
  39.6 22.6 %collective-permute-done.ahead_ref.refs_2_ = bf16[3072,256]{1,0:T(8,128)(2,1)} collective-permute-done((bf16[3072,256]{1,0:T(8,128)(2,1)S(1)}, bf16[3072,256]{1,0:T(8,128)(2,1)}, u32[]{:S(2)}, u32[]{:S(2)}) %collective-permute-start) | collective-permute-done | bytes 1572896 | tf_op jit(solution)/shard_map/ppermute | solution.py:164
  62.2 7.9 %collective-permute-done.1.behind_ref.refs_5_ = bf16[3072,256]{1,0:T(8,128)(2,1)} collective-permute-done((bf16[3072,256]{1,0:T(8,128)(2,1)S(1)}, bf16[3072,256]{1,0:T(8,128)(2,1)}, u32[]{:S(2)}, u32[]{:S(2)}) %collective-permute-start.1) | collective-permute-done | bytes 1572896 | tf_op jit(solution)/shard_map/ppermute | solution.py:164
  70.1 3.2 %shard_map.74 = (bf16[1536,256]{1,0:T(8,128)(2,1)}, bf16[1536,256]{1,0:T(8,128)(2,1)}) custom-call(bf16[3072,256]{1,0:T(8,128)(2,1)} %collective-permute-done.ahead_ref.refs_2_, bf16[3072,256]{1,0:T(8,128)(2,1)} %collective-permute-done.1.behind_ref.refs_5_), custom_call_target="tpu_custom_call" | custom-call | flops 40000000000 | tf_op jit(solution)/shard_map/pallas_call | solution.py:175
  73.3 1.9 collective-permute-start.2
  75.2 3.4 %collective-permute-start.3 = (bf16[1536,256]{1,0:T(8,128)(2,1)}, bf16[1536,256]{1,0:T(8,128)(2,1)}, u32[]{:S(2)}, u32[]{:S(2)}) collective-permute-start(bf16[1536,256]{1,0:T(8,128)(2,1)} %get-tuple-element.23), channel_id=1, source_target_pairs={{0,1},{1,2},{2,3},{3,0},{4,5},{5,6},{6,7},{7,4},{8,9},{9,10},{10,1... | collective-permute-start | bytes 2359304 | tf_op jit(solution)/shard_map/ppermute | solution.py:171
  81.9 28.3 %collective-permute-done.2.refs_3_ = bf16[1536,256]{1,0:T(8,128)(2,1)} collective-permute-done((bf16[1536,256]{1,0:T(8,128)(2,1)}, bf16[1536,256]{1,0:T(8,128)(2,1)}, u32[]{:S(2)}, u32[]{:S(2)}) %collective-permute-start.2) | collective-permute-done | bytes 786464 | tf_op jit(solution)/shard_map/ppermute | solution.py:171
  110.2 3.1 %collective-permute-done.3.refs_4_ = bf16[1536,256]{1,0:T(8,128)(2,1)} collective-permute-done((bf16[1536,256]{1,0:T(8,128)(2,1)}, bf16[1536,256]{1,0:T(8,128)(2,1)}, u32[]{:S(2)}, u32[]{:S(2)}) %collective-permute-start.3) | collective-permute-done | bytes 786464 | tf_op jit(solution)/shard_map/ppermute | solution.py:171
  114.8 10.3 %all-to-all-start.1 = ((bf16[8,256,256]{2,1,0:T(8,128)(2,1)}), bf16[8,256,256]{2,1,0:T(8,128)(2,1)}, u32[]{:S(2)}, u32[]{:S(2)}) async-start(bf16[8,256,256]{2,1,0:T(8,128)(2,1)} %broadcast_select_fusion), calls=%async_computation.1 | async-start | bytes 2097152 | tf_op jit(solution)/shard_map/all_to_all | solution.py:222
  125.1 8.0 %shard_map.75 = bf16[128,2,2048]{2,1,0:T(2,128)(2,1)S(1)} custom-call(s32[1]{0:T(128)} %bitcast.3.at_ref, bf16[128,2,2560]{2,1,0:T(2,128)(2,1)S(1)} %all-to-all-done.rows_ref, bf16[4,3072,256]{2,1,0:T(8,128)(2,1)} %bitcast.35, bf16[3072,256]{1,0:T(8,128)(2,1)S(1)} %pad_maximum_fusion.refs_1_, bf16[3072,256]{1,0:T(8,128)(2,1)} %collective-permute-done.ahead_ref.refs_2_, ...), custom_call_target="tpu_custom_call" | custom-call | tf_op jit(solution)/shard_map/pallas_call | solution.py:175
  134.1 6.2 %all-to-all-done.1.rows_ref = bf16[8,256,256]{2,1,0:T(8,128)(2,1)} async-done(((bf16[8,256,256]{2,1,0:T(8,128)(2,1)}), bf16[8,256,256]{2,1,0:T(8,128)(2,1)}, u32[]{:S(2)}, u32[]{:S(2)}) %all-to-all-start.1) | async-done | bytes 1048608 | tf_op jit(solution)/shard_map/all_to_all | solution.py:222
  140.3 20.7 %all-to-all-start.2 = ((bf16[128,2,2048]{2,1,0:T(2,128)(2,1)}), bf16[128,2,2048]{2,1,0:T(2,128)(2,1)}, u32[]{:S(2)}, u32[]{:S(2)}) async-start(bf16[128,2,2048]{2,1,0:T(2,128)(2,1)} %copy-done), calls=%async_computation.2 | async-start | bytes 2097152 | tf_op jit(solution)/shard_map/all_to_all | solution.py:206
  161.0 8.0 %shard_map.76 = bf16[8,256,256]{2,1,0:T(8,128)(2,1)S(1)} custom-call(s32[2]{0:T(128)S(1)} %pad_add_fusion.at_ref, bf16[8,256,256]{2,1,0:T(8,128)(2,1)} %all-to-all-done.1.rows_ref, bf16[4,3072,256]{2,1,0:T(8,128)(2,1)} %bitcast.36, bf16[3072,256]{1,0:T(8,128)(2,1)S(1)} %pad_maximum_fusion.refs_1_, bf16[3072,256]{1,0:T(8,128)(2,1)} %collective-permute-done.ahead_ref.refs_2_, ...), custom_call_target="tpu_custom_call" | custom-call | tf_op jit(solution)/shard_map/pallas_call | solution.py:175
  169.1 4.6 %collective-permute-start.4 = (bf16[256,256]{1,0:T(8,128)(2,1)S(1)}, bf16[256,256]{1,0:T(8,128)(2,1)S(1)}, u32[]{:S(2)}, u32[]{:S(2)}) collective-permute-start(bf16[256,256]{1,0:T(8,128)(2,1)S(1)} %get-tuple-element.41), channel_id=1, source_target_pairs={{0,28},{4,24},{8,20},{12,16},{16,12},{20,8},{24,4},{28,0},{1,29},{... | collective-permute-start | bytes 393224 | tf_op jit(solution)/shard_map/ppermute | solution.py:236
  173.6 2.2 collective-permute-start.5
  175.8 3.7 %collective-permute-start.6 = (bf16[256,256]{1,0:T(8,128)(2,1)S(1)}, bf16[256,256]{1,0:T(8,128)(2,1)S(1)}, u32[]{:S(2)}, u32[]{:S(2)}) collective-permute-start(bf16[256,256]{1,0:T(8,128)(2,1)S(1)} %get-tuple-element.39), channel_id=1, source_target_pairs={{0,20},{4,16},{8,28},{12,24},{16,4},{20,0},{24,12},{28,8},{1,21},{... | collective-permute-start | bytes 393224 | tf_op jit(solution)/shard_map/ppermute | solution.py:236
  179.6 3.4 %collective-permute-start.7 = (bf16[256,256]{1,0:T(8,128)(2,1)S(1)}, bf16[256,256]{1,0:T(8,128)(2,1)S(1)}, u32[]{:S(2)}, u32[]{:S(2)}) collective-permute-start(bf16[256,256]{1,0:T(8,128)(2,1)S(1)} %get-tuple-element.38), channel_id=1, source_target_pairs={{0,16},{4,20},{8,24},{12,28},{16,0},{20,4},{24,8},{28,12},{1,17},{... | collective-permute-start | bytes 393224 | tf_op jit(solution)/shard_map/ppermute | solution.py:236
  183.0 2.2 collective-permute-start.8
  185.2 3.3 %collective-permute-start.9 = (bf16[256,256]{1,0:T(8,128)(2,1)S(1)}, bf16[256,256]{1,0:T(8,128)(2,1)S(1)}, u32[]{:S(2)}, u32[]{:S(2)}) collective-permute-start(bf16[256,256]{1,0:T(8,128)(2,1)S(1)} %get-tuple-element.36), channel_id=1, source_target_pairs={{0,8},{4,12},{8,0},{12,4},{16,24},{20,28},{24,16},{28,20},{1,9},{5... | collective-permute-start | bytes 393224 | tf_op jit(solution)/shard_map/ppermute | solution.py:236
  188.5 1.9 collective-permute-done.5
  190.4 2.7 %collective-permute-start.10 = (bf16[256,256]{1,0:T(8,128)(2,1)S(1)}, bf16[256,256]{1,0:T(8,128)(2,1)S(1)}, u32[]{:S(2)}, u32[]{:S(2)}) collective-permute-start(bf16[256,256]{1,0:T(8,128)(2,1)S(1)} %get-tuple-element.35), channel_id=1, source_target_pairs={{0,4},{4,0},{8,12},{12,8},{16,20},{20,16},{24,28},{28,24},{1,5},{5... | collective-permute-start | bytes 393224 | tf_op jit(solution)/shard_map/ppermute | solution.py:236
  195.1 1.7 collective-permute-done.9
  197.0 19.2 %all-to-all-done.2.refs_1_ = bf16[128,2,2048]{2,1,0:T(2,128)(2,1)} async-done(((bf16[128,2,2048]{2,1,0:T(2,128)(2,1)}), bf16[128,2,2048]{2,1,0:T(2,128)(2,1)}, u32[]{:S(2)}, u32[]{:S(2)}) %all-to-all-start.2) | async-done | bytes 1048608 | tf_op jit(solution)/shard_map/all_to_all | solution.py:206
  217.0 6.4 %all-to-all-start.3 = ((bf16[128,2,512]{2,1,0:T(2,128)(2,1)}), bf16[128,2,512]{2,1,0:T(2,128)(2,1)S(1)}, u32[]{:S(2)}, u32[]{:S(2)}) async-start(bf16[128,2,512]{2,1,0:T(2,128)(2,1)} %reshape.27), calls=%async_computation.3 | async-start | bytes 524288 | tf_op jit(solution)/shard_map/all_to_all | solution.py:206
  223.6 22.4 %all-to-all-done.3.refs_2_ = bf16[128,2,512]{2,1,0:T(2,128)(2,1)S(1)} async-done(((bf16[128,2,512]{2,1,0:T(2,128)(2,1)}), bf16[128,2,512]{2,1,0:T(2,128)(2,1)S(1)}, u32[]{:S(2)}, u32[]{:S(2)}) %all-to-all-start.3) | async-done | bytes 262176 | tf_op jit(solution)/shard_map/all_to_all | solution.py:206
  246.0 3.3 %shard_map.77 = bf16[128,2048]{1,0:T(8,128)(2,1)} custom-call(s32[2]{0:T(128)S(1)} %bitcast.34, bf16[128,2,2048]{2,1,0:T(2,128)(2,1)} %all-to-all-done.2.refs_1_, bf16[128,2,512]{2,1,0:T(2,128)(2,1)S(1)} %all-to-all-done.3.refs_2_, s32[128,2]{1,0:T(8,128)S(1)} %get-tuple-element.34.refs_3_, f32[128,2]{1,0:T(8,128)S(1)} %copy.9.refs_4_), custom_call_target="tpu_custom_call" | custom-call | tf_op jit(solution)/shard_map/pallas_call | solution.py:175
  (37 shorter events, 5.7 us)
Async XLA Ops:
  6.5 1.5 copy-start.4
  6.5 118.6 %all-gather.3.cloned.1.call-start = ((), (), s32[]{:S(2)}) async-start(), calls=%async_computation.4 | async-start | bytes 7864320 | tf_op jit(solution)/shard_map/all_gather | solution.py:197
  9.4 7.8 %copy-start.5 = (s32[128,2]{0,1:T(2,128)S(1)}, s32[128,2]{0,1:T(2,128)}, u32[]{:S(2)}) copy-start(s32[128,2]{0,1:T(2,128)} %param.9) | copy-start | bytes 3076
  9.4 7.9 %copy-start.2 = (bf16[128,2048]{1,0:T(8,128)(2,1)S(1)}, bf16[128,2048]{1,0:T(8,128)(2,1)}, u32[]{:S(2)}) copy-start(bf16[128,2048]{1,0:T(8,128)(2,1)} %refs_0_.1) | copy-start | bytes 1572868
  9.4 7.9 %copy-start.3 = (f32[2048]{0:T(1024)S(1)}, f32[2048]{0:T(1024)}, u32[]{:S(2)}) copy-start(f32[2048]{0:T(1024)} %param.8) | copy-start | bytes 24580
  10.8 51.4 %collective-permute-start = (bf16[3072,256]{1,0:T(8,128)(2,1)S(1)}, bf16[3072,256]{1,0:T(8,128)(2,1)}, u32[]{:S(2)}, u32[]{:S(2)}) collective-permute-start(bf16[3072,256]{1,0:T(8,128)(2,1)S(1)} %pad_maximum_fusion.refs_1_), channel_id=1, source_target_pairs={{0,3},{1,0},{2,1},{3,2},{4,7},{5,4},{6,5},{7,6},{8,11},{9,8},{10,9... | collective-permute-start | bytes 4718600 | tf_op jit(solution)/shard_map/ppermute | solution.py:164
  15.2 55.0 %collective-permute-start.1 = (bf16[3072,256]{1,0:T(8,128)(2,1)S(1)}, bf16[3072,256]{1,0:T(8,128)(2,1)}, u32[]{:S(2)}, u32[]{:S(2)}) collective-permute-start(bf16[3072,256]{1,0:T(8,128)(2,1)S(1)} %pad_maximum_fusion.refs_1_), channel_id=1, source_target_pairs={{0,1},{1,2},{2,3},{3,0},{4,5},{5,6},{6,7},{7,4},{8,9},{9,10},{10,1... | collective-permute-start | bytes 4718600 | tf_op jit(solution)/shard_map/ppermute | solution.py:164
  18.7 1.1 copy-start.1
  19.8 93.5 %all-to-all-start = ((bf16[128,2,2560]{2,1,0:T(2,128)(2,1)}), bf16[128,2,2560]{2,1,0:T(2,128)(2,1)S(1)}, u32[]{:S(2)}, u32[]{:S(2)}) async-start(bf16[128,2,2560]{2,1,0:T(2,128)(2,1)} %copy-done.1), calls=%async_computation | async-start | bytes 2621440 | tf_op jit(solution)/shard_map/all_to_all | solution.py:206
  73.3 36.8 %collective-permute-start.2 = (bf16[1536,256]{1,0:T(8,128)(2,1)}, bf16[1536,256]{1,0:T(8,128)(2,1)}, u32[]{:S(2)}, u32[]{:S(2)}) collective-permute-start(bf16[1536,256]{1,0:T(8,128)(2,1)} %get-tuple-element.22), channel_id=1, source_target_pairs={{0,3},{1,0},{2,1},{3,2},{4,7},{5,4},{6,5},{7,6},{8,11},{9,8},{10,9... | collective-permute-start | bytes 2359304 | tf_op jit(solution)/shard_map/ppermute | solution.py:171
  75.2 38.1 %collective-permute-start.3 = (bf16[1536,256]{1,0:T(8,128)(2,1)}, bf16[1536,256]{1,0:T(8,128)(2,1)}, u32[]{:S(2)}, u32[]{:S(2)}) collective-permute-start(bf16[1536,256]{1,0:T(8,128)(2,1)} %get-tuple-element.23), channel_id=1, source_target_pairs={{0,1},{1,2},{2,3},{3,0},{4,5},{5,6},{6,7},{7,4},{8,9},{9,10},{10,1... | collective-permute-start | bytes 2359304 | tf_op jit(solution)/shard_map/ppermute | solution.py:171
  114.8 25.5 %all-to-all-start.1 = ((bf16[8,256,256]{2,1,0:T(8,128)(2,1)}), bf16[8,256,256]{2,1,0:T(8,128)(2,1)}, u32[]{:S(2)}, u32[]{:S(2)}) async-start(bf16[8,256,256]{2,1,0:T(8,128)(2,1)} %broadcast_select_fusion), calls=%async_computation.1 | async-start | bytes 2097152 | tf_op jit(solution)/shard_map/all_to_all | solution.py:222
  133.1 1.0 copy-start
  140.3 75.9 %all-to-all-start.2 = ((bf16[128,2,2048]{2,1,0:T(2,128)(2,1)}), bf16[128,2,2048]{2,1,0:T(2,128)(2,1)}, u32[]{:S(2)}, u32[]{:S(2)}) async-start(bf16[128,2,2048]{2,1,0:T(2,128)(2,1)} %copy-done), calls=%async_computation.2 | async-start | bytes 2097152 | tf_op jit(solution)/shard_map/all_to_all | solution.py:206
  169.1 16.1 %collective-permute-start.4 = (bf16[256,256]{1,0:T(8,128)(2,1)S(1)}, bf16[256,256]{1,0:T(8,128)(2,1)S(1)}, u32[]{:S(2)}, u32[]{:S(2)}) collective-permute-start(bf16[256,256]{1,0:T(8,128)(2,1)S(1)} %get-tuple-element.41), channel_id=1, source_target_pairs={{0,28},{4,24},{8,20},{12,16},{16,12},{20,8},{24,4},{28,0},{1,29},{... | collective-permute-start | bytes 393224 | tf_op jit(solution)/shard_map/ppermute | solution.py:236
  173.6 16.7 %collective-permute-start.5 = (bf16[256,256]{1,0:T(8,128)(2,1)S(1)}, bf16[256,256]{1,0:T(8,128)(2,1)S(1)}, u32[]{:S(2)}, u32[]{:S(2)}) collective-permute-start(bf16[256,256]{1,0:T(8,128)(2,1)S(1)} %get-tuple-element.40), channel_id=1, source_target_pairs={{0,24},{4,28},{8,16},{12,20},{16,8},{20,12},{24,0},{28,4},{1,25},{... | collective-permute-start | bytes 393224 | tf_op jit(solution)/shard_map/ppermute | solution.py:236
  175.8 19.3 %collective-permute-start.6 = (bf16[256,256]{1,0:T(8,128)(2,1)S(1)}, bf16[256,256]{1,0:T(8,128)(2,1)S(1)}, u32[]{:S(2)}, u32[]{:S(2)}) collective-permute-start(bf16[256,256]{1,0:T(8,128)(2,1)S(1)} %get-tuple-element.39), channel_id=1, source_target_pairs={{0,20},{4,16},{8,28},{12,24},{16,4},{20,0},{24,12},{28,8},{1,21},{... | collective-permute-start | bytes 393224 | tf_op jit(solution)/shard_map/ppermute | solution.py:236
  179.6 15.6 %collective-permute-start.7 = (bf16[256,256]{1,0:T(8,128)(2,1)S(1)}, bf16[256,256]{1,0:T(8,128)(2,1)S(1)}, u32[]{:S(2)}, u32[]{:S(2)}) collective-permute-start(bf16[256,256]{1,0:T(8,128)(2,1)S(1)} %get-tuple-element.38), channel_id=1, source_target_pairs={{0,16},{4,20},{8,24},{12,28},{16,0},{20,4},{24,8},{28,12},{1,17},{... | collective-permute-start | bytes 393224 | tf_op jit(solution)/shard_map/ppermute | solution.py:236
  183.0 12.2 %collective-permute-start.8 = (bf16[256,256]{1,0:T(8,128)(2,1)S(1)}, bf16[256,256]{1,0:T(8,128)(2,1)S(1)}, u32[]{:S(2)}, u32[]{:S(2)}) collective-permute-start(bf16[256,256]{1,0:T(8,128)(2,1)S(1)} %get-tuple-element.37), channel_id=1, source_target_pairs={{0,12},{4,8},{8,4},{12,0},{16,28},{20,24},{24,20},{28,16},{1,13},{... | collective-permute-start | bytes 393224 | tf_op jit(solution)/shard_map/ppermute | solution.py:236
  185.2 11.6 %collective-permute-start.9 = (bf16[256,256]{1,0:T(8,128)(2,1)S(1)}, bf16[256,256]{1,0:T(8,128)(2,1)S(1)}, u32[]{:S(2)}, u32[]{:S(2)}) collective-permute-start(bf16[256,256]{1,0:T(8,128)(2,1)S(1)} %get-tuple-element.36), channel_id=1, source_target_pairs={{0,8},{4,12},{8,0},{12,4},{16,24},{20,28},{24,16},{28,20},{1,9},{5... | collective-permute-start | bytes 393224 | tf_op jit(solution)/shard_map/ppermute | solution.py:236
  190.4 6.5 %collective-permute-start.10 = (bf16[256,256]{1,0:T(8,128)(2,1)S(1)}, bf16[256,256]{1,0:T(8,128)(2,1)S(1)}, u32[]{:S(2)}, u32[]{:S(2)}) collective-permute-start(bf16[256,256]{1,0:T(8,128)(2,1)S(1)} %get-tuple-element.35), channel_id=1, source_target_pairs={{0,4},{4,0},{8,12},{12,8},{16,20},{20,16},{24,28},{28,24},{1,5},{5... | collective-permute-start | bytes 393224 | tf_op jit(solution)/shard_map/ppermute | solution.py:236
  196.9 26.6 %copy-start.6 = (f32[128,2]{0,1:T(2,128)S(1)}, f32[128,2]{0,1:T(2,128)}, u32[]{:S(2)}) copy-start(f32[128,2]{0,1:T(2,128)} %param.10) | copy-start | bytes 3076
  217.0 29.0 %all-to-all-start.3 = ((bf16[128,2,512]{2,1,0:T(2,128)(2,1)}), bf16[128,2,512]{2,1,0:T(2,128)(2,1)S(1)}, u32[]{:S(2)}, u32[]{:S(2)}) async-start(bf16[128,2,512]{2,1,0:T(2,128)(2,1)} %reshape.27), calls=%async_computation.3 | async-start | bytes 524288 | tf_op jit(solution)/shard_map/all_to_all | solution.py:206
Sparse Core Ops, SparseCore 0:
  9.5 112.8 all-gather.2

commit v6 on v5

--- a/solution.py
+++ b/solution.py
@@ -92,15 +92,18 @@
 
 
 def blocks_of(at, all_ref, own, ahead, far_a, far_b, behind):
-    deep = all_ref.shape[1] * 2 // 3
-    half = far_a.shape[0]
+    near = own.shape[0]
+    deep = (near + all_ref.shape[1]) // 3
+    half, rest = far_a.shape[0], deep + deep // 2
     for k, ref in enumerate((own, ahead, None, behind)):
         index = lax.rem(at + k, 4)
         if ref is None:
-            up, right = [far_a, far_b.at[: deep - half]], [far_b.at[deep - half :]]
+            up, right = [far_a, far_b.at[: deep - half]], far_b.at[deep - half :]
         else:
-            up, right = [ref.at[:deep]], [ref.at[deep:]]
-        yield index, [all_ref.at[index, :deep]], up, ([all_ref.at[index, deep:]], right)
+            up, right = [ref.at[:deep]], ref.at[deep:]
+        yield index, [all_ref.at[index, :deep]], up, (
+            [all_ref.at[index, deep:rest]], [right, all_ref.at[index, rest:]]
+        )
 
 
 def product(rows, parts):
@@ -194,8 +197,12 @@
     units = w_gate.shape[2] * 4
 
     cols = w_down.shape[2] // 2
-    gate = lax.all_gather(jnp.concatenate([w_gate[0], w_down[0, :, :cols]], 0), "dp", axis=0, tiled=False)
-    packed = gather_ring(jnp.concatenate([w_up[0], w_down[0, :, cols:]], 0))
+    split = w_down.shape[1] // 2
+    left, right = w_down[0, :, :cols], w_down[0, :, cols:]
+    gate = lax.all_gather(
+        jnp.concatenate([w_gate[0], left, right[split:]], 0), "dp", axis=0, tiled=False
+    )
+    packed = gather_ring(jnp.concatenate([w_up[0], right[:split]], 0))
     sent, target, hot = call(
         lambda *refs: first_kernel(plane, *refs),
         [shape((experts, SLOT, width + 2 * piece), bf16), shape((toks, 2), i32), shape((1, 2), i32)],

time: 257 us -> 248 us (0.965)
  starting transfers between devices: 90.8 us -> 83.7 us
  local copies, waits for them, and re-layouts: 5.68 us -> 10.8 us
  waiting for transfers between devices: 113 us -> 108 us
    ppermute x1, waiting for transfers between devices: 22.6 us -> 10.8 us  [gather_ring(): lax.ppermute(x, 'dp', ring(4, -1))]
    all_to_all x3, waiting for transfers between devices: 41.7 us -> 52 us  [body(): lax.all_to_all(x if x.ndim == 3 else x.reshape(experts, SLOT, x.shape[1])...]
    all_gather x1, waiting for transfers between devices: 0.01 us -> 7.51 us  [body(): lax.all_gather(jnp.concatenate([w_gate[0], left, right[split:]], 0), 'dp'...]
    all_to_all x1, waiting for transfers between devices: 6.2 us -> 0.01 us  [body(): pieces = lax.all_to_all(parcel, PLANE, 0, 0, tiled=True)]
    all_to_all x1, starting transfers between devices: 10.3 us -> 4.2 us  [body(): pieces = lax.all_to_all(parcel, PLANE, 0, 0, tiled=True)]
    ppermute x1, waiting for transfers between devices: 28.3 us -> 22.7 us  [pass_on(): lax.ppermute(a, 'dp', ring(4, -1))]
  transfers between devices with their start and end apart: 16 -> 16, of which waited for: 9 -> 10; matrix products, arithmetic and copies ran while one was open for 2% -> 2% of each run, Pallas kernels for 8% -> 8%
where the time goes in v6:
time: 248 us; the launch traced here: 247 us
  waiting for transfers between devices  108 us (44%)
  starting transfers between devices  83.7 us (34%)
  Pallas kernels  23.3 us (9%)
  between operations  18.2 us (7%)
  local copies, waits for them, and re-layouts  10.8 us (4%)
  other arithmetic  2.8 us (1%)
    all_to_all x3, waiting for transfers between devices, body(): lax.all_to_all(x if x.ndim == 3 else x.reshape(experts, SLOT, x.shape[1])...  52 us
    all_to_all x3, starting transfers between devices, body(): lax.all_to_all(x if x.ndim == 3 else x.reshape(experts, SLOT, x.shape[1])...  45.9 us
    pallas_call x5, Pallas kernels, call(): pl.pallas_call(kernel, out_shape=out, in_specs=[SMEM] * scalars + [VMEM]...  23.3 us
    ppermute x1, waiting for transfers between devices, pass_on(): lax.ppermute(a, 'dp', ring(4, -1))  22.7 us
    ppermute x7, starting transfers between devices, body(): lax.ppermute(over[b], PLANE, [(j, j ^ b) for j in range(plane)])  22 us
    ppermute x1, waiting for transfers between devices, gather_ring(): lax.ppermute(x, 'dp', ring(4, -1))  10.8 us
    ppermute x1, waiting for transfers between devices, gather_ring(): lax.ppermute(x, 'dp', ring(4, 1))  8.07 us
    all_gather x1, waiting for transfers between devices, body(): lax.all_gather(jnp.concatenate([w_gate[0], left, right[split:]], 0), 'dp'...  7.51 us
  transfers between devices with their start and end apart: 16, of which 10 were waited for; matrix products, arithmetic and copies ran while one was open for 2% of the time, Pallas kernels for 8%

profile of v6, /device:TPU:33, one launch (start us, length us, event | category | flops | bytes accessed | tf_op | source)
XLA Modules:
  0.0 246.9 jit_solution(7681072779566074583)
XLA Ops:
  8.8 1.4 pad_maximum_fusion
  11.5 4.4 %collective-permute-start = (bf16[2560,256]{1,0:T(8,128)(2,1)S(1)}, bf16[2560,256]{1,0:T(8,128)(2,1)}, u32[]{:S(2)}, u32[]{:S(2)}) collective-permute-start(bf16[2560,256]{1,0:T(8,128)(2,1)S(1)} %pad_maximum_fusion.1.refs_1_), channel_id=1, source_target_pairs={{0,3},{1,0},{2,1},{3,2},{4,7},{5,4},{6,5},{7,6},{8,11},{9,8},{10,9... | collective-permute-start | bytes 3932168 | tf_op jit(solution)/shard_map/ppermute | solution.py:167
  15.9 1.9 collective-permute-start.1
  18.0 1.5 shard_map.73
  20.5 19.8 %all-to-all-start = ((bf16[128,2,2560]{2,1,0:T(2,128)(2,1)}), bf16[128,2,2560]{2,1,0:T(2,128)(2,1)S(1)}, u32[]{:S(2)}, u32[]{:S(2)}) async-start(bf16[128,2,2560]{2,1,0:T(2,128)(2,1)} %copy-done.1), calls=%async_computation | async-start | bytes 2621440 | tf_op jit(solution)/shard_map/all_to_all | solution.py:213
  40.3 10.8 %collective-permute-done.ahead_ref.refs_2_ = bf16[2560,256]{1,0:T(8,128)(2,1)} collective-permute-done((bf16[2560,256]{1,0:T(8,128)(2,1)S(1)}, bf16[2560,256]{1,0:T(8,128)(2,1)}, u32[]{:S(2)}, u32[]{:S(2)}) %collective-permute-start) | collective-permute-done | bytes 1310752 | tf_op jit(solution)/shard_map/ppermute | solution.py:167
  51.1 8.1 %collective-permute-done.1.behind_ref.refs_5_ = bf16[2560,256]{1,0:T(8,128)(2,1)} collective-permute-done((bf16[2560,256]{1,0:T(8,128)(2,1)S(1)}, bf16[2560,256]{1,0:T(8,128)(2,1)}, u32[]{:S(2)}, u32[]{:S(2)}) %collective-permute-start.1) | collective-permute-done | bytes 1310752 | tf_op jit(solution)/shard_map/ppermute | solution.py:167
  59.2 2.9 %shard_map.74 = (bf16[1280,256]{1,0:T(8,128)(2,1)}, bf16[1280,256]{1,0:T(8,128)(2,1)}) custom-call(bf16[2560,256]{1,0:T(8,128)(2,1)} %collective-permute-done.ahead_ref.refs_2_, bf16[2560,256]{1,0:T(8,128)(2,1)} %collective-permute-done.1.behind_ref.refs_5_), custom_call_target="tpu_custom_call" | custom-call | flops 40000000000 | tf_op jit(solution)/shard_map/pallas_call | solution.py:178
  62.0 1.9 collective-permute-start.2
  63.9 3.4 %collective-permute-start.3 = (bf16[1280,256]{1,0:T(8,128)(2,1)}, bf16[1280,256]{1,0:T(8,128)(2,1)}, u32[]{:S(2)}, u32[]{:S(2)}) collective-permute-start(bf16[1280,256]{1,0:T(8,128)(2,1)} %get-tuple-element.23), channel_id=1, source_target_pairs={{0,1},{1,2},{2,3},{3,0},{4,5},{5,6},{6,7},{7,4},{8,9},{9,10},{10,1... | collective-permute-start | bytes 1966088 | tf_op jit(solution)/shard_map/ppermute | solution.py:174
  70.6 22.7 %collective-permute-done.2.refs_3_ = bf16[1280,256]{1,0:T(8,128)(2,1)S(1)} collective-permute-done((bf16[1280,256]{1,0:T(8,128)(2,1)}, bf16[1280,256]{1,0:T(8,128)(2,1)S(1)}, u32[]{:S(2)}, u32[]{:S(2)}) %collective-permute-start.2) | collective-permute-done | bytes 655392 | tf_op jit(solution)/shard_map/ppermute | solution.py:174
  93.2 3.1 %collective-permute-done.3.refs_4_ = bf16[1280,256]{1,0:T(8,128)(2,1)} collective-permute-done((bf16[1280,256]{1,0:T(8,128)(2,1)}, bf16[1280,256]{1,0:T(8,128)(2,1)}, u32[]{:S(2)}, u32[]{:S(2)}) %collective-permute-start.3) | collective-permute-done | bytes 655392 | tf_op jit(solution)/shard_map/ppermute | solution.py:174
  96.4 10.3 %all-to-all-done.rows_ref = bf16[128,2,2560]{2,1,0:T(2,128)(2,1)S(1)} async-done(((bf16[128,2,2560]{2,1,0:T(2,128)(2,1)}), bf16[128,2,2560]{2,1,0:T(2,128)(2,1)S(1)}, u32[]{:S(2)}, u32[]{:S(2)}) %all-to-all-start) | async-done | bytes 1310752 | tf_op jit(solution)/shard_map/all_to_all | solution.py:213
  107.5 1.8 reshape.28
  111.4 4.2 %all-to-all-start.1 = ((bf16[8,256,256]{2,1,0:T(8,128)(2,1)}), bf16[8,256,256]{2,1,0:T(8,128)(2,1)}, u32[]{:S(2)}, u32[]{:S(2)}) async-start(bf16[8,256,256]{2,1,0:T(8,128)(2,1)} %broadcast_select_fusion), calls=%async_computation.1 | async-start | bytes 2097152 | tf_op jit(solution)/shard_map/all_to_all | solution.py:229
  115.6 7.5 %all-gather.3.cloned.1.call-done = bf16[14336,256]{1,0:T(8,128)(2,1)} async-done(((bf16[3584,256]{1,0:T(8,128)(2,1)}), bf16[14336,256]{1,0:T(8,128)(2,1)}) %all-gather.3.cloned.1.call-update) | async-done | bytes 7340048 | tf_op jit(solution)/shard_map/all_gather | solution.py:202
  123.1 7.8 %shard_map.75 = bf16[128,2,2048]{2,1,0:T(2,128)(2,1)S(1)} custom-call(s32[1]{0:T(128)} %bitcast.3.at_ref, bf16[128,2,2560]{2,1,0:T(2,128)(2,1)S(1)} %all-to-all-done.rows_ref, bf16[4,3584,256]{2,1,0:T(8,128)(2,1)} %bitcast.37, bf16[2560,256]{1,0:T(8,128)(2,1)S(1)} %pad_maximum_fusion.1.refs_1_, bf16[2560,256]{1,0:T(8,128)(2,1)} %collective-permute-done.ahead_ref.refs_2_, ...), custom_call_target="tpu_custom_call" | custom-call | tf_op jit(solution)/shard_map/pallas_call | solution.py:178
  131.9 19.7 %all-to-all-start.2 = ((bf16[128,2,2048]{2,1,0:T(2,128)(2,1)}), bf16[128,2,2048]{2,1,0:T(2,128)(2,1)}, u32[]{:S(2)}, u32[]{:S(2)}) async-start(bf16[128,2,2048]{2,1,0:T(2,128)(2,1)} %copy-done), calls=%async_computation.2 | async-start | bytes 2097152 | tf_op jit(solution)/shard_map/all_to_all | solution.py:213
  151.7 7.9 %shard_map.76 = bf16[8,256,256]{2,1,0:T(8,128)(2,1)S(1)} custom-call(s32[2]{0:T(128)S(1)} %pad_add_fusion.at_ref, bf16[8,256,256]{2,1,0:T(8,128)(2,1)} %all-to-all-done.1.rows_ref, bf16[4,3584,256]{2,1,0:T(8,128)(2,1)} %bitcast.38, bf16[2560,256]{1,0:T(8,128)(2,1)S(1)} %pad_maximum_fusion.1.refs_1_, ...), custom_call_target="tpu_custom_call" | custom-call | tf_op jit(solution)/shard_map/pallas_call | solution.py:178
  159.7 4.6 %collective-permute-start.4 = (bf16[256,256]{1,0:T(8,128)(2,1)S(1)}, bf16[256,256]{1,0:T(8,128)(2,1)S(1)}, u32[]{:S(2)}, u32[]{:S(2)}) collective-permute-start(bf16[256,256]{1,0:T(8,128)(2,1)S(1)} %get-tuple-element.41), channel_id=1, source_target_pairs={{0,28},{4,24},{8,20},{12,16},{16,12},{20,8},{24,4},{28,0},{1,29},{... | collective-permute-start | bytes 393224 | tf_op jit(solution)/shard_map/ppermute | solution.py:243
  164.2 2.2 collective-permute-start.5
  166.4 3.7 %collective-permute-start.6 = (bf16[256,256]{1,0:T(8,128)(2,1)S(1)}, bf16[256,256]{1,0:T(8,128)(2,1)S(1)}, u32[]{:S(2)}, u32[]{:S(2)}) collective-permute-start(bf16[256,256]{1,0:T(8,128)(2,1)S(1)} %get-tuple-element.39), channel_id=1, source_target_pairs={{0,20},{4,16},{8,28},{12,24},{16,4},{20,0},{24,12},{28,8},{1,21},{... | collective-permute-start | bytes 393224 | tf_op jit(solution)/shard_map/ppermute | solution.py:243
  170.1 3.4 %collective-permute-start.7 = (bf16[256,256]{1,0:T(8,128)(2,1)S(1)}, bf16[256,256]{1,0:T(8,128)(2,1)S(1)}, u32[]{:S(2)}, u32[]{:S(2)}) collective-permute-start(bf16[256,256]{1,0:T(8,128)(2,1)S(1)} %get-tuple-element.38), channel_id=1, source_target_pairs={{0,16},{4,20},{8,24},{12,28},{16,0},{20,4},{24,8},{28,12},{1,17},{... | collective-permute-start | bytes 393224 | tf_op jit(solution)/shard_map/ppermute | solution.py:243
  173.6 2.2 collective-permute-start.8
  175.8 3.3 %collective-permute-start.9 = (bf16[256,256]{1,0:T(8,128)(2,1)S(1)}, bf16[256,256]{1,0:T(8,128)(2,1)S(1)}, u32[]{:S(2)}, u32[]{:S(2)}) collective-permute-start(bf16[256,256]{1,0:T(8,128)(2,1)S(1)} %get-tuple-element.36), channel_id=1, source_target_pairs={{0,8},{4,12},{8,0},{12,4},{16,24},{20,28},{24,16},{28,20},{1,9},{5... | collective-permute-start | bytes 393224 | tf_op jit(solution)/shard_map/ppermute | solution.py:243
  179.1 1.9 collective-permute-done.5
  181.0 2.7 %collective-permute-start.10 = (bf16[256,256]{1,0:T(8,128)(2,1)S(1)}, bf16[256,256]{1,0:T(8,128)(2,1)S(1)}, u32[]{:S(2)}, u32[]{:S(2)}) collective-permute-start(bf16[256,256]{1,0:T(8,128)(2,1)S(1)} %get-tuple-element.35), channel_id=1, source_target_pairs={{0,4},{4,0},{8,12},{12,8},{16,20},{20,16},{24,28},{28,24},{1,5},{5... | collective-permute-start | bytes 393224 | tf_op jit(solution)/shard_map/ppermute | solution.py:243
  185.6 1.8 collective-permute-done.9
  187.6 19.3 %all-to-all-done.2.refs_1_ = bf16[128,2,2048]{2,1,0:T(2,128)(2,1)} async-done(((bf16[128,2,2048]{2,1,0:T(2,128)(2,1)}), bf16[128,2,2048]{2,1,0:T(2,128)(2,1)}, u32[]{:S(2)}, u32[]{:S(2)}) %all-to-all-start.2) | async-done | bytes 1048608 | tf_op jit(solution)/shard_map/all_to_all | solution.py:213
  207.7 6.4 %all-to-all-start.3 = ((bf16[128,2,512]{2,1,0:T(2,128)(2,1)}), bf16[128,2,512]{2,1,0:T(2,128)(2,1)S(1)}, u32[]{:S(2)}, u32[]{:S(2)}) async-start(bf16[128,2,512]{2,1,0:T(2,128)(2,1)} %reshape.29), calls=%async_computation.3 | async-start | bytes 524288 | tf_op jit(solution)/shard_map/all_to_all | solution.py:213
  214.3 22.4 %all-to-all-done.3.refs_2_ = bf16[128,2,512]{2,1,0:T(2,128)(2,1)S(1)} async-done(((bf16[128,2,512]{2,1,0:T(2,128)(2,1)}), bf16[128,2,512]{2,1,0:T(2,128)(2,1)S(1)}, u32[]{:S(2)}, u32[]{:S(2)}) %all-to-all-start.3) | async-done | bytes 262176 | tf_op jit(solution)/shard_map/all_to_all | solution.py:213
  236.7 3.3 %shard_map.77 = bf16[128,2048]{1,0:T(8,128)(2,1)} custom-call(s32[2]{0:T(128)S(1)} %bitcast.36, bf16[128,2,2048]{2,1,0:T(2,128)(2,1)} %all-to-all-done.2.refs_1_, bf16[128,2,512]{2,1,0:T(2,128)(2,1)S(1)} %all-to-all-done.3.refs_2_, s32[128,2]{1,0:T(8,128)S(1)} %get-tuple-element.34.refs_3_, f32[128,2]{1,0:T(8,128)S(1)} %copy.9.refs_4_), custom_call_target="tpu_custom_call" | custom-call | tf_op jit(solution)/shard_map/pallas_call | solution.py:178
  (40 shorter events, 10.5 us)
Async XLA Ops:
  6.5 2.2 copy-start.4
  6.5 116.6 %all-gather.3.cloned.1.call-start = ((), (), s32[]{:S(2)}) async-start(), calls=%async_computation.4 | async-start | bytes 9175040 | tf_op jit(solution)/shard_map/all_gather | solution.py:202
  10.2 1.2 copy-start.5
  10.2 7.6 %copy-start.6 = (s32[128,2]{0,1:T(2,128)S(1)}, s32[128,2]{0,1:T(2,128)}, u32[]{:S(2)}) copy-start(s32[128,2]{0,1:T(2,128)} %param.9) | copy-start | bytes 3076
  10.2 7.8 %copy-start.2 = (bf16[128,2048]{1,0:T(8,128)(2,1)S(1)}, bf16[128,2048]{1,0:T(8,128)(2,1)}, u32[]{:S(2)}) copy-start(bf16[128,2048]{1,0:T(8,128)(2,1)} %refs_0_.1) | copy-start | bytes 1572868
  10.2 7.8 %copy-start.3 = (f32[2048]{0:T(1024)S(1)}, f32[2048]{0:T(1024)}, u32[]{:S(2)}) copy-start(f32[2048]{0:T(1024)} %param.8) | copy-start | bytes 24580
  11.5 39.6 %collective-permute-start = (bf16[2560,256]{1,0:T(8,128)(2,1)S(1)}, bf16[2560,256]{1,0:T(8,128)(2,1)}, u32[]{:S(2)}, u32[]{:S(2)}) collective-permute-start(bf16[2560,256]{1,0:T(8,128)(2,1)S(1)} %pad_maximum_fusion.1.refs_1_), channel_id=1, source_target_pairs={{0,3},{1,0},{2,1},{3,2},{4,7},{5,4},{6,5},{7,6},{8,11},{9,8},{10,9... | collective-permute-start | bytes 3932168 | tf_op jit(solution)/shard_map/ppermute | solution.py:167
  15.9 43.3 %collective-permute-start.1 = (bf16[2560,256]{1,0:T(8,128)(2,1)S(1)}, bf16[2560,256]{1,0:T(8,128)(2,1)}, u32[]{:S(2)}, u32[]{:S(2)}) collective-permute-start(bf16[2560,256]{1,0:T(8,128)(2,1)S(1)} %pad_maximum_fusion.1.refs_1_), channel_id=1, source_target_pairs={{0,1},{1,2},{2,3},{3,0},{4,5},{5,6},{6,7},{7,4},{8,9},{9,10},{10,1... | collective-permute-start | bytes 3932168 | tf_op jit(solution)/shard_map/ppermute | solution.py:167
  19.4 1.1 copy-start.1
  20.5 86.1 %all-to-all-start = ((bf16[128,2,2560]{2,1,0:T(2,128)(2,1)}), bf16[128,2,2560]{2,1,0:T(2,128)(2,1)S(1)}, u32[]{:S(2)}, u32[]{:S(2)}) async-start(bf16[128,2,2560]{2,1,0:T(2,128)(2,1)} %copy-done.1), calls=%async_computation | async-start | bytes 2621440 | tf_op jit(solution)/shard_map/all_to_all | solution.py:213
  62.0 31.2 %collective-permute-start.2 = (bf16[1280,256]{1,0:T(8,128)(2,1)}, bf16[1280,256]{1,0:T(8,128)(2,1)S(1)}, u32[]{:S(2)}, u32[]{:S(2)}) collective-permute-start(bf16[1280,256]{1,0:T(8,128)(2,1)} %get-tuple-element.22), channel_id=1, source_target_pairs={{0,3},{1,0},{2,1},{3,2},{4,7},{5,4},{6,5},{7,6},{8,11},{9,8},{10,9... | collective-permute-start | bytes 1966088 | tf_op jit(solution)/shard_map/ppermute | solution.py:174
  63.9 32.4 %collective-permute-start.3 = (bf16[1280,256]{1,0:T(8,128)(2,1)}, bf16[1280,256]{1,0:T(8,128)(2,1)}, u32[]{:S(2)}, u32[]{:S(2)}) collective-permute-start(bf16[1280,256]{1,0:T(8,128)(2,1)} %get-tuple-element.23), channel_id=1, source_target_pairs={{0,1},{1,2},{2,3},{3,0},{4,5},{5,6},{6,7},{7,4},{8,9},{9,10},{10,1... | collective-permute-start | bytes 1966088 | tf_op jit(solution)/shard_map/ppermute | solution.py:174
  111.4 20.5 %all-to-all-start.1 = ((bf16[8,256,256]{2,1,0:T(8,128)(2,1)}), bf16[8,256,256]{2,1,0:T(8,128)(2,1)}, u32[]{:S(2)}, u32[]{:S(2)}) async-start(bf16[8,256,256]{2,1,0:T(8,128)(2,1)} %broadcast_select_fusion), calls=%async_computation.1 | async-start | bytes 2097152 | tf_op jit(solution)/shard_map/all_to_all | solution.py:229
  130.9 1.0 copy-start
  131.9 75.0 %all-to-all-start.2 = ((bf16[128,2,2048]{2,1,0:T(2,128)(2,1)}), bf16[128,2,2048]{2,1,0:T(2,128)(2,1)}, u32[]{:S(2)}, u32[]{:S(2)}) async-start(bf16[128,2,2048]{2,1,0:T(2,128)(2,1)} %copy-done), calls=%async_computation.2 | async-start | bytes 2097152 | tf_op jit(solution)/shard_map/all_to_all | solution.py:213
  159.7 16.1 %collective-permute-start.4 = (bf16[256,256]{1,0:T(8,128)(2,1)S(1)}, bf16[256,256]{1,0:T(8,128)(2,1)S(1)}, u32[]{:S(2)}, u32[]{:S(2)}) collective-permute-start(bf16[256,256]{1,0:T(8,128)(2,1)S(1)} %get-tuple-element.41), channel_id=1, source_target_pairs={{0,28},{4,24},{8,20},{12,16},{16,12},{20,8},{24,4},{28,0},{1,29},{... | collective-permute-start | bytes 393224 | tf_op jit(solution)/shard_map/ppermute | solution.py:243
  164.2 16.8 %collective-permute-start.5 = (bf16[256,256]{1,0:T(8,128)(2,1)S(1)}, bf16[256,256]{1,0:T(8,128)(2,1)S(1)}, u32[]{:S(2)}, u32[]{:S(2)}) collective-permute-start(bf16[256,256]{1,0:T(8,128)(2,1)S(1)} %get-tuple-element.40), channel_id=1, source_target_pairs={{0,24},{4,28},{8,16},{12,20},{16,8},{20,12},{24,0},{28,4},{1,25},{... | collective-permute-start | bytes 393224 | tf_op jit(solution)/shard_map/ppermute | solution.py:243
  166.4 19.2 %collective-permute-start.6 = (bf16[256,256]{1,0:T(8,128)(2,1)S(1)}, bf16[256,256]{1,0:T(8,128)(2,1)S(1)}, u32[]{:S(2)}, u32[]{:S(2)}) collective-permute-start(bf16[256,256]{1,0:T(8,128)(2,1)S(1)} %get-tuple-element.39), channel_id=1, source_target_pairs={{0,20},{4,16},{8,28},{12,24},{16,4},{20,0},{24,12},{28,8},{1,21},{... | collective-permute-start | bytes 393224 | tf_op jit(solution)/shard_map/ppermute | solution.py:243
  170.1 15.5 %collective-permute-start.7 = (bf16[256,256]{1,0:T(8,128)(2,1)S(1)}, bf16[256,256]{1,0:T(8,128)(2,1)S(1)}, u32[]{:S(2)}, u32[]{:S(2)}) collective-permute-start(bf16[256,256]{1,0:T(8,128)(2,1)S(1)} %get-tuple-element.38), channel_id=1, source_target_pairs={{0,16},{4,20},{8,24},{12,28},{16,0},{20,4},{24,8},{28,12},{1,17},{... | collective-permute-start | bytes 393224 | tf_op jit(solution)/shard_map/ppermute | solution.py:243
  173.6 12.1 %collective-permute-start.8 = (bf16[256,256]{1,0:T(8,128)(2,1)S(1)}, bf16[256,256]{1,0:T(8,128)(2,1)S(1)}, u32[]{:S(2)}, u32[]{:S(2)}) collective-permute-start(bf16[256,256]{1,0:T(8,128)(2,1)S(1)} %get-tuple-element.37), channel_id=1, source_target_pairs={{0,12},{4,8},{8,4},{12,0},{16,28},{20,24},{24,20},{28,16},{1,13},{... | collective-permute-start | bytes 393224 | tf_op jit(solution)/shard_map/ppermute | solution.py:243
  175.8 11.6 %collective-permute-start.9 = (bf16[256,256]{1,0:T(8,128)(2,1)S(1)}, bf16[256,256]{1,0:T(8,128)(2,1)S(1)}, u32[]{:S(2)}, u32[]{:S(2)}) collective-permute-start(bf16[256,256]{1,0:T(8,128)(2,1)S(1)} %get-tuple-element.36), channel_id=1, source_target_pairs={{0,8},{4,12},{8,0},{12,4},{16,24},{20,28},{24,16},{28,20},{1,9},{5... | collective-permute-start | bytes 393224 | tf_op jit(solution)/shard_map/ppermute | solution.py:243
  181.0 6.4 %collective-permute-start.10 = (bf16[256,256]{1,0:T(8,128)(2,1)S(1)}, bf16[256,256]{1,0:T(8,128)(2,1)S(1)}, u32[]{:S(2)}, u32[]{:S(2)}) collective-permute-start(bf16[256,256]{1,0:T(8,128)(2,1)S(1)} %get-tuple-element.35), channel_id=1, source_target_pairs={{0,4},{4,0},{8,12},{12,8},{16,20},{20,16},{24,28},{28,24},{1,5},{5... | collective-permute-start | bytes 393224 | tf_op jit(solution)/shard_map/ppermute | solution.py:243
  185.6 28.5 %copy-start.7 = (f32[128,2]{0,1:T(2,128)S(1)}, f32[128,2]{0,1:T(2,128)}, u32[]{:S(2)}) copy-start(f32[128,2]{0,1:T(2,128)} %param.10) | copy-start | bytes 3076
  207.7 29.0 %all-to-all-start.3 = ((bf16[128,2,512]{2,1,0:T(2,128)(2,1)}), bf16[128,2,512]{2,1,0:T(2,128)(2,1)S(1)}, u32[]{:S(2)}, u32[]{:S(2)}) async-start(bf16[128,2,512]{2,1,0:T(2,128)(2,1)} %reshape.29), calls=%async_computation.3 | async-start | bytes 524288 | tf_op jit(solution)/shard_map/all_to_all | solution.py:213
Sparse Core Ops, SparseCore 0:
  10.3 112.7 all-gather.2
